TPU v7x, 32 devices: a whole 2x2x4 slice. The times are simulated.
32 devices in a mesh: ctx: 4 (over y, core), fsdp: 8 (over z, x).
Axes of the slice: x: 2, y: 2, z: 4, core: 2. Of those that a mesh axis runs over, the one named last changes fastest.
Arguments:
- inputs: bfloat16 [2, 8, 512, 1024], P(None, 'fsdp', 'ctx'), may hold values from -7.1875 to 7.1875
- timestep: bfloat16 [2, 8, 1024], P(None, 'fsdp'), may hold values from -0.59765625 to 0.59765625
- doc_ids: int32 [2, 8, 512], P(None, 'fsdp', 'ctx'), may hold values from 0 to 3, never falling along the last dimension, each value on 1 to 384 neighbouring positions
- w_qkv: bfloat16 [1024, 3072], P('fsdp'), may hold values from -0.1875 to 0.1875
- w_out: bfloat16 [1024, 1024], P('fsdp'), may hold values from -3 to 3
- w_up: bfloat16 [1024, 4096], P('fsdp'), may hold values from -0.1875 to 0.1875
- w_down: bfloat16 [4096, 1024], P('fsdp'), may hold values from -0.09375 to 0.09375
- bias_model: bfloat16 [4096], P('fsdp'), may hold values from -0.29882812 to 0.29882812
- bias_up: bfloat16 [4096], P('fsdp'), may hold values from -3 to 3
- norm_gains: bfloat16 [2048], P('fsdp'), may hold values from 0.099609375 to 1.8984375
- norm_shifts: bfloat16 [2048], P('fsdp'), may hold values from -3 to 3
- cotangent: bfloat16 [2, 8, 512, 1024], P(None, 'fsdp', 'ctx'), may hold values from -6 to 6
Outputs:
- block_output: bfloat16 [2, 8, 512, 1024], P(None, 'fsdp', 'ctx')
- input_grad: float32 [2, 8, 512, 1024], P(None, 'fsdp', 'ctx')
- grad_qkv: float32 [1024, 3072], P('fsdp')
- grad_out: float32 [1024, 1024], P('fsdp')
- grad_up: float32 [1024, 4096], P('fsdp')
- grad_down: float32 [4096, 1024], P('fsdp')
- grad_bias_model: float32 [4096], P('fsdp')
- grad_bias_up: float32 [4096], P('fsdp')
- grad_gains: float32 [2048], P('fsdp')
- grad_shifts: float32 [2048], P('fsdp')
Inputs may be any that keep to these rules, and one draw needn't show every extreme that they name: `doc_ids`: document numbers along a stream never fall; each document holds 1 to 384 consecutive tokens and one holds exactly 384; attention stays within a document.
All inputs are finite; a program needn't handle non-finite values.
Results may differ from a plain program's by a relative error of at most 0.014.
The roundings to bfloat16 on the way count: a program that leaves them out, or rounds other values in their place, can miss the bound.
Values may be sent and summed in bfloat16 or wider, within the bound.
No kernel may reach another device: no remote copies, remote signals or barrier semaphores. Data moves between devices by JAX's collectives and lax.ppermute only.
A program may use at most 192 MiB of HBM per device.

v0:
```python
import functools
import math

import jax
import jax.numpy as jnp
from jax import lax
from jax.experimental import pallas as pl
from jax.experimental.pallas import tpu as pltpu
from jax.sharding import PartitionSpec as P

HEADS = 16
EPS = 1e-05
LOG2E = math.log2(math.e)
VEC = 8
PAD = 2 * VEC
f32 = jnp.float32
bf16 = jnp.bfloat16


def dot(left, right, dims=((1,), (0,))):
    return lax.dot_general(left, right, (dims, ((), ())), preferred_element_type=f32)


def over_ctx(value, mask):
    size = lax.axis_size("ctx")
    return lax.ppermute(value, "ctx", [(i, i ^ mask) for i in range(size)])


def over_fsdp(value, mask):
    size = lax.axis_size("fsdp")
    return lax.ppermute(value, "fsdp", [(i, i ^ mask) for i in range(size)])


def after(value, *others):
    return lax.optimization_barrier((value, *others))[0]


def shape(dims, dtype=f32):
    return jax.ShapeDtypeStruct(tuple(dims), dtype)


def kernel_call(body, outs, args, scalars=(), scratch=(), flops=50_000_000_000):
    scalars = [jnp.asarray(s, jnp.int32).reshape(-1) for s in scalars]
    specs = [pl.BlockSpec(memory_space=pltpu.SMEM)] * len(scalars)
    specs += [pl.BlockSpec(memory_space=pltpu.VMEM)] * len(args)
    largest = max(math.prod(a.shape) * 4 for a in [*args, *outs])
    held = sum(math.prod(a.shape) * jnp.dtype(a.dtype).itemsize for a in scratch)
    limit = min(held + max(6 * 2**20, 2 * largest), 56 * 2**20)
    return pl.pallas_call(
        body,
        in_specs=specs,
        out_specs=[pl.BlockSpec(memory_space=pltpu.VMEM)] * len(outs),
        out_shape=list(outs),
        scratch_shapes=list(scratch),
        compiler_params=pltpu.CompilerParams(vmem_limit_bytes=limit),
        cost_estimate=pl.CostEstimate(flops=flops, bytes_accessed=1024, transcendentals=0),
    )(*scalars, *args)


def attend_kernel(head_size, scale, block_ref, whole_ref, key_doc_ref, query_doc_ref, out_ref, log_ref):
    width = out_ref.shape[1]
    same = key_doc_ref[...] == query_doc_ref[...]
    for head in range(width // head_size):
        cut = head * head_size
        query = block_ref[:, cut : cut + head_size]
        key = whole_ref[:, width + cut : width + cut + head_size]
        value = whole_ref[:, 2 * width + cut : 2 * width + cut + head_size]
        scores = jnp.where(same, dot(key, query, ((1,), (1,))), -1e30)
        top = jnp.max(scores, axis=0, keepdims=True)
        expo = jnp.exp2((scores - top) * (scale * LOG2E))
        total = jnp.sum(expo, axis=0, keepdims=True)
        probs = (expo * (1.0 / total)).astype(bf16)
        out_ref[:, cut : cut + head_size] = dot(value, probs, ((0,), (0,))).T.astype(bf16)
        log_ref[head : head + 1, :] = top * (scale * LOG2E) + jnp.log2(total)


def attend(projected, key_docs, query_docs, head_size):
    length, width = projected.shape[0], projected.shape[1] // 3
    heads = width // head_size
    block = min(512, length)
    return pl.pallas_call(
        functools.partial(attend_kernel, head_size, 1.0 / math.sqrt(head_size)),
        grid=(length // block,),
        in_specs=[
            pl.BlockSpec((block, 3 * width), lambda i: (i, 0)),
            pl.BlockSpec((length, 3 * width), lambda i: (0, 0)),
            pl.BlockSpec((length, 1), lambda i: (0, 0)),
            pl.BlockSpec((1, block), lambda i: (0, i)),
        ],
        out_specs=[
            pl.BlockSpec((block, width), lambda i: (i, 0)),
            pl.BlockSpec((heads, block), lambda i: (0, i)),
        ],
        out_shape=[shape((length, width), bf16), shape((heads, length))],
        compiler_params=pltpu.CompilerParams(vmem_limit_bytes=(24 if length <= 512 else 48) * 2**20),
        cost_estimate=pl.CostEstimate(
            flops=0, bytes_accessed=1024, transcendentals=0,
        ),
    )(projected, projected, key_docs, query_docs)


def attend_back_kernel(head_size, scale, steps, first, pieces, *refs):
    block_ref, whole_ref, key_doc_ref, query_doc_ref, log_ref = refs[:5]
    grad_refs, (query_out, pair_out, pair_sum) = refs[5 : 5 + pieces], refs[5 + pieces :]
    width = query_out.shape[1]
    step = pl.program_id(0)
    same = key_doc_ref[...] == query_doc_ref[...]

    if steps > 1:
        @pl.when(step == 0)
        def _():
            pair_sum[...] = jnp.zeros_like(pair_sum)

    def add(place, value):
        if steps > 1:
            pair_sum[:, place : place + head_size] += value
        else:
            pair_out[:, place : place + head_size] = value.astype(bf16)

    for head in range(width // head_size):
        cut = head * head_size
        query = block_ref[:, cut : cut + head_size]
        key = whole_ref[:, width + cut : width + cut + head_size]
        value = whole_ref[:, 2 * width + cut : 2 * width + cut + head_size]
        span = slice(first + cut, first + cut + head_size)
        grad = jnp.concatenate([ref[:, span] for ref in grad_refs]) if pieces > 1 else grad_refs[0][:, span]
        scores = dot(key, query, ((1,), (1,)))
        probs = jnp.where(
            same, jnp.exp2(scores * (scale * LOG2E) - log_ref[head : head + 1, :]), 0.0
        )
        d_probs = dot(value, grad, ((1,), (1,)))
        inner = jnp.sum(probs * d_probs, axis=0, keepdims=True)
        d_scores = (probs * (d_probs - inner)).astype(bf16)
        query_out[:, cut : cut + head_size] = (
            dot(key, d_scores, ((0,), (0,))).T * scale
        ).astype(bf16)
        add(cut, dot(d_scores, query) * scale)
        add(width + cut, dot(probs.astype(bf16), grad))

    if steps > 1:
        @pl.when(step == steps - 1)
        def _():
            pair_out[...] = pair_sum[...].astype(bf16)


def attend_back(projected, grads, first, key_docs, query_docs, logs, head_size):
    length, width = projected.shape[0], projected.shape[1] // 3
    heads = width // head_size
    block = min(512, length)
    steps = length // block
    if steps > 1:
        grads = [jnp.concatenate(grads)]
    grad_rows = [grad.shape[0] // steps for grad in grads]
    return pl.pallas_call(
        functools.partial(
            attend_back_kernel, head_size, 1.0 / math.sqrt(head_size), steps, first, len(grads)
        ),
        grid=(steps,),
        in_specs=[
            pl.BlockSpec((block, 3 * width), lambda i: (i, 0)),
            pl.BlockSpec((length, 3 * width), lambda i: (0, 0)),
            pl.BlockSpec((length, 1), lambda i: (0, 0)),
            pl.BlockSpec((1, block), lambda i: (0, i)),
            pl.BlockSpec((heads, block), lambda i: (0, i)),
        ]
        + [pl.BlockSpec((rows, grads[0].shape[1]), lambda i: (i, 0)) for rows in grad_rows],
        out_specs=[
            pl.BlockSpec((block, width), lambda i: (i, 0)),
            pl.BlockSpec((length, 2 * width), lambda i: (0, 0)),
        ],
        out_shape=[shape((length, width), bf16), shape((length, 2 * width), bf16)],
        scratch_shapes=[pltpu.VMEM((length if steps > 1 else 8, 2 * width), f32)],
        compiler_params=pltpu.CompilerParams(vmem_limit_bytes=(24 if length <= 512 else 56) * 2**20),
        cost_estimate=pl.CostEstimate(flops=0, bytes_accessed=1024, transcendentals=0),
    )(projected, projected, key_docs, query_docs, logs, *grads)


def place_kernel(count, rows, columns, where_ref, *refs):
    pieces, (qkv_ref, small_ref, mine_ref, theirs_ref) = refs[:count], refs[count:]
    for j, piece in enumerate(pieces):
        spare = piece.shape[0] - rows
        start = pl.multiple_of(where_ref[j] * rows, rows)
        qkv_ref[pl.ds(start, rows), :] = piece[:rows, :columns]
        start = pl.multiple_of(where_ref[j] * spare, spare)
        small_ref[pl.ds(start, spare), :] = piece[rows:, :columns]
        for way, ref in enumerate((mine_ref, theirs_ref), 1):
            start = pl.multiple_of(where_ref[way * count + j] * rows, rows)
            ref[pl.ds(start, rows), :] = piece[:rows, columns:]


def place(pieces, orders, rows, columns):
    count, spare = len(pieces), pieces[0].shape[0] - rows
    rest = pieces[0].shape[1] - columns
    return kernel_call(
        functools.partial(place_kernel, count, rows, columns),
        [
            shape((count * rows, columns), bf16), shape((count * spare, columns), bf16),
            shape((count * rows, rest), bf16), shape((count * rows, rest), bf16),
        ],
        pieces,
        scalars=[jnp.concatenate(orders)],
    )


def gather_near(shard):
    size = lax.axis_size("fsdp")
    return [shard] + [over_fsdp(shard, 2 * k) for k in range(1, size // 2)]


def gather_far(near):
    pieces = []
    for value in near:
        pieces += [value, over_fsdp(value, 1)]
    return pieces


def gather_tokens(own):
    have, mask = own, 1
    while 2 * mask < lax.axis_size("ctx"):
        got = over_ctx(have, 2 * mask)
        if lax.axis_size("ctx") == 4:
            return got
        have = jnp.concatenate([have, got])
        mask *= 2
    return have[own.shape[0] :]


def reduce_tokens(own, rest):
    ways = lax.axis_size("ctx") // 2
    if ways == 2:
        return own, over_ctx(rest, 2)
    have, mask = jnp.concatenate([own, rest.astype(f32)]), ways // 2
    while mask > 1:
        half = have.shape[0] // 2
        have = have[:half] + over_ctx(have[half:].astype(bf16), 2 * mask).astype(f32)
        mask //= 2
    half = have.shape[0] // 2
    return have[:half], over_ctx(have[half:].astype(bf16), 2)


def norm_parts(value):
    centred = value - jnp.mean(value, axis=-1, keepdims=True)
    inverse = lax.rsqrt(jnp.mean(centred * centred, axis=-1, keepdims=True) + EPS)
    return centred * inverse, inverse


def norm_back(grad, normal, inverse, gain):
    inner = grad * gain
    return inverse * (
        inner
        - jnp.mean(inner, axis=-1, keepdims=True)
        - normal * jnp.mean(inner * normal, axis=-1, keepdims=True)
    )


def column_sums(*values):
    rows = [jnp.sum(value, axis=0, keepdims=True) for value in values]
    return jnp.concatenate(rows + [jnp.zeros_like(rows[0])] * (8 - len(rows)))


def out_kernel(
    core_ref, att_ref, mine_ref, other_ref, x_ref, vec_ref, normal_ref, inverse_ref, normed_ref, hidden_ref
):
    half = mine_ref.shape[1]
    core = core_ref[0]
    for way, ref in ((core, mine_ref), (1 - core, other_ref)):
        hidden_ref[:, pl.ds(pl.multiple_of(way * half, half), half)] = dot(att_ref[...], ref[...])
    hidden1 = hidden_ref[...] + (x_ref[...].astype(f32) + vec_ref[0:1, :]) + vec_ref[1:2, :]
    normal, inverse = norm_parts(hidden1)
    normal_ref[...] = normal
    inverse_ref[...] = inverse
    normed_ref[...] = (normal * vec_ref[2:3, :] + vec_ref[3:4, :]).astype(bf16)


def views(refs, width):
    if len(refs) == 2:
        return refs
    return refs[0].at[:, : refs[0].shape[1] - width], refs[0].at[:, refs[0].shape[1] - width :]


def forward_kernel(count, first, rows_ref, bias_ref, *refs):
    up_ref, down_ref = views(refs[:count], rows_ref.shape[1])
    act_ref, slope_ref, feed_ref = refs[-3:]
    upward = dot(rows_ref[...], up_ref[...]) + bias_ref[...]
    lower = 0.5 + 0.5 * lax.erf(upward * math.sqrt(0.5))
    density = jnp.exp2(upward * upward * (-0.5 * LOG2E)) * (1.0 / math.sqrt(2.0 * math.pi))
    act = (upward * lower).astype(bf16)
    act_ref[...] = act
    slope_ref[...] = lower + upward * density
    feed = dot(act, down_ref[...])
    if not first:
        feed = feed + refs[count][...]
    feed_ref[...] = feed.astype(feed_ref.dtype)


def feed_forward(rows, weights, bias, feed, dtype):
    count, group_ff = rows.shape[0], bias.shape[1]
    return kernel_call(
        functools.partial(forward_kernel, len(weights), feed is None),
        [shape((count, group_ff), bf16), shape((count, group_ff)), shape(rows.shape, dtype)],
        [rows, bias, *weights] + ([] if feed is None else [feed]),
    )


def backward_kernel(count, first, rows_ref, slope_ref, *refs):
    up_ref, down_ref = views(refs[:count], rows_ref.shape[1])
    d_up_ref, sum_ref, total_ref = refs[-3:]
    d_up = (dot(rows_ref[...], down_ref[...], ((1,), (1,))) * slope_ref[...]).astype(bf16)
    d_up_ref[...] = d_up
    sum_ref[...] = column_sums(d_up.astype(f32))
    total = dot(d_up, up_ref[...], ((1,), (1,)))
    if not first:
        total = total + refs[count][...]
    total_ref[...] = total.astype(total_ref.dtype)


def feed_backward(rows, weights, slope, total, dtype):
    count, group_ff = slope.shape
    return kernel_call(
        functools.partial(backward_kernel, len(weights), total is None),
        [shape((count, group_ff), bf16), shape((8, group_ff)), shape(rows.shape, dtype)],
        [rows, slope, *weights] + ([] if total is None else [total]),
    )


def turn_kernel(
    normal_ref, feed_ref, got_ref, cot_ref, vec_ref, keep_ref, send_ref, d_hidden_ref, d_feed_ref, sum_ref
):
    normed1 = normal_ref[...] * vec_ref[2:3, :] + vec_ref[3:4, :]
    hidden2 = normed1 + (feed_ref[...] + got_ref[...].astype(f32) + vec_ref[4:5, :])
    normal, inverse = norm_parts(hidden2)
    gain = vec_ref[5:6, :]
    result = (normal * gain + vec_ref[6:7, :]).astype(bf16)
    keep_ref[...] = result[: keep_ref.shape[0]]
    send_ref[...] = result[keep_ref.shape[0] :]
    cot = cot_ref[...].astype(f32)
    d_hidden2 = norm_back(cot, normal, inverse, gain)
    d_hidden_ref[...] = d_hidden2
    d_feed = d_hidden2.astype(bf16)
    d_feed_ref[...] = d_feed
    sum_ref[...] = column_sums(cot * normal, cot, d_feed.astype(f32))


def branch_kernel(
    core_ref, d_hidden2_ref, own_ref, got_ref, normal_ref, inverse_ref, mine_ref, other_ref, vec_ref,
    d_hidden1_ref, d_branch_ref, near_ref, far_ref, sum_ref,
):
    core, half, near = core_ref[0], mine_ref.shape[1], near_ref.shape[1]
    d_normed = d_hidden2_ref[...] + (own_ref[...] + got_ref[...].astype(f32))
    normal = normal_ref[...]
    d_hidden1 = norm_back(d_normed, normal, inverse_ref[...], vec_ref[2:3, :])
    d_hidden1_ref[...] = d_hidden1
    d_branch = d_hidden1.astype(bf16)
    d_branch_ref[...] = d_branch
    first = d_branch_ref[:, pl.ds(pl.multiple_of(core * half, half), half)]
    second = d_branch_ref[:, pl.ds(pl.multiple_of((1 - core) * half, half), half)]
    for ref, start in ((far_ref, near), (near_ref, 0)):
        span = slice(start, start + ref.shape[1])
        ref[...] = (
            dot(first, mine_ref[span, :], ((1,), (1,)))
            + dot(second, other_ref[span, :], ((1,), (1,)))
        ).astype(bf16)
    sum_ref[...] = column_sums(d_normed * normal, d_normed, d_branch.astype(f32))


def grad_kernel(one_ref, two_ref, left_ref, right_ref, out_ref):
    out_ref[...] = (
        dot(one_ref[...], left_ref[...], ((0,), (0,))) + dot(two_ref[...], right_ref[...], ((0,), (0,)))
    ).astype(bf16)


def grad_split_kernel(shard, odd_ref, keep_ref, got_ref, near_ref, far_ref):
    odd = odd_ref[0]
    for parity, ref in ((1 - odd, far_ref), (odd, near_ref)):
        for j in range(ref.shape[0]):
            rows = pl.ds(pl.multiple_of((2 * j + parity) * shard, shard), shard)
            ref[j] = (keep_ref[rows, :].astype(f32) + got_ref[rows, :].astype(f32)).astype(bf16)


def add_kernel(near_ref, got_ref, out_ref):
    out_ref[...] = (near_ref[...].astype(f32) + got_ref[...].astype(f32)).astype(out_ref.dtype)


def out_grad_kernel(ctx_ref, att_ref, d_branch_ref, keep_ref, send_ref):
    ctx = ctx_ref[0]
    core = ctx_ref[1]
    group, half = ctx_ref_group(att_ref, keep_ref), keep_ref.shape[1]
    for way, ref in ((core, keep_ref), (1 - core, send_ref)):
        columns = d_branch_ref[:, pl.ds(pl.multiple_of(way * half, half), half)]
        grad = dot(att_ref[...], columns, ((0,), (0,)))
        for i in range(grad.shape[0] // group):
            start = pl.multiple_of((ctx ^ i) * group, group)
            ref[pl.ds(start, group), :] = grad[i * group : (i + 1) * group].astype(ref.dtype)


def ctx_ref_group(att_ref, keep_ref):
    return att_ref.shape[1] // lax.axis_size("ctx")


def split_kernel(bit_ref, keep_ref, got_ref, kept_ref, send_ref):
    half = kept_ref.shape[1]
    for way, ref in ((bit_ref[0], kept_ref), (1 - bit_ref[0], send_ref)):
        span = pl.ds(pl.multiple_of(way * half, half), half)
        ref[...] = (keep_ref[:, span] + got_ref[:, span].astype(f32)).astype(ref.dtype)


def pack(values):
    high = values.astype(bf16)
    return jnp.concatenate([high, (values - high.astype(f32)).astype(bf16)])


def unpack(rows):
    return rows[:VEC].astype(f32) + rows[VEC:].astype(f32)


def qkv_send_kernel(shard, r0_ref, dq_ref, dkv_ref, out_ref):
    width = dq_ref.shape[1]
    query = dot(r0_ref[...], dq_ref[...], ((0,), (0,)))
    pair = dot(r0_ref[...], dkv_ref[...], ((0,), (0,)))
    for block in range(out_ref.shape[0]):
        rows = slice(block * shard, (block + 1) * shard)
        out_ref[block, :, :width] = query[rows].astype(bf16)
        out_ref[block, :, width:] = pair[rows].astype(bf16)


def split_by_parity(shard, odd, grad_ref, got_ref, vec_ref, near_ref, far_ref):
    for parity, ref in ((1 - odd, far_ref), (odd, near_ref)):
        for j in range(ref.shape[0]):
            block = 2 * j + parity
            rows = pl.ds(pl.multiple_of(block * shard, shard), shard)
            ref[j, :shard] = (grad_ref[rows, :] + got_ref[block].astype(f32)).astype(ref.dtype)
            vec = vec_ref[block]
            ref[j, shard:] = vec if ref.dtype == f32 else pack(vec)


def qkv_keep_kernel(
    shard, odd_ref, r0_ref, dq_ref, dkv_ref, got_ref, vec_ref, near_ref, far_ref, grad_ref
):
    width = dq_ref.shape[1]
    grad_ref[:, :width] = dot(r0_ref[...], dq_ref[...], ((0,), (0,)))
    grad_ref[:, width:] = dot(r0_ref[...], dkv_ref[...], ((0,), (0,)))
    split_by_parity(shard, odd_ref[0], grad_ref, got_ref, vec_ref, near_ref, far_ref)


def qkv_vec_keep_kernel(
    shard, place_ref, r0_ref, dq_ref, dkv_ref, dq_other_ref, dkv_other_ref, got_ref, sums1_ref, sums2_ref,
    up_own_ref, up_rest_ref, up_own_other_ref, up_rest_other_ref, near_ref, far_ref, grad_ref, flat_ref,
    up_ref, vec_ref,
):
    odd, ctx = place_ref[0], place_ref[1]
    width = dq_ref.shape[1]
    size = vec_ref.shape[0]
    flat_ref[...] = jnp.zeros_like(flat_ref)
    up_ref[...] = jnp.zeros_like(up_ref)
    vec_ref[...] = jnp.zeros_like(vec_ref)
    cut = up_own_ref.shape[1] // size
    pairs = (
        (dq_ref, dkv_ref, up_own_ref, up_rest_ref),
        (dq_other_ref, dkv_other_ref, up_own_other_ref, up_rest_other_ref),
    )
    for i, (query, pair, own, rest) in enumerate(pairs):
        who = ctx ^ i
        span = pl.ds(pl.multiple_of(who * width, width), width)
        flat_ref[0:1, span] = jnp.sum(query[...].astype(f32), axis=0, keepdims=True)
        flat_ref[1:2, span] = jnp.sum(pair[:, width:].astype(f32), axis=0, keepdims=True)
        for f in range(size):
            start = pl.multiple_of((f * (up_ref.shape[1] // cut // size) + who) * cut, cut)
            here = slice(f * cut, (f + 1) * cut)
            up_ref[0:1, pl.ds(start, cut)] = own[0:1, here] + rest[0:1, here]
    full = flat_ref.shape[1]
    model = (flat_ref[0:1], flat_ref[1:2], sums1_ref[2:3], sums2_ref[2:3])
    rows = (model, (up_ref[0:1],), (sums1_ref[0:1], sums2_ref[0:1]), (sums1_ref[1:2], sums2_ref[1:2]))
    for row, sources in enumerate(rows):
        length = sources[0].shape[1]
        part = len(sources) * length // size
        for f in range(size):
            source, start = sources[f * part // length], f * part % length
            vec_ref[f, row : row + 1, :part] = source[:, start : start + part]
    grad_ref[:, :width] = dot(r0_ref[...], dq_ref[...], ((0,), (0,)))
    grad_ref[:, width:] = dot(r0_ref[...], dkv_ref[...], ((0,), (0,)))
    split_by_parity(shard, odd, grad_ref, got_ref, vec_ref, near_ref, far_ref)


def input_kernel(dq_ref, dkv_ref, dq_other_ref, dkv_other_ref, mine_ref, other_ref, own_ref, rest_ref):
    width = dq_ref.shape[1]
    cut = own_ref.shape[0]
    for ref, rows in ((rest_ref, slice(cut, dq_ref.shape[0])), (own_ref, slice(0, cut))):
        total = 0.0
        for query, pair, weights in (
            (dq_ref, dkv_ref, mine_ref), (dq_other_ref, dkv_other_ref, other_ref)
        ):
            total = total + dot(query[rows, :], weights[:, :width], ((1,), (1,)))
            total = total + dot(pair[rows, :], weights[:, width:], ((1,), (1,)))
        ref[...] = total.astype(ref.dtype)


def input_sum_kernel(one_ref, two_ref, got_ref, keep_ref, send_ref):
    total = one_ref[...] + (two_ref[...] + got_ref[...].astype(f32))
    keep_ref[...] = total[: keep_ref.shape[0]]
    send_ref[...] = total[keep_ref.shape[0] :]


def out_keep_kernel(shard, odd_ref, keep_ref, got_ref, near_ref, far_ref):
    odd = odd_ref[0]
    for parity, ref in ((1 - odd, far_ref), (odd, near_ref)):
        for j in range(ref.shape[0]):
            rows = pl.ds(pl.multiple_of((2 * j + parity) * shard, shard), shard)
            ref[j] = (keep_ref[rows, :] + got_ref[rows, :].astype(f32)).astype(ref.dtype)


def z_send_kernel(shard, z_ref, near_ref, got_ref, out_near_ref, out_got_ref, *outs):
    z = z_ref[0]
    columns = near_ref.shape[2]
    for k, ref in enumerate(outs):
        block = z ^ k
        got = got_ref[block]
        near = near_ref[block]
        ref[:shard, :columns] = (near[:shard] + got[:shard].astype(f32)).astype(ref.dtype)
        ref[:shard, columns:] = (
            out_near_ref[block] + out_got_ref[block].astype(f32)
        ).astype(ref.dtype)
        vec = near[shard:] + unpack(got[shard:])
        ref[shard:, :columns] = vec if ref.dtype == f32 else pack(vec)
        ref[shard:, columns:] = jnp.zeros_like(ref[shard:, columns:])


def z_sum_kernel(shard, mine_ref, *refs):
    gots, out_ref = refs[:-1], refs[-1]
    value, vec = mine_ref[:shard], mine_ref[shard:]
    for ref in gots:
        value = value + ref[:shard].astype(f32)
        vec = vec + unpack(ref[shard:])
    out_ref[:shard] = value.astype(bf16)
    out_ref[shard:] = pack(vec)


def tail_kernel(shard, group, ctx_ref, *refs):
    pieces, (qkv_ref, out_ref, vec_ref) = refs[:4], refs[4:]
    ctx = ctx_ref[0]
    width = 4 * group
    for i, piece in enumerate(pieces):
        who = ctx ^ i
        for third in range(3):
            start = pl.multiple_of(third * width + who * group, group)
            qkv_ref[:, pl.ds(start, group)] = piece[
                :shard, third * group : (third + 1) * group
            ].astype(f32)
        start = pl.multiple_of(((who % 2) * 2 + who // 2) * group, group)
        out_ref[:, pl.ds(start, group)] = piece[:shard, 3 * group :].astype(f32)
    vec = [unpack(piece[shard:, : 3 * group]) for piece in pieces]
    vec_ref[...] = (vec[0] + vec[1]) + (vec[2] + vec[3])


def rows_tail_kernel(rows, ctx_ref, *refs):
    pieces, out_ref = refs[:-1], refs[-1]
    for i, piece in enumerate(pieces):
        start = pl.multiple_of((ctx_ref[0] ^ i) * rows, rows)
        out_ref[pl.ds(start, rows), :] = piece[...].astype(f32)


def columns_tail_kernel(cut, ctx_ref, *refs):
    pieces, out_ref = refs[:-1], refs[-1]
    for i, piece in enumerate(pieces):
        for block in range(piece.shape[1] // cut):
            start = pl.multiple_of((block * len(pieces) + (ctx_ref[0] ^ i)) * cut, cut)
            out_ref[:, pl.ds(start, cut)] = piece[:, block * cut : (block + 1) * cut].astype(f32)


def per_device(
    inputs, timestep, doc_ids, w_qkv, w_out, w_up, w_down, bias_model, bias_up,
    norm_gains, norm_shifts, cotangent,
):
    ctx, ctx_size = lax.axis_index("ctx"), lax.axis_size("ctx")
    fsdp, fsdp_size = lax.axis_index("fsdp"), lax.axis_size("fsdp")
    core, ways = ctx % 2, ctx_size // 2
    tokens, width = inputs.shape[2], w_out.shape[1]
    hidden = w_up.shape[1]
    head_size = width // HEADS
    own_rows = 2 * tokens
    rest_rows = (ways - 1) * own_rows
    group = width // ctx_size
    columns = 3 * group
    group_ff = hidden // ctx_size
    shard = w_out.shape[0]
    shard_ff = w_down.shape[0]
    cut_ff = hidden // (fsdp_size * ctx_size)
    fsdp_range = jnp.arange(fsdp_size)
    natural = fsdp_range ^ fsdp

    small = jnp.concatenate([bias_model, bias_up, norm_gains, norm_shifts])
    small_count = small.shape[0]
    qkv_group = lax.dynamic_index_in_dim(
        w_qkv.reshape(shard, 3, ctx_size, group), ctx, 2, False
    ).reshape(shard, columns)
    small_rows = jnp.pad(small, (0, PAD * columns - small_count)).reshape(PAD, columns)
    out_send = lax.dynamic_index_in_dim(w_out.reshape(shard, 2, width // 2), core, 1, False)
    first_send = jnp.concatenate(
        [
            jnp.concatenate([qkv_group, small_rows]),
            jnp.concatenate([out_send, jnp.zeros((PAD, width // 2), bf16)]),
        ],
        axis=1,
    )
    first_pieces = gather_far(gather_near(first_send))
    up_send = lax.dynamic_index_in_dim(
        w_up.reshape(shard, fsdp_size, ctx_size, cut_ff), ctx, 2, False
    ).reshape(shard, group_ff)
    down_send = lax.dynamic_index_in_dim(
        w_down.reshape(ctx_size, shard_ff // ctx_size, width), ctx, 0, False
    )
    merged = up_send.shape == down_send.shape and ctx_size == 4 and cut_ff % 128 == 0
    feed_sends = [jnp.concatenate([up_send, down_send], axis=1)] if merged else [up_send, down_send]
    feed_mine = [lax.all_gather(send, "fsdp", axis=0, tiled=True) for send in feed_sends]

    docs = doc_ids[:, 0].astype(bf16)
    doc_rows = jnp.pad(docs[:, None, :], ((0, 0), (0, PAD - 1), (0, width - tokens)))
    mine, theirs = (
        [lax.dynamic_index_in_dim(a, c, 0, False) for a in (inputs[:, 0], doc_rows, cotangent[:, 0])]
        for c in (core, 1 - core)
    )
    swapped = over_ctx(jnp.concatenate(theirs), 1)
    x_own = jnp.concatenate([mine[0], swapped[:tokens]])
    cot_own = jnp.concatenate([mine[2], swapped[tokens + PAD :]])
    doc_own = jnp.concatenate([mine[1][:1, :tokens], swapped[tokens : tokens + 1, :tokens]], axis=1)
    packed = jnp.concatenate([x_own, jnp.pad(doc_own, ((0, PAD - 1), (0, width - own_rows)))])
    rest = gather_tokens(packed).reshape(ways - 1, own_rows + PAD, width)
    x_rest = rest[:, :own_rows].reshape(rest_rows, width)
    doc_all = jnp.concatenate([doc_own[0], rest[:, own_rows, :own_rows].reshape(-1)]).astype(f32)
    key_docs, query_docs = doc_all[:, None], doc_all[None, :]
    time_row = lax.dynamic_index_in_dim(timestep[:, 0], core, 0, True).astype(f32)
    rounded0 = (jnp.concatenate([x_own, x_rest]).astype(f32) + time_row).astype(bf16)

    ratio = fsdp_size // ctx_size
    orders = [natural] + [
        ((natural // ratio) ^ who) * ratio + natural % ratio for who in (ctx, ctx ^ 1)
    ]
    w_qkv_mine, small_all, out_mine, out_theirs = place(first_pieces, orders, shard, columns)
    w_qkv_pair = (w_qkv_mine, over_ctx(w_qkv_mine, 1))
    small_all = small_all.reshape(fsdp_size, PAD * columns)[:, :small_count].astype(f32)
    starts = [0, bias_model.shape[0]]
    starts.append(starts[1] + bias_up.shape[0])
    starts.append(starts[2] + norm_gains.shape[0])
    starts.append(small_count)
    b_model, b_up, gains, shifts = (
        small_all[:, a:b].reshape(-1) for a, b in zip(starts[:-1], starts[1:])
    )
    vecs = jnp.stack(
        [
            time_row[0], b_model[2 * width : 3 * width], gains[:width], shifts[:width],
            b_model[3 * width :], gains[width:], shifts[width:], jnp.zeros((width,), f32),
        ]
    )
    b_up_groups = b_up.reshape(fsdp_size, ctx_size, cut_ff)

    b_up_pair = [
        lax.dynamic_index_in_dim(b_up_groups, ctx ^ i, 1, False).reshape(1, group_ff)
        for i in range(2)
    ]

    projected, attended, logs = [], [], []
    for i in range(2):
        who = ctx ^ i
        b_query = lax.dynamic_slice_in_dim(b_model, who * group, group)
        b_value = lax.dynamic_slice_in_dim(b_model, width + who * group, group)
        bias = jnp.concatenate([b_query, jnp.zeros_like(b_query), b_value])
        weights = after(w_qkv_pair[i], *attended, *b_up_pair, vecs, cot_own)
        proj = (dot(rounded0, weights) + bias[None]).astype(bf16)
        out, log = attend(proj, key_docs, query_docs, head_size)
        projected.append(proj)
        attended.append(out)
        logs.append(log)
    attended_pair = jnp.concatenate(attended, axis=1)
    attended_cols = [attended_pair[:own_rows]]
    for k in range(1, ways):
        attended_cols.append(over_ctx(attended_pair[k * own_rows : (k + 1) * own_rows], 2 * k))
    attended_own = jnp.concatenate(attended_cols, axis=1)

    out_other = over_ctx(out_theirs, 1)
    normal1, inverse1, normed_own = kernel_call(
        out_kernel,
        [shape((own_rows, width)), shape((own_rows, 1)), shape((own_rows, width), bf16)],
        [attended_own, out_mine, out_other, x_own, vecs],
        scalars=[core],
        scratch=[pltpu.VMEM((own_rows, width), f32)],
    )
    normed_rest = gather_tokens(normed_own)

    feed_mine = [after(w, normed_rest) for w in feed_mine]
    feed_pair = (feed_mine, [over_ctx(w, 1) for w in feed_mine])
    acts, slopes, feeds = {}, {}, {"rest": None, "own": None}
    token = normed_own
    for part, i in (("own", 0), ("rest", 0), ("rest", 1), ("own", 1)):
        rows = normed_own if part == "own" else normed_rest
        acts[part, i], slopes[part, i], feeds[part] = feed_forward(
            after(rows, token), feed_pair[i], b_up_pair[i], feeds[part],
            bf16 if i == 1 and part == "rest" else f32,
        )
        token = acts[part, i]
    feed_own, feed_got = reduce_tokens(feeds["own"], feeds["rest"])

    result_keep, result_send, d_hidden2, d_feed_own, sums2 = kernel_call(
        turn_kernel,
        [
            shape((tokens, width), bf16), shape((tokens, width), bf16), shape((own_rows, width)),
            shape((own_rows, width), bf16), shape((8, width)),
        ],
        [normal1, feed_own, feed_got, cot_own, vecs],
    )
    d_feed_rest = gather_tokens(d_feed_own)

    def gradient(args, flops=50_000_000_000):
        return kernel_call(grad_kernel, [shape((width, width), bf16)], args, flops=flops)[0]

    def split(kept, got):
        return kernel_call(
            functools.partial(grad_split_kernel, shard),
            [shape((fsdp_size // 2, shard, width), bf16)] * 2,
            [kept, got],
            scalars=[fsdp % 2],
        )

    sides = [[2 * k + p for k in range(fsdp_size // 2)] for p in range(2)]

    def finish(near, got):
        mixed = kernel_call(add_kernel, [shape(near.shape, bf16)], [near, got])[0]
        return mixed, lax.psum_scatter(
            mixed.reshape(-1, width), "fsdp", scatter_dimension=0, tiled=True,
            axis_index_groups=sides,
        )

    d_ups, d_up_sums, d_normed = {}, {}, {}
    token = d_feed_own
    for part, rows in (("own", d_feed_own), ("rest", d_feed_rest)):
        total = None
        if merged and part == "rest":
            down_args = [
                [acts["own", i], acts["rest", i], after(d_feed_own, token), d_feed_rest] for i in range(2)
            ]
            down_away = gradient(down_args[1])
            token = down_away
        for i in range(2):
            d_ups[part, i], d_up_sums[part, i], total = feed_backward(
                after(rows, token), feed_pair[i], slopes[part, i], total,
                bf16 if i == 1 and part == "rest" else f32,
            )
            token = d_ups[part, i]
        d_normed[part] = total
    dn_own, dn_got = reduce_tokens(d_normed["own"], d_normed["rest"])

    if merged:
        down_args[0][2] = after(d_feed_own, token)
        down_near, down_far = split(gradient(down_args[0]), over_ctx(down_away, 1))
        up_args = [
            [after(normed_own, down_far), normed_rest, d_ups["own", i], d_ups["rest", i]] for i in range(2)
        ]
        up_away = gradient(up_args[1], 0)
        up_near, up_far = split(gradient(up_args[0], 0), over_ctx(up_away, 1))
        dn_got = after(dn_got, up_far)
        down_got = over_fsdp(down_far, 1)
    else:
        totals = []
        for left, right in ((acts, None), (None, d_ups)):
            grads = []
            for i in range(2):
                one = jnp.concatenate([left["own", i], left["rest", i]]) if left else (
                    jnp.concatenate([normed_own, normed_rest])
                )
                two = jnp.concatenate([right["own", i], right["rest", i]]) if right else (
                    jnp.concatenate([d_feed_own, d_feed_rest])
                )
                grads.append(dot(one, two, ((0,), (0,))))
            mixed = (grads[0] + over_ctx(grads[1].astype(bf16), 1).astype(f32)).astype(bf16)
            totals.append(lax.psum_scatter(mixed, "fsdp", scatter_dimension=0, tiled=True))

    d_hidden1, d_branch, d_att_near, d_att_far, sums1 = kernel_call(
        branch_kernel,
        [
            shape((own_rows, width)), shape((own_rows, width), bf16),
            shape((own_rows, 2 * group), bf16), shape((own_rows, width - 2 * group), bf16),
            shape((8, width)),
        ],
        [d_hidden2, dn_own, dn_got, normal1, inverse1, out_mine, out_other, vecs],
        scalars=[core],
        flops=0,
    )
    if ways == 2:
        d_attended = [d_att_near, over_ctx(d_att_far, 2)]
    else:
        d_attended = [d_att_near] + [
            over_ctx(d_att_far[:, 2 * (k - 1) * group : 2 * k * group], 2 * k)
            for k in range(1, ways)
        ]

    d_projected = [None, None]
    for i in (1, 0):
        d_query, d_pair = attend_back(
            projected[i], d_attended, i * group, key_docs, query_docs, logs[i], head_size,
        )
        d_projected[i] = (d_query, d_pair)
        if i:
            qkv_away = kernel_call(
                functools.partial(qkv_send_kernel, shard),
                [shape((fsdp_size, shard, columns), bf16)],
                [rounded0, *d_projected[1]],
            )[0]
            token = qkv_away
            if merged:
                down_mixed, down_total = finish(down_near, after(down_got, qkv_away))
                up_got = over_fsdp(after(up_far, down_mixed), 1)
                token = down_mixed
            out_keep, out_away = kernel_call(
                out_grad_kernel,
                [shape((width, width // 2)), shape((width, width // 2), bf16)],
                [after(attended_own, token), d_branch],
                scalars=[jnp.stack([ctx, core])],
            )
            out_got = over_ctx(out_away, 1)
            for k in range(int(math.log2(ways))):
                half = out_keep.shape[1] // 2
                bit = (ctx >> (k + 1)) % 2
                if half % 128 == 0:
                    out_keep, out_away = kernel_call(
                        split_kernel, [shape((width, half)), shape((width, half), bf16)],
                        [out_keep, out_got], scalars=[bit],
                    )
                else:
                    both = (out_keep + out_got.astype(f32)).reshape(width, 2, half)
                    out_keep = lax.dynamic_index_in_dim(both, bit, 1, False)
                    out_away = lax.dynamic_index_in_dim(both, 1 - bit, 1, False).astype(bf16)
                out_got = over_ctx(out_away, 2 << k)
            d_attended[0] = after(d_attended[0], out_away)

    qkv_got = over_ctx(qkv_away, 1)
    keep_outs = [
        shape((fsdp_size // 2, shard + VEC, columns)),
        shape((fsdp_size // 2, shard + PAD, columns), bf16),
    ]
    quarter = out_keep.shape[1]
    if merged:
        near, far = kernel_call(
            functools.partial(qkv_vec_keep_kernel, shard),
            keep_outs,
            [
                rounded0, *d_projected[0], *d_projected[1], qkv_got, sums1, sums2,
                *(d_up_sums[part, i] for i in range(2) for part in ("own", "rest")),
            ],
            scalars=[jnp.stack([fsdp % 2, ctx])],
            scratch=[
                pltpu.VMEM((width, columns), f32), pltpu.VMEM((8, width), f32),
                pltpu.VMEM((8, hidden), f32), pltpu.VMEM((fsdp_size, VEC, columns), f32),
            ],
        )
    else:
        def in_groups(pair, size):
            stacked = jnp.stack(pair)
            ordered = jnp.where(core == 0, stacked, stacked[::-1])
            return lax.dynamic_update_slice_in_dim(
                jnp.zeros((ctx_size, size), f32), ordered, ctx - core, 0
            )

        column = lambda value: jnp.sum(value.astype(f32), axis=0)
        vec_query = in_groups([column(d[0]) for d in d_projected], group).reshape(-1)
        vec_value = in_groups([column(d[1][:, group:]) for d in d_projected], group).reshape(-1)
        vec_up = jnp.swapaxes(
            in_groups(
                [d_up_sums["own", i][0] + d_up_sums["rest", i][0] for i in range(2)], group_ff
            ).reshape(ctx_size, fsdp_size, cut_ff), 0, 1,
        ).reshape(fsdp_size, -1)
        vec_model = jnp.concatenate([vec_query, vec_value, sums1[2], sums2[2]]).reshape(fsdp_size, -1)
        vec_gain = jnp.concatenate([sums1[0], sums2[0]]).reshape(fsdp_size, -1)
        vec_shift = jnp.concatenate([sums1[1], sums2[1]]).reshape(fsdp_size, -1)
        vectors = jnp.concatenate([vec_model, vec_up, vec_gain, vec_shift], axis=1)
        vectors = jnp.pad(vectors, ((0, 0), (0, VEC * columns - small_count))).reshape(
            fsdp_size, VEC, columns
        )
        near, far = kernel_call(
            functools.partial(qkv_keep_kernel, shard),
            keep_outs,
            [rounded0, *d_projected[0], qkv_got, vectors],
            scalars=[fsdp % 2],
            scratch=[pltpu.VMEM((width, columns), f32)],
        )
    got = over_fsdp(far, 1)
    if merged:
        up_mixed, up_total = finish(up_near, after(up_got, far))
    out_near, out_far = kernel_call(
        functools.partial(out_keep_kernel, shard),
        [
            shape((fsdp_size // 2, shard, quarter)),
            shape((fsdp_size // 2, shard, quarter), bf16),
        ],
        [after(out_keep, far), out_got],
        scalars=[fsdp % 2],
    )
    out_cross = over_fsdp(out_far, 1)

    dx_own, dx_rest = kernel_call(
        input_kernel,
        [shape((own_rows, width)), shape((rest_rows, width), bf16)],
        [after(d_projected[0][0], out_far, got), d_projected[0][1], *d_projected[1], *w_qkv_pair],
    )
    if merged:
        got = after(got, up_mixed)
    sends = kernel_call(
        functools.partial(z_send_kernel, shard),
        [shape((shard + VEC, columns + quarter))]
        + [shape((shard + PAD, columns + quarter), bf16)] * (fsdp_size // 2 - 1),
        [near, got, out_near, out_cross],
        scalars=[fsdp // 2],
    )
    mine_block = sends[0]
    total = kernel_call(
        functools.partial(z_sum_kernel, shard),
        [shape((shard + PAD, columns + quarter), bf16)],
        [mine_block, *(over_fsdp(value, 2 * k) for k, value in enumerate(sends[1:], 1))],
    )[0]

    dx_own, dx_got = reduce_tokens(dx_own, dx_rest)
    input_keep, input_send = kernel_call(
        input_sum_kernel, [shape((tokens, width))] * 2, [d_hidden1, dx_own, dx_got]
    )

    if merged:
        def quarters(own, direct=False):
            if direct:
                return [own] + [over_ctx(own, i) for i in range(1, 4)]
            far_own = over_ctx(own, 2)
            other = over_ctx(jnp.concatenate([own, far_own]), 1)
            return [own, other[: own.shape[0]], far_own, other[own.shape[0] :]]

        grad_down = kernel_call(
            functools.partial(rows_tail_kernel, shard),
            [shape((shard_ff, width))],
            quarters(after(down_total, up_mixed)),
            scalars=[ctx],
        )[0]
        grad_up = kernel_call(
            functools.partial(columns_tail_kernel, cut_ff),
            [shape((shard, hidden))],
            quarters(up_total),
            scalars=[ctx],
        )[0]
        grad_qkv, grad_out, vec_done = kernel_call(
            functools.partial(tail_kernel, shard, group),
            [shape((shard, 3 * width)), shape((shard, width)), shape((VEC, columns))],
            quarters(total, direct=True),
            scalars=[ctx],
        )
        counts = [b - a for a, b in zip(starts[:-1], starts[1:])]
        vectors = [vec_done[row, :count] for row, count in enumerate(counts)]
    else:
        spread = lambda own: lax.all_gather(own, "ctx", axis=0)
        tail = spread(total)
        grad_qkv = jnp.transpose(
            tail[:, :shard, :columns].reshape(ctx_size, shard, 3, group), (1, 2, 0, 3)
        ).reshape(shard, 3 * width).astype(f32)
        order = []
        levels = int(math.log2(ctx_size))
        for place_index in range(ctx_size):
            order.append(
                sum(((place_index >> (levels - 1 - b)) & 1) << b for b in range(levels))
            )
        grad_out = jnp.concatenate([tail[d, :shard, columns:] for d in order], axis=1).astype(f32)
        vec = tail[:, shard:, :columns].astype(f32)
        vec_done = jnp.sum(vec[:, :VEC] + vec[:, VEC:], axis=0).reshape(-1)
        vectors = [vec_done[a:b] for a, b in zip(starts[:-1], starts[1:])]
        grad_down = spread(totals[0]).reshape(shard_ff, width).astype(f32)
        grad_up = jnp.transpose(
            spread(totals[1]).reshape(ctx_size, shard, fsdp_size, cut_ff), (1, 2, 0, 3)
        ).reshape(shard, hidden).astype(f32)

    def give_back(keep, send):
        got = over_ctx(send, 1)
        return jnp.stack([jnp.where(core == 0, keep, got), jnp.where(core == 0, got, keep)])

    block_output = give_back(result_keep, result_send)[:, None]
    input_grad = give_back(input_keep, input_send)[:, None]
    return (
        block_output, input_grad, grad_qkv, grad_out, grad_up, grad_down,
        *vectors,
    )


def solution(mesh):
    token = P(None, "fsdp", "ctx", None)
    rows = P("fsdp", None)
    flat = P("fsdp")
    return jax.shard_map(
        per_device,
        mesh=mesh,
        in_specs=(
            token, P(None, "fsdp", None), P(None, "fsdp", "ctx"), rows, rows, rows, rows,
            flat, flat, flat, flat, token,
        ),
        out_specs=(token, token, rows, rows, rows, rows, flat, flat, flat, flat),
        check_vma=False,
    )
```

profile of v0, /device:TPU:9, one launch (start us, length us, event | category | flops | bytes accessed | tf_op | source)
XLA Modules:
  0.0 328.3 jit_solution(11075776750204340440)
XLA Ops:
  18.2 2.6 reshape.208
  20.8 2.8 dynamic-slice_reduce_fusion
  25.6 2.5 collective-permute-done.5.refs_4_
  29.3 29.6 %collective-permute-done.7.refs_6_ = bf16[144,1280]{1,0:T(8,128)(2,1)S(1)} collective-permute-done((bf16[144,1280]{1,0:T(8,128)(2,1)S(1)}, bf16[144,1280]{1,0:T(8,128)(2,1)S(1)}, u32[]{:S(2)}, u32[]{:S(2)}) %collective-permute-start.7) | collective-permute-done | bytes 368672 | tf_op jit(solution)/shard_map/ppermute | solution.py:31
  69.9 4.9 %collective-permute-start.9 = (bf16[1024,768]{1,0:T(8,128)(2,1)}, bf16[1024,768]{1,0:T(8,128)(2,1)}, u32[]{:S(2)}, u32[]{:S(2)}) collective-permute-start(bf16[1024,768]{1,0:T(8,128)(2,1)} %copy-done.33), channel_id=1, source_target_pairs={{0,8},{8,0},{16,24},{24,16},{1,9},{9,1},{17,25},{25,17},{2,10},{10... | collective-permute-start | bytes 4718600 | tf_op jit(solution)/shard_map/ppermute | solution.py:26
  78.7 2.7 shard_map.196
  84.7 2.7 shard_map.197
  88.9 3.9 %collective-permute-done.10 = bf16[256,512]{1,0:T(8,128)(2,1)S(1)} collective-permute-done((bf16[256,512]{1,0:T(8,128)(2,1)S(1)}, bf16[256,512]{1,0:T(8,128)(2,1)S(1)}, u32[]{:S(2)}, u32[]{:S(2)}) %collective-permute-start.10) | collective-permute-done | bytes 262176 | tf_op jit(solution)/shard_map/ppermute | solution.py:26
  96.4 8.0 %collective-permute-done.12.rows_ref.two_ref = bf16[256,1024]{1,0:T(8,128)(2,1)S(1)} collective-permute-done((bf16[256,1024]{1,0:T(8,128)(2,1)S(1)}, bf16[256,1024]{1,0:T(8,128)(2,1)S(1)}, u32[]{:S(2)}, u32[]{:S(2)}) %collective-permute-start.12) | collective-permute-done | bytes 524320 | tf_op jit(solution)/shard_map/ppermute | solution.py:26
  105.6 3.8 %collective-permute-start.13 = (bf16[1024,2048]{1,0:T(8,128)(2,1)}, bf16[1024,2048]{1,0:T(8,128)(2,1)S(1)}, u32[]{:S(2)}, u32[]{:S(2)}) collective-permute-start(bf16[1024,2048]{1,0:T(8,128)(2,1)} %all-gather.2.cloned.1.call-done.refs_0_), channel_id=1, source_target_pairs={{0,8},{8,0},{16,24},{24,16},{1,9},{9,1},{17,25},{25,17},{2,10},{10... | collective-permute-start | bytes 12582920 | tf_op jit(solution)/shard_map/ppermute | solution.py:26
  121.1 10.2 %collective-permute-done.14.got_ref = bf16[256,1024]{1,0:T(8,128)(2,1)S(1)} collective-permute-done((bf16[256,1024]{1,0:T(8,128)(2,1)S(1)}, bf16[256,1024]{1,0:T(8,128)(2,1)S(1)}, u32[]{:S(2)}, u32[]{:S(2)}) %collective-permute-start.14) | collective-permute-done | bytes 524320 | tf_op jit(solution)/shard_map/ppermute | solution.py:26
  138.0 7.6 %collective-permute-done.16.right_ref.rows_ref = bf16[256,1024]{1,0:T(8,128)(2,1)S(1)} collective-permute-done((bf16[256,1024]{1,0:T(8,128)(2,1)S(1)}, bf16[256,1024]{1,0:T(8,128)(2,1)S(1)}, u32[]{:S(2)}, u32[]{:S(2)}) %collective-permute-start.16) | collective-permute-done | bytes 524320 | tf_op jit(solution)/shard_map/ppermute | solution.py:26
  145.6 2.6 shard_map.206
  165.2 6.5 %collective-permute-done.17.got_ref = bf16[256,1024]{1,0:T(8,128)(2,1)S(1)} collective-permute-done((bf16[256,1024]{1,0:T(8,128)(2,1)S(1)}, bf16[256,1024]{1,0:T(8,128)(2,1)S(1)}, u32[]{:S(2)}, u32[]{:S(2)}) %collective-permute-start.17) | collective-permute-done | bytes 524320 | tf_op jit(solution)/shard_map/ppermute | solution.py:26
  176.3 3.9 %collective-permute-start.20 = (bf16[4,128,1024]{2,1,0:T(8,128)(2,1)S(1)}, bf16[4,128,1024]{2,1,0:T(8,128)(2,1)S(1)}, u32[]{:S(2)}, u32[]{:S(2)}) collective-permute-start(bf16[4,128,1024]{2,1,0:T(8,128)(2,1)S(1)} %get-tuple-element.151), channel_id=1, source_target_pairs={{0,1},{1,0},{2,3},{3,2},{4,5},{5,4},{6,7},{7,6},{8,9},{9,8},{10,11... | collective-permute-start | bytes 3145736 | tf_op jit(solution)/shard_map/ppermute | solution.py:31
  181.4 4.2 %shard_map.215 = (bf16[512,256]{1,0:T(8,128)(2,1)S(1)}, bf16[512,512]{1,0:T(8,128)(2,1)S(1)}) custom-call(bf16[512,768]{1,0:T(8,128)(2,1)S(1)} %copy-done.5, bf16[512,768]{1,0:T(8,128)(2,1)S(1)} %copy-done.5, f32[512,1]{1,0:T(8,128)S(1)} %copy-done.7, f32[1,512]{1,0:T(1,128)S(1)} %copy-done.29, f32[4,512]{1,0:T(4,128)S(1)} %get-tuple-element.160.refs_4_, ...), custom_call_target="tpu_custom_call" | custom-call | bytes 1024 | tf_op jit(solution)/shard_map/pallas_call | solution.py:154
  186.8 15.3 %collective-permute-done.20.got_ref = bf16[4,128,1024]{2,1,0:T(8,128)(2,1)S(1)} collective-permute-done((bf16[4,128,1024]{2,1,0:T(8,128)(2,1)S(1)}, bf16[4,128,1024]{2,1,0:T(8,128)(2,1)S(1)}, u32[]{:S(2)}, u32[]{:S(2)}) %collective-permute-start.20) | collective-permute-done | bytes 1048608 | tf_op jit(solution)/shard_map/ppermute | solution.py:31
  215.2 4.1 %shard_map.220 = (bf16[512,256]{1,0:T(8,128)(2,1)S(1)}, bf16[512,512]{1,0:T(8,128)(2,1)S(1)}) custom-call(bf16[512,768]{1,0:T(8,128)(2,1)S(1)} %copy-done.3, bf16[512,768]{1,0:T(8,128)(2,1)S(1)} %copy-done.3, f32[512,1]{1,0:T(8,128)S(1)} %copy-done.8, f32[1,512]{1,0:T(1,128)S(1)} %copy-done.30, f32[4,512]{1,0:T(4,128)S(1)} %get-tuple-element.157.refs_4_, ...), custom_call_target="tpu_custom_call" | custom-call | bytes 1024 | tf_op jit(solution)/shard_map/pallas_call | solution.py:154
  219.5 2.9 shard_map.221
  224.0 10.9 %collective-permute-done.28.got_ref = bf16[4,128,1024]{2,1,0:T(8,128)(2,1)} collective-permute-done((bf16[4,128,1024]{2,1,0:T(8,128)(2,1)}, bf16[4,128,1024]{2,1,0:T(8,128)(2,1)}, u32[]{:S(2)}, u32[]{:S(2)}) %collective-permute-start.28) | collective-permute-done | bytes 1048608 | tf_op jit(solution)/shard_map/ppermute | solution.py:31
  241.6 4.5 %collective-permute-done.38.refs_2_ = bf16[128,1024]{1,0:T(8,128)(2,1)S(1)} collective-permute-done((bf16[128,1024]{1,0:T(8,128)(2,1)}, bf16[128,1024]{1,0:T(8,128)(2,1)S(1)}, u32[]{:S(2)}, u32[]{:S(2)}) %collective-permute-start.38) | collective-permute-done | bytes 262176 | tf_op jit(solution)/shard_map/ppermute | solution.py:26
  246.9 2.5 collective-permute-start.39
  249.4 4.3 %collective-permute-done.25.got_ref = bf16[4,144,768]{2,1,0:T(8,128)(2,1)S(1)} collective-permute-done((bf16[4,144,768]{2,1,0:T(8,128)(2,1)}, bf16[4,144,768]{2,1,0:T(8,128)(2,1)S(1)}, u32[]{:S(2)}, u32[]{:S(2)}) %collective-permute-start.25) | collective-permute-done | bytes 884768 | tf_op jit(solution)/shard_map/ppermute | solution.py:31
  253.7 5.7 %collective-permute-done.29.out_got_ref = bf16[4,128,256]{2,1,0:T(8,128)(2,1)S(1)} collective-permute-done((bf16[4,128,256]{2,1,0:T(8,128)(2,1)S(1)}, bf16[4,128,256]{2,1,0:T(8,128)(2,1)S(1)}, u32[]{:S(2)}, u32[]{:S(2)}) %collective-permute-start.29) | collective-permute-done | bytes 262176 | tf_op jit(solution)/shard_map/ppermute | solution.py:31
  261.2 5.6 %collective-permute-start.31 = (bf16[144,1024]{1,0:T(8,128)(2,1)S(1)}, bf16[144,1024]{1,0:T(8,128)(2,1)S(1)}, u32[]{:S(2)}, u32[]{:S(2)}) collective-permute-start(bf16[144,1024]{1,0:T(8,128)(2,1)S(1)} %get-tuple-element.196), channel_id=1, source_target_pairs={{0,4},{1,5},{2,6},{3,7},{4,0},{5,1},{6,2},{7,3},{8,12},{9,13},{10,... | collective-permute-start | bytes 884744 | tf_op jit(solution)/shard_map/ppermute | solution.py:31
  266.8 3.2 shard_map.223
  270.3 11.0 %collective-permute-done.30.refs_0_ = bf16[144,1024]{1,0:T(8,128)(2,1)S(1)} collective-permute-done((bf16[144,1024]{1,0:T(8,128)(2,1)S(1)}, bf16[144,1024]{1,0:T(8,128)(2,1)S(1)}, u32[]{:S(2)}, u32[]{:S(2)}) %collective-permute-start.30) | collective-permute-done | bytes 294944 | tf_op jit(solution)/shard_map/ppermute | solution.py:31
  281.2 2.6 collective-permute-done.31.refs_1_
  283.8 12.0 %collective-permute-done.32.refs_2_ = bf16[144,1024]{1,0:T(8,128)(2,1)S(1)} collective-permute-done((bf16[144,1024]{1,0:T(8,128)(2,1)S(1)}, bf16[144,1024]{1,0:T(8,128)(2,1)S(1)}, u32[]{:S(2)}, u32[]{:S(2)}) %collective-permute-start.32) | collective-permute-done | bytes 294944 | tf_op jit(solution)/shard_map/ppermute | solution.py:31
  302.5 2.6 collective-permute-done.34.refs_2_
  305.1 6.9 %collective-permute-done.35.refs_3_ = bf16[144,1024]{1,0:T(8,128)(2,1)S(1)} collective-permute-done((bf16[144,1024]{1,0:T(8,128)(2,1)S(1)}, bf16[144,1024]{1,0:T(8,128)(2,1)S(1)}, u32[]{:S(2)}, u32[]{:S(2)}) %collective-permute-start.35) | collective-permute-done | bytes 294944 | tf_op jit(solution)/shard_map/ppermute | solution.py:26
  314.0 3.0 collective-permute-done.36.refs_2_
  (331 shorter events, 117.2 us)
Async XLA Ops:
  7.2 98.4 %all-gather.2.cloned.1.call-start = ((), (), s32[]{:S(2)}) async-start(), calls=%async_computation.2 | async-start | bytes 4718592 | tf_op jit(solution)/shard_map/all_gather | solution.py:613
  9.6 15.6 %collective-permute-start.3 = (bf16[144,1280]{1,0:T(8,128)(2,1)S(1)}, bf16[144,1280]{1,0:T(8,128)(2,1)S(1)}, u32[]{:S(2)}, u32[]{:S(2)}) collective-permute-start(bf16[144,1280]{1,0:T(8,128)(2,1)S(1)} %fusion.3.refs_0_), channel_id=1, source_target_pairs={{0,2},{1,3},{2,0},{3,1},{4,6},{5,7},{6,4},{7,5},{8,10},{9,11},{10,... | collective-permute-start | bytes 1105928 | tf_op jit(solution)/shard_map/ppermute | solution.py:31
  9.7 18.4 %collective-permute-start.5 = (bf16[144,1280]{1,0:T(8,128)(2,1)S(1)}, bf16[144,1280]{1,0:T(8,128)(2,1)S(1)}, u32[]{:S(2)}, u32[]{:S(2)}) collective-permute-start(bf16[144,1280]{1,0:T(8,128)(2,1)S(1)} %fusion.3.refs_0_), channel_id=1, source_target_pairs={{0,4},{1,5},{2,6},{3,7},{4,0},{5,1},{6,2},{7,3},{8,12},{9,13},{10,... | collective-permute-start | bytes 1105928 | tf_op jit(solution)/shard_map/ppermute | solution.py:31
  12.2 46.7 %collective-permute-start.7 = (bf16[144,1280]{1,0:T(8,128)(2,1)S(1)}, bf16[144,1280]{1,0:T(8,128)(2,1)S(1)}, u32[]{:S(2)}, u32[]{:S(2)}) collective-permute-start(bf16[144,1280]{1,0:T(8,128)(2,1)S(1)} %fusion.3.refs_0_), channel_id=1, source_target_pairs={{0,6},{1,7},{2,4},{3,5},{4,2},{5,3},{6,0},{7,1},{8,14},{9,15},{10,... | collective-permute-start | bytes 1105928 | tf_op jit(solution)/shard_map/ppermute | solution.py:31
  12.4 51.7 %collective-permute-start.2 = (bf16[144,1280]{1,0:T(8,128)(2,1)S(1)}, bf16[144,1280]{1,0:T(8,128)(2,1)}, u32[]{:S(2)}, u32[]{:S(2)}) collective-permute-start(bf16[144,1280]{1,0:T(8,128)(2,1)S(1)} %fusion.3.refs_0_), channel_id=1, source_target_pairs={{0,1},{1,0},{2,3},{3,2},{4,5},{5,4},{6,7},{7,6},{8,9},{9,8},{10,11... | collective-permute-start | bytes 1105928 | tf_op jit(solution)/shard_map/ppermute | solution.py:31
  16.4 43.7 %collective-permute-start = (bf16[272,1024]{1,0:T(8,128)(2,1)}, bf16[272,1024]{1,0:T(8,128)(2,1)}, u32[]{:S(2)}, u32[]{:S(2)}) collective-permute-start(bf16[272,1024]{1,0:T(8,128)(2,1)} %pad_maximum_fusion), channel_id=1, source_target_pairs={{0,8},{8,0},{16,24},{24,16},{1,9},{9,1},{17,25},{25,17},{2,10},{10... | collective-permute-start | bytes 1671176 | tf_op jit(solution)/shard_map/ppermute | solution.py:26
  24.5 215.1 %reduce-scatter.5.cloned.1.call-start = ((), (), s32[]{:S(2)}) async-start(), calls=%async_computation.4 | async-start | bytes 1310720 | tf_op jit(solution)/shard_map/reduce_scatter | solution.py:726
  25.3 38.8 %collective-permute-start.4 = (bf16[144,1280]{1,0:T(8,128)(2,1)S(1)}, bf16[144,1280]{1,0:T(8,128)(2,1)S(1)}, u32[]{:S(2)}, u32[]{:S(2)}) collective-permute-start(bf16[144,1280]{1,0:T(8,128)(2,1)S(1)} %collective-permute-done.3.refs_2_), channel_id=1, source_target_pairs={{0,1},{1,0},{2,3},{3,2},{4,5},{5,4},{6,7},{7,6},{8,9},{9,8},{10,11... | collective-permute-start | bytes 1105928 | tf_op jit(solution)/shard_map/ppermute | solution.py:31
  28.1 35.9 %collective-permute-start.6 = (bf16[144,1280]{1,0:T(8,128)(2,1)S(1)}, bf16[144,1280]{1,0:T(8,128)(2,1)S(1)}, u32[]{:S(2)}, u32[]{:S(2)}) collective-permute-start(bf16[144,1280]{1,0:T(8,128)(2,1)S(1)} %collective-permute-done.5.refs_4_), channel_id=1, source_target_pairs={{0,1},{1,0},{2,3},{3,2},{4,5},{5,4},{6,7},{7,6},{8,9},{9,8},{10,11... | collective-permute-start | bytes 1105928 | tf_op jit(solution)/shard_map/ppermute | solution.py:31
  62.7 12.3 %collective-permute-start.1 = (bf16[272,1024]{1,0:T(8,128)(2,1)}, bf16[272,1024]{1,0:T(8,128)(2,1)}, u32[]{:S(2)}, u32[]{:S(2)}) collective-permute-start(bf16[272,1024]{1,0:T(8,128)(2,1)} %fusion.2), channel_id=1, source_target_pairs={{0,16},{8,24},{16,0},{24,8},{1,17},{9,25},{17,1},{25,9},{2,18},{10... | collective-permute-start | bytes 1671176 | tf_op jit(solution)/shard_map/ppermute | solution.py:26
  69.9 12.4 %collective-permute-start.9 = (bf16[1024,768]{1,0:T(8,128)(2,1)}, bf16[1024,768]{1,0:T(8,128)(2,1)}, u32[]{:S(2)}, u32[]{:S(2)}) collective-permute-start(bf16[1024,768]{1,0:T(8,128)(2,1)} %copy-done.33), channel_id=1, source_target_pairs={{0,8},{8,0},{16,24},{24,16},{1,9},{9,1},{17,25},{25,17},{2,10},{10... | collective-permute-start | bytes 4718600 | tf_op jit(solution)/shard_map/ppermute | solution.py:26
  74.8 18.1 %collective-permute-start.11 = (bf16[1024,512]{1,0:T(8,128)(2,1)}, bf16[1024,512]{1,0:T(8,128)(2,1)S(1)}, u32[]{:S(2)}, u32[]{:S(2)}) collective-permute-start(bf16[1024,512]{1,0:T(8,128)(2,1)} %copy-done.39), channel_id=1, source_target_pairs={{0,8},{8,0},{16,24},{24,16},{1,9},{9,1},{17,25},{25,17},{2,10},{10... | collective-permute-start | bytes 3145736 | tf_op jit(solution)/shard_map/ppermute | solution.py:26
  105.6 10.8 %collective-permute-start.13 = (bf16[1024,2048]{1,0:T(8,128)(2,1)}, bf16[1024,2048]{1,0:T(8,128)(2,1)S(1)}, u32[]{:S(2)}, u32[]{:S(2)}) collective-permute-start(bf16[1024,2048]{1,0:T(8,128)(2,1)} %all-gather.2.cloned.1.call-done.refs_0_), channel_id=1, source_target_pairs={{0,8},{8,0},{16,24},{24,16},{1,9},{9,1},{17,25},{25,17},{2,10},{10... | collective-permute-start | bytes 12582920 | tf_op jit(solution)/shard_map/ppermute | solution.py:26
  118.0 13.2 %collective-permute-start.14 = (bf16[256,1024]{1,0:T(8,128)(2,1)S(1)}, bf16[256,1024]{1,0:T(8,128)(2,1)S(1)}, u32[]{:S(2)}, u32[]{:S(2)}) collective-permute-start(bf16[256,1024]{1,0:T(8,128)(2,1)S(1)} %get-tuple-element.127), channel_id=1, source_target_pairs={{0,16},{8,24},{16,0},{24,8},{1,17},{9,25},{17,1},{25,9},{2,18},{10... | collective-permute-start | bytes 1572872 | tf_op jit(solution)/shard_map/ppermute | solution.py:26
  133.4 12.2 %collective-permute-start.16 = (bf16[256,1024]{1,0:T(8,128)(2,1)S(1)}, bf16[256,1024]{1,0:T(8,128)(2,1)S(1)}, u32[]{:S(2)}, u32[]{:S(2)}) collective-permute-start(bf16[256,1024]{1,0:T(8,128)(2,1)S(1)} %get-tuple-element.150.rows_ref.left_ref), channel_id=1, source_target_pairs={{0,16},{8,24},{16,0},{24,8},{1,17},{9,25},{17,1},{25,9},{2,18},{10... | collective-permute-start | bytes 1572872 | tf_op jit(solution)/shard_map/ppermute | solution.py:26
  158.6 13.1 %collective-permute-start.17 = (bf16[256,1024]{1,0:T(8,128)(2,1)S(1)}, bf16[256,1024]{1,0:T(8,128)(2,1)S(1)}, u32[]{:S(2)}, u32[]{:S(2)}) collective-permute-start(bf16[256,1024]{1,0:T(8,128)(2,1)S(1)} %get-tuple-element.148), channel_id=1, source_target_pairs={{0,16},{8,24},{16,0},{24,8},{1,17},{9,25},{17,1},{25,9},{2,18},{10... | collective-permute-start | bytes 1572872 | tf_op jit(solution)/shard_map/ppermute | solution.py:26
  176.3 25.8 %collective-permute-start.20 = (bf16[4,128,1024]{2,1,0:T(8,128)(2,1)S(1)}, bf16[4,128,1024]{2,1,0:T(8,128)(2,1)S(1)}, u32[]{:S(2)}, u32[]{:S(2)}) collective-permute-start(bf16[4,128,1024]{2,1,0:T(8,128)(2,1)S(1)} %get-tuple-element.151), channel_id=1, source_target_pairs={{0,1},{1,0},{2,3},{3,2},{4,5},{5,4},{6,7},{7,6},{8,9},{9,8},{10,11... | collective-permute-start | bytes 3145736 | tf_op jit(solution)/shard_map/ppermute | solution.py:31
  209.3 30.4 %collective-permute-start.15 = (bf16[128,1024]{1,0:T(8,128)(2,1)}, bf16[128,1024]{1,0:T(8,128)(2,1)}, u32[]{:S(2)}, u32[]{:S(2)}) collective-permute-start(bf16[128,1024]{1,0:T(8,128)(2,1)} %get-tuple-element.129), channel_id=1, source_target_pairs={{0,8},{8,0},{16,24},{24,16},{1,9},{9,1},{17,25},{25,17},{2,10},{10... | collective-permute-start | bytes 786440 | tf_op jit(solution)/shard_map/ppermute | solution.py:26
  209.3 10.1 %collective-permute-start.23 = (bf16[8,128,768]{2,1,0:T(8,128)(2,1)S(1)}, bf16[8,128,768]{2,1,0:T(8,128)(2,1)S(1)}, u32[]{:S(2)}, u32[]{:S(2)}) collective-permute-start(bf16[8,128,768]{2,1,0:T(8,128)(2,1)S(1)} %shard_map.216), channel_id=1, source_target_pairs={{0,8},{8,0},{16,24},{24,16},{1,9},{9,1},{17,25},{25,17},{2,10},{10... | collective-permute-start | bytes 4718600 | tf_op jit(solution)/shard_map/ppermute | solution.py:26
  209.8 25.0 %collective-permute-start.28 = (bf16[4,128,1024]{2,1,0:T(8,128)(2,1)}, bf16[4,128,1024]{2,1,0:T(8,128)(2,1)}, u32[]{:S(2)}, u32[]{:S(2)}) collective-permute-start(bf16[4,128,1024]{2,1,0:T(8,128)(2,1)} %copy-done.38), channel_id=1, source_target_pairs={{0,1},{1,0},{2,3},{3,2},{4,5},{5,4},{6,7},{7,6},{8,9},{9,8},{10,11... | collective-permute-start | bytes 3145736 | tf_op jit(solution)/shard_map/ppermute | solution.py:31
  211.3 90.0 %reduce-scatter.3.cloned.1.call-start = ((), (), s32[]{:S(2)}) async-start(), calls=%async_computation.3 | async-start | bytes 1310720 | tf_op jit(solution)/shard_map/reduce_scatter | solution.py:726
  215.1 19.7 %collective-permute-start.24 = (bf16[1024,256]{1,0:T(8,128)(2,1)S(1)}, bf16[1024,256]{1,0:T(8,128)(2,1)S(1)}, u32[]{:S(2)}, u32[]{:S(2)}) collective-permute-start(bf16[1024,256]{1,0:T(8,128)(2,1)S(1)} %get-tuple-element.169), channel_id=1, source_target_pairs={{0,16},{8,24},{16,0},{24,8},{1,17},{9,25},{17,1},{25,9},{2,18},{10... | collective-permute-start | bytes 1572872 | tf_op jit(solution)/shard_map/ppermute | solution.py:26
  222.4 31.2 %collective-permute-start.25 = (bf16[4,144,768]{2,1,0:T(8,128)(2,1)}, bf16[4,144,768]{2,1,0:T(8,128)(2,1)S(1)}, u32[]{:S(2)}, u32[]{:S(2)}) collective-permute-start(bf16[4,144,768]{2,1,0:T(8,128)(2,1)} %get-tuple-element.180), channel_id=1, source_target_pairs={{0,1},{1,0},{2,3},{3,2},{4,5},{5,4},{6,7},{7,6},{8,9},{9,8},{10,11... | collective-permute-start | bytes 2654216 | tf_op jit(solution)/shard_map/ppermute | solution.py:31
  235.7 23.7 %collective-permute-start.29 = (bf16[4,128,256]{2,1,0:T(8,128)(2,1)S(1)}, bf16[4,128,256]{2,1,0:T(8,128)(2,1)S(1)}, u32[]{:S(2)}, u32[]{:S(2)}) collective-permute-start(bf16[4,128,256]{2,1,0:T(8,128)(2,1)S(1)} %get-tuple-element.182), channel_id=1, source_target_pairs={{0,1},{1,0},{2,3},{3,2},{4,5},{5,4},{6,7},{7,6},{8,9},{9,8},{10,11... | collective-permute-start | bytes 786440 | tf_op jit(solution)/shard_map/ppermute | solution.py:31
  246.9 51.3 %collective-permute-start.39 = (bf16[256,1024]{1,0:T(8,128)(2,1)}, bf16[256,1024]{1,0:T(8,128)(2,1)}, u32[]{:S(2)}, u32[]{:S(2)}) collective-permute-start(bf16[256,1024]{1,0:T(8,128)(2,1)} %pad_maximum_fusion.6), channel_id=1, source_target_pairs={{0,8},{8,0},{16,24},{24,16},{1,9},{9,1},{17,25},{25,17},{2,10},{10... | collective-permute-start | bytes 1572872 | tf_op jit(solution)/shard_map/ppermute | solution.py:26
  261.1 20.1 %collective-permute-start.30 = (bf16[144,1024]{1,0:T(8,128)(2,1)S(1)}, bf16[144,1024]{1,0:T(8,128)(2,1)S(1)}, u32[]{:S(2)}, u32[]{:S(2)}) collective-permute-start(bf16[144,1024]{1,0:T(8,128)(2,1)S(1)} %get-tuple-element.195), channel_id=1, source_target_pairs={{0,2},{1,3},{2,0},{3,1},{4,6},{5,7},{6,4},{7,5},{8,10},{9,11},{10,... | collective-permute-start | bytes 884744 | tf_op jit(solution)/shard_map/ppermute | solution.py:31
  261.2 22.7 %collective-permute-start.31 = (bf16[144,1024]{1,0:T(8,128)(2,1)S(1)}, bf16[144,1024]{1,0:T(8,128)(2,1)S(1)}, u32[]{:S(2)}, u32[]{:S(2)}) collective-permute-start(bf16[144,1024]{1,0:T(8,128)(2,1)S(1)} %get-tuple-element.196), channel_id=1, source_target_pairs={{0,4},{1,5},{2,6},{3,7},{4,0},{5,1},{6,2},{7,3},{8,12},{9,13},{10,... | collective-permute-start | bytes 884744 | tf_op jit(solution)/shard_map/ppermute | solution.py:31
  266.8 29.0 %collective-permute-start.32 = (bf16[144,1024]{1,0:T(8,128)(2,1)S(1)}, bf16[144,1024]{1,0:T(8,128)(2,1)S(1)}, u32[]{:S(2)}, u32[]{:S(2)}) collective-permute-start(bf16[144,1024]{1,0:T(8,128)(2,1)S(1)} %get-tuple-element.197), channel_id=1, source_target_pairs={{0,6},{1,7},{2,4},{3,5},{4,2},{5,3},{6,0},{7,1},{8,14},{9,15},{10,... | collective-permute-start | bytes 884744 | tf_op jit(solution)/shard_map/ppermute | solution.py:31
  270.1 30.7 %collective-permute-start.26 = (bf16[256,1024]{1,0:T(8,128)(2,1)S(1)}, bf16[256,1024]{1,0:T(8,128)(2,1)S(1)}, u32[]{:S(2)}, u32[]{:S(2)}) collective-permute-start(bf16[256,1024]{1,0:T(8,128)(2,1)S(1)} %get-tuple-element.185), channel_id=1, source_target_pairs={{0,16},{8,24},{16,0},{24,8},{1,17},{9,25},{17,1},{25,9},{2,18},{10... | collective-permute-start | bytes 1572872 | tf_op jit(solution)/shard_map/ppermute | solution.py:26
  297.7 14.3 %collective-permute-start.35 = (bf16[144,1024]{1,0:T(8,128)(2,1)S(1)}, bf16[144,1024]{1,0:T(8,128)(2,1)S(1)}, u32[]{:S(2)}, u32[]{:S(2)}) collective-permute-start(bf16[144,1024]{1,0:T(8,128)(2,1)S(1)} %shard_map.227.refs_0_), channel_id=1, source_target_pairs={{0,24},{8,16},{16,8},{24,0},{1,25},{9,17},{17,9},{25,1},{2,26},{10... | collective-permute-start | bytes 884744 | tf_op jit(solution)/shard_map/ppermute | solution.py:26
  301.0 17.5 %collective-permute-start.27 = (f32[128,1024]{1,0:T(8,128)S(1)}, f32[128,1024]{1,0:T(8,128)S(1)}, u32[]{:S(2)}, u32[]{:S(2)}) collective-permute-start(f32[128,1024]{1,0:T(8,128)S(1)} %get-tuple-element.187), channel_id=1, source_target_pairs={{0,8},{8,0},{16,24},{24,16},{1,9},{9,1},{17,25},{25,17},{2,10},{10... | collective-permute-start | bytes 1572872 | tf_op jit(solution)/shard_map/ppermute | solution.py:26
  301.3 15.7 %collective-permute-start.36 = (bf16[128,1024]{1,0:T(8,128)(2,1)}, bf16[128,1024]{1,0:T(8,128)(2,1)S(1)}, u32[]{:S(2)}, u32[]{:S(2)}) collective-permute-start(bf16[128,1024]{1,0:T(8,128)(2,1)} %reduce-scatter.3.cloned.1.call-done.refs_0_), channel_id=1, source_target_pairs={{0,16},{8,24},{16,0},{24,8},{1,17},{9,25},{17,1},{25,9},{2,18},{10... | collective-permute-start | bytes 786440 | tf_op jit(solution)/shard_map/ppermute | solution.py:26
  (93 other events, 557.8 us)
Sparse Core Ops, SparseCore 0:
  24.7 80.9 all-gather.1
  211.4 26.2 reduce-scatter.4
  241.7 36.3 reduce-scatter.2
where the time goes:
time: 332 us; the launch traced here: 328 us
  waiting for transfers between devices  154 us (46%)
  Pallas kernels  60.2 us (18%)
  starting transfers between devices  53.8 us (16%)
  local copies, waits for them, and re-layouts  34.2 us (10%)
  between operations  15.6 us (5%)
  other arithmetic  7.22 us (2%)
  matrix products  3.38 us (1%)
    ppermute x14, waiting for transfers between devices, over_fsdp(): return lax.ppermute(value, 'fsdp', [(i, i ^ mask) for i in range(size)])  95.1 us
    ppermute x26, waiting for transfers between devices, over_ctx(): return lax.ppermute(value, 'ctx', [(i, i ^ mask) for i in range(size)])  57.5 us
    pallas_call x32, Pallas kernels, kernel_call(): pl.pallas_call(body, in_specs=specs, out_specs=[pl.BlockSpec(memory_space...  46.5 us
    ppermute x26, starting transfers between devices, over_ctx(): return lax.ppermute(value, 'ctx', [(i, i ^ mask) for i in range(size)])  32.3 us
    ppermute x14, starting transfers between devices, over_fsdp(): return lax.ppermute(value, 'fsdp', [(i, i ^ mask) for i in range(size)])  20.7 us
    unnamed x178, local copies, waits for them, and re-layouts  18.7 us
    pallas_call x2, Pallas kernels, attend_back(): pl.pallas_call(functools.partial(attend_back_kernel, head_size, 1.0 / mat...  8.34 us
  transfers between devices with their start and end apart: 43, of which 24 were waited for; matrix products, arithmetic and copies ran while one was open for 7% of the time, Pallas kernels for 13%

commit v1 on v0

--- a/solution.py
+++ b/solution.py
@@ -798,20 +798,19 @@
         )
         d_projected[i] = (d_query, d_pair)
         if i:
+            if merged:
+                down_mixed, down_total = finish(down_near, after(down_got, d_query))
+                up_got = over_fsdp(after(up_far, down_mixed), 1)
+                d_query = after(d_query, down_mixed)
             qkv_away = kernel_call(
                 functools.partial(qkv_send_kernel, shard),
                 [shape((fsdp_size, shard, columns), bf16)],
-                [rounded0, *d_projected[1]],
+                [rounded0, d_query, d_pair],
             )[0]
-            token = qkv_away
-            if merged:
-                down_mixed, down_total = finish(down_near, after(down_got, qkv_away))
-                up_got = over_fsdp(after(up_far, down_mixed), 1)
-                token = down_mixed
             out_keep, out_away = kernel_call(
                 out_grad_kernel,
                 [shape((width, width // 2)), shape((width, width // 2), bf16)],
-                [after(attended_own, token), d_branch],
+                [after(attended_own, qkv_away), d_branch],
                 scalars=[jnp.stack([ctx, core])],
             )
             out_got = over_ctx(out_away, 1)

time: 332 us -> 320 us (0.964)
  waiting for transfers between devices: 154 us -> 135 us
  starting transfers between devices: 53.8 us -> 59.2 us
    ppermute x14, waiting for transfers between devices: 95.1 us -> 77.4 us  [over_fsdp(): return lax.ppermute(value, 'fsdp', [(i, i ^ mask) for i in range(size)])]
    unnamed x178 -> x172, local copies, waits for them, and re-layouts: 18.7 us -> 19.8 us
  transfers between devices with their start and end apart: 43 -> 43, of which waited for: 24 -> 22; matrix products, arithmetic and copies ran while one was open for 7% -> 8% of each run, Pallas kernels for 13% -> 14%
where the time goes in v1:
time: 320 us; the launch traced here: 316 us
  waiting for transfers between devices  135 us (42%)
  Pallas kernels  60.7 us (19%)
  starting transfers between devices  59.2 us (18%)
  local copies, waits for them, and re-layouts  35.3 us (11%)
  between operations  15.6 us (5%)
  other arithmetic  7.19 us (2%)
  matrix products  3.37 us (1%)
    ppermute x14, waiting for transfers between devices, over_fsdp(): return lax.ppermute(value, 'fsdp', [(i, i ^ mask) for i in range(size)])  77.4 us
    ppermute x26, waiting for transfers between devices, over_ctx(): return lax.ppermute(value, 'ctx', [(i, i ^ mask) for i in range(size)])  56.1 us
    pallas_call x32, Pallas kernels, kernel_call(): pl.pallas_call(body, in_specs=specs, out_specs=[pl.BlockSpec(memory_space...  47 us
    ppermute x26, starting transfers between devices, over_ctx(): return lax.ppermute(value, 'ctx', [(i, i ^ mask) for i in range(size)])  35.2 us
    ppermute x14, starting transfers between devices, over_fsdp(): return lax.ppermute(value, 'fsdp', [(i, i ^ mask) for i in range(size)])  23.2 us
    unnamed x172, local copies, waits for them, and re-layouts  19.8 us
    pallas_call x2, Pallas kernels, attend_back(): pl.pallas_call(functools.partial(attend_back_kernel, head_size, 1.0 / mat...  8.34 us
  transfers between devices with their start and end apart: 43, of which 22 were waited for; matrix products, arithmetic and copies ran while one was open for 8% of the time, Pallas kernels for 14%

profile of v1, /device:TPU:9, one launch (start us, length us, event | category | flops | bytes accessed | tf_op | source)
XLA Modules:
  0.0 316.2 jit_solution(13548525577178007143)
XLA Ops:
  18.2 2.6 reshape.208
  20.8 2.8 dynamic-slice_reduce_fusion
  29.3 29.6 %collective-permute-done.7.refs_6_ = bf16[144,1280]{1,0:T(8,128)(2,1)S(1)} collective-permute-done((bf16[144,1280]{1,0:T(8,128)(2,1)S(1)}, bf16[144,1280]{1,0:T(8,128)(2,1)S(1)}, u32[]{:S(2)}, u32[]{:S(2)}) %collective-permute-start.7) | collective-permute-done | bytes 368672 | tf_op jit(solution)/shard_map/ppermute | solution.py:31
  69.9 4.9 %collective-permute-start.9 = (bf16[1024,768]{1,0:T(8,128)(2,1)}, bf16[1024,768]{1,0:T(8,128)(2,1)}, u32[]{:S(2)}, u32[]{:S(2)}) collective-permute-start(bf16[1024,768]{1,0:T(8,128)(2,1)} %copy-done.32), channel_id=1, source_target_pairs={{0,8},{8,0},{16,24},{24,16},{1,9},{9,1},{17,25},{25,17},{2,10},{10... | collective-permute-start | bytes 4718600 | tf_op jit(solution)/shard_map/ppermute | solution.py:26
  78.7 2.7 shard_map.196
  84.7 2.7 shard_map.197
  88.9 3.9 %collective-permute-done.10 = bf16[256,512]{1,0:T(8,128)(2,1)S(1)} collective-permute-done((bf16[256,512]{1,0:T(8,128)(2,1)S(1)}, bf16[256,512]{1,0:T(8,128)(2,1)S(1)}, u32[]{:S(2)}, u32[]{:S(2)}) %collective-permute-start.10) | collective-permute-done | bytes 262176 | tf_op jit(solution)/shard_map/ppermute | solution.py:26
  96.4 8.0 %collective-permute-done.12.rows_ref.two_ref = bf16[256,1024]{1,0:T(8,128)(2,1)S(1)} collective-permute-done((bf16[256,1024]{1,0:T(8,128)(2,1)S(1)}, bf16[256,1024]{1,0:T(8,128)(2,1)S(1)}, u32[]{:S(2)}, u32[]{:S(2)}) %collective-permute-start.12) | collective-permute-done | bytes 524320 | tf_op jit(solution)/shard_map/ppermute | solution.py:26
  105.6 3.8 %collective-permute-start.13 = (bf16[1024,2048]{1,0:T(8,128)(2,1)}, bf16[1024,2048]{1,0:T(8,128)(2,1)S(1)}, u32[]{:S(2)}, u32[]{:S(2)}) collective-permute-start(bf16[1024,2048]{1,0:T(8,128)(2,1)} %all-gather.2.cloned.1.call-done.refs_0_), channel_id=1, source_target_pairs={{0,8},{8,0},{16,24},{24,16},{1,9},{9,1},{17,25},{25,17},{2,10},{10... | collective-permute-start | bytes 12582920 | tf_op jit(solution)/shard_map/ppermute | solution.py:26
  121.1 10.2 %collective-permute-done.14.got_ref = bf16[256,1024]{1,0:T(8,128)(2,1)S(1)} collective-permute-done((bf16[256,1024]{1,0:T(8,128)(2,1)S(1)}, bf16[256,1024]{1,0:T(8,128)(2,1)S(1)}, u32[]{:S(2)}, u32[]{:S(2)}) %collective-permute-start.14) | collective-permute-done | bytes 524320 | tf_op jit(solution)/shard_map/ppermute | solution.py:26
  137.6 7.7 %collective-permute-done.16.right_ref.rows_ref = bf16[256,1024]{1,0:T(8,128)(2,1)S(1)} collective-permute-done((bf16[256,1024]{1,0:T(8,128)(2,1)S(1)}, bf16[256,1024]{1,0:T(8,128)(2,1)S(1)}, u32[]{:S(2)}, u32[]{:S(2)}) %collective-permute-start.16) | collective-permute-done | bytes 524320 | tf_op jit(solution)/shard_map/ppermute | solution.py:26
  145.2 2.6 shard_map.206
  159.6 3.9 %collective-permute-start.21 = (bf16[4,128,1024]{2,1,0:T(8,128)(2,1)S(1)}, bf16[4,128,1024]{2,1,0:T(8,128)(2,1)S(1)}, u32[]{:S(2)}, u32[]{:S(2)}) collective-permute-start(bf16[4,128,1024]{2,1,0:T(8,128)(2,1)S(1)} %get-tuple-element.152), channel_id=1, source_target_pairs={{0,1},{1,0},{2,3},{3,2},{4,5},{5,4},{6,7},{7,6},{8,9},{9,8},{10,11... | collective-permute-start | bytes 3145736 | tf_op jit(solution)/shard_map/ppermute | solution.py:31
  167.3 4.1 %collective-permute-done.17.got_ref = bf16[256,1024]{1,0:T(8,128)(2,1)S(1)} collective-permute-done((bf16[256,1024]{1,0:T(8,128)(2,1)S(1)}, bf16[256,1024]{1,0:T(8,128)(2,1)S(1)}, u32[]{:S(2)}, u32[]{:S(2)}) %collective-permute-start.17) | collective-permute-done | bytes 524320 | tf_op jit(solution)/shard_map/ppermute | solution.py:26
  175.9 5.2 %collective-permute-done.20.refs_6_ = bf16[256,512]{1,0:T(8,128)(2,1)S(1)} collective-permute-done((bf16[256,512]{1,0:T(8,128)(2,1)S(1)}, bf16[256,512]{1,0:T(8,128)(2,1)S(1)}, u32[]{:S(2)}, u32[]{:S(2)}) %collective-permute-start.20) | collective-permute-done | bytes 262176 | tf_op jit(solution)/shard_map/ppermute | solution.py:26
  181.1 4.2 %shard_map.215 = (bf16[512,256]{1,0:T(8,128)(2,1)S(1)}, bf16[512,512]{1,0:T(8,128)(2,1)S(1)}) custom-call(bf16[512,768]{1,0:T(8,128)(2,1)S(1)} %copy-done.5, bf16[512,768]{1,0:T(8,128)(2,1)S(1)} %copy-done.5, f32[512,1]{1,0:T(8,128)S(1)} %copy-done.7, f32[1,512]{1,0:T(1,128)S(1)} %copy-done.28, f32[4,512]{1,0:T(4,128)S(1)} %get-tuple-element.160.refs_4_, ...), custom_call_target="tpu_custom_call" | custom-call | bytes 1024 | tf_op jit(solution)/shard_map/pallas_call | solution.py:154
  194.2 3.9 %collective-permute-start.28 = (bf16[4,128,1024]{2,1,0:T(8,128)(2,1)}, bf16[4,128,1024]{2,1,0:T(8,128)(2,1)}, u32[]{:S(2)}, u32[]{:S(2)}) collective-permute-start(bf16[4,128,1024]{2,1,0:T(8,128)(2,1)} %copy-done.37), channel_id=1, source_target_pairs={{0,1},{1,0},{2,3},{3,2},{4,5},{5,4},{6,7},{7,6},{8,9},{9,8},{10,11... | collective-permute-start | bytes 3145736 | tf_op jit(solution)/shard_map/ppermute | solution.py:31
  203.2 4.1 %shard_map.220 = (bf16[512,256]{1,0:T(8,128)(2,1)S(1)}, bf16[512,512]{1,0:T(8,128)(2,1)S(1)}) custom-call(bf16[512,768]{1,0:T(8,128)(2,1)S(1)} %copy-done.3, bf16[512,768]{1,0:T(8,128)(2,1)S(1)} %copy-done.3, f32[512,1]{1,0:T(8,128)S(1)} %copy-done.8, f32[1,512]{1,0:T(1,128)S(1)} %copy-done.29, f32[4,512]{1,0:T(4,128)S(1)} %get-tuple-element.158.refs_4_, ...), custom_call_target="tpu_custom_call" | custom-call | bytes 1024 | tf_op jit(solution)/shard_map/pallas_call | solution.py:154
  207.5 3.1 shard_map.221
  212.4 9.5 %collective-permute-done.28.got_ref = bf16[4,128,1024]{2,1,0:T(8,128)(2,1)} collective-permute-done((bf16[4,128,1024]{2,1,0:T(8,128)(2,1)}, bf16[4,128,1024]{2,1,0:T(8,128)(2,1)}, u32[]{:S(2)}, u32[]{:S(2)}) %collective-permute-start.28) | collective-permute-done | bytes 1048608 | tf_op jit(solution)/shard_map/ppermute | solution.py:31
  230.5 3.1 collective-permute-done.38.refs_2_
  234.4 2.5 collective-permute-start.39
  237.0 3.9 %collective-permute-done.25.got_ref = bf16[4,144,768]{2,1,0:T(8,128)(2,1)S(1)} collective-permute-done((bf16[4,144,768]{2,1,0:T(8,128)(2,1)S(1)}, bf16[4,144,768]{2,1,0:T(8,128)(2,1)S(1)}, u32[]{:S(2)}, u32[]{:S(2)}) %collective-permute-start.25) | collective-permute-done | bytes 884768 | tf_op jit(solution)/shard_map/ppermute | solution.py:31
  240.9 5.6 %collective-permute-done.29.out_got_ref = bf16[4,128,256]{2,1,0:T(8,128)(2,1)S(1)} collective-permute-done((bf16[4,128,256]{2,1,0:T(8,128)(2,1)}, bf16[4,128,256]{2,1,0:T(8,128)(2,1)S(1)}, u32[]{:S(2)}, u32[]{:S(2)}) %collective-permute-start.29) | collective-permute-done | bytes 262176 | tf_op jit(solution)/shard_map/ppermute | solution.py:31
  249.3 5.7 %collective-permute-start.31 = (bf16[144,1024]{1,0:T(8,128)(2,1)S(1)}, bf16[144,1024]{1,0:T(8,128)(2,1)S(1)}, u32[]{:S(2)}, u32[]{:S(2)}) collective-permute-start(bf16[144,1024]{1,0:T(8,128)(2,1)S(1)} %get-tuple-element.198), channel_id=1, source_target_pairs={{0,4},{1,5},{2,6},{3,7},{4,0},{5,1},{6,2},{7,3},{8,12},{9,13},{10,... | collective-permute-start | bytes 884744 | tf_op jit(solution)/shard_map/ppermute | solution.py:31
  255.0 3.2 %shard_map.223 = (f32[256,1024]{1,0:T(8,128)S(1)}, bf16[256,1024]{1,0:T(8,128)(2,1)S(1)}) custom-call(bf16[512,256]{1,0:T(8,128)(2,1)S(1)} %copy-done.48, bf16[512,512]{1,0:T(8,128)(2,1)S(1)} %copy-done.40, bf16[512,256]{1,0:T(8,128)(2,1)S(1)} %copy-done.46, bf16[512,512]{1,0:T(8,128)(2,1)S(1)} %get-tuple-element.166.dkv_ref.dkv_other_ref, ...), custom_call_target="tpu_custom_call" | custom-call | flops 49999998976 | bytes 1024 | tf_op jit(solution)/shard_map/pallas_call | solution.py:49
  259.7 9.4 %collective-permute-done.30.refs_0_ = bf16[144,1024]{1,0:T(8,128)(2,1)S(1)} collective-permute-done((bf16[144,1024]{1,0:T(8,128)(2,1)S(1)}, bf16[144,1024]{1,0:T(8,128)(2,1)S(1)}, u32[]{:S(2)}, u32[]{:S(2)}) %collective-permute-start.30) | collective-permute-done | bytes 294944 | tf_op jit(solution)/shard_map/ppermute | solution.py:31
  269.1 2.6 collective-permute-done.31.refs_1_
  271.8 11.9 %collective-permute-done.32.refs_2_ = bf16[144,1024]{1,0:T(8,128)(2,1)S(1)} collective-permute-done((bf16[144,1024]{1,0:T(8,128)(2,1)S(1)}, bf16[144,1024]{1,0:T(8,128)(2,1)S(1)}, u32[]{:S(2)}, u32[]{:S(2)}) %collective-permute-start.32) | collective-permute-done | bytes 294944 | tf_op jit(solution)/shard_map/ppermute | solution.py:31
  290.3 2.6 collective-permute-done.34.refs_2_
  292.9 7.0 %collective-permute-done.35.refs_3_ = bf16[144,1024]{1,0:T(8,128)(2,1)S(1)} collective-permute-done((bf16[144,1024]{1,0:T(8,128)(2,1)S(1)}, bf16[144,1024]{1,0:T(8,128)(2,1)S(1)}, u32[]{:S(2)}, u32[]{:S(2)}) %collective-permute-start.35) | collective-permute-done | bytes 294944 | tf_op jit(solution)/shard_map/ppermute | solution.py:26
  301.9 2.9 collective-permute-done.36.refs_2_
  (325 shorter events, 120.7 us)
Async XLA Ops:
  7.2 98.4 %all-gather.2.cloned.1.call-start = ((), (), s32[]{:S(2)}) async-start(), calls=%async_computation.2 | async-start | bytes 4718592 | tf_op jit(solution)/shard_map/all_gather | solution.py:613
  9.6 15.6 %collective-permute-start.3 = (bf16[144,1280]{1,0:T(8,128)(2,1)S(1)}, bf16[144,1280]{1,0:T(8,128)(2,1)S(1)}, u32[]{:S(2)}, u32[]{:S(2)}) collective-permute-start(bf16[144,1280]{1,0:T(8,128)(2,1)S(1)} %fusion.3.refs_0_), channel_id=1, source_target_pairs={{0,2},{1,3},{2,0},{3,1},{4,6},{5,7},{6,4},{7,5},{8,10},{9,11},{10,... | collective-permute-start | bytes 1105928 | tf_op jit(solution)/shard_map/ppermute | solution.py:31
  9.7 18.4 %collective-permute-start.5 = (bf16[144,1280]{1,0:T(8,128)(2,1)S(1)}, bf16[144,1280]{1,0:T(8,128)(2,1)S(1)}, u32[]{:S(2)}, u32[]{:S(2)}) collective-permute-start(bf16[144,1280]{1,0:T(8,128)(2,1)S(1)} %fusion.3.refs_0_), channel_id=1, source_target_pairs={{0,4},{1,5},{2,6},{3,7},{4,0},{5,1},{6,2},{7,3},{8,12},{9,13},{10,... | collective-permute-start | bytes 1105928 | tf_op jit(solution)/shard_map/ppermute | solution.py:31
  12.2 46.7 %collective-permute-start.7 = (bf16[144,1280]{1,0:T(8,128)(2,1)S(1)}, bf16[144,1280]{1,0:T(8,128)(2,1)S(1)}, u32[]{:S(2)}, u32[]{:S(2)}) collective-permute-start(bf16[144,1280]{1,0:T(8,128)(2,1)S(1)} %fusion.3.refs_0_), channel_id=1, source_target_pairs={{0,6},{1,7},{2,4},{3,5},{4,2},{5,3},{6,0},{7,1},{8,14},{9,15},{10,... | collective-permute-start | bytes 1105928 | tf_op jit(solution)/shard_map/ppermute | solution.py:31
  12.4 51.7 %collective-permute-start.2 = (bf16[144,1280]{1,0:T(8,128)(2,1)S(1)}, bf16[144,1280]{1,0:T(8,128)(2,1)}, u32[]{:S(2)}, u32[]{:S(2)}) collective-permute-start(bf16[144,1280]{1,0:T(8,128)(2,1)S(1)} %fusion.3.refs_0_), channel_id=1, source_target_pairs={{0,1},{1,0},{2,3},{3,2},{4,5},{5,4},{6,7},{7,6},{8,9},{9,8},{10,11... | collective-permute-start | bytes 1105928 | tf_op jit(solution)/shard_map/ppermute | solution.py:31
  16.4 43.7 %collective-permute-start = (bf16[272,1024]{1,0:T(8,128)(2,1)}, bf16[272,1024]{1,0:T(8,128)(2,1)}, u32[]{:S(2)}, u32[]{:S(2)}) collective-permute-start(bf16[272,1024]{1,0:T(8,128)(2,1)} %pad_maximum_fusion), channel_id=1, source_target_pairs={{0,8},{8,0},{16,24},{24,16},{1,9},{9,1},{17,25},{25,17},{2,10},{10... | collective-permute-start | bytes 1671176 | tf_op jit(solution)/shard_map/ppermute | solution.py:26
  24.5 202.7 %reduce-scatter.5.cloned.1.call-start = ((), (), s32[]{:S(2)}) async-start(), calls=%async_computation.4 | async-start | bytes 1310720 | tf_op jit(solution)/shard_map/reduce_scatter | solution.py:726
  25.3 38.8 %collective-permute-start.4 = (bf16[144,1280]{1,0:T(8,128)(2,1)S(1)}, bf16[144,1280]{1,0:T(8,128)(2,1)S(1)}, u32[]{:S(2)}, u32[]{:S(2)}) collective-permute-start(bf16[144,1280]{1,0:T(8,128)(2,1)S(1)} %collective-permute-done.3.refs_2_), channel_id=1, source_target_pairs={{0,1},{1,0},{2,3},{3,2},{4,5},{5,4},{6,7},{7,6},{8,9},{9,8},{10,11... | collective-permute-start | bytes 1105928 | tf_op jit(solution)/shard_map/ppermute | solution.py:31
  28.1 35.9 %collective-permute-start.6 = (bf16[144,1280]{1,0:T(8,128)(2,1)S(1)}, bf16[144,1280]{1,0:T(8,128)(2,1)S(1)}, u32[]{:S(2)}, u32[]{:S(2)}) collective-permute-start(bf16[144,1280]{1,0:T(8,128)(2,1)S(1)} %collective-permute-done.5.refs_4_), channel_id=1, source_target_pairs={{0,1},{1,0},{2,3},{3,2},{4,5},{5,4},{6,7},{7,6},{8,9},{9,8},{10,11... | collective-permute-start | bytes 1105928 | tf_op jit(solution)/shard_map/ppermute | solution.py:31
  62.7 12.3 %collective-permute-start.1 = (bf16[272,1024]{1,0:T(8,128)(2,1)}, bf16[272,1024]{1,0:T(8,128)(2,1)}, u32[]{:S(2)}, u32[]{:S(2)}) collective-permute-start(bf16[272,1024]{1,0:T(8,128)(2,1)} %fusion.2), channel_id=1, source_target_pairs={{0,16},{8,24},{16,0},{24,8},{1,17},{9,25},{17,1},{25,9},{2,18},{10... | collective-permute-start | bytes 1671176 | tf_op jit(solution)/shard_map/ppermute | solution.py:26
  69.9 12.4 %collective-permute-start.9 = (bf16[1024,768]{1,0:T(8,128)(2,1)}, bf16[1024,768]{1,0:T(8,128)(2,1)}, u32[]{:S(2)}, u32[]{:S(2)}) collective-permute-start(bf16[1024,768]{1,0:T(8,128)(2,1)} %copy-done.32), channel_id=1, source_target_pairs={{0,8},{8,0},{16,24},{24,16},{1,9},{9,1},{17,25},{25,17},{2,10},{10... | collective-permute-start | bytes 4718600 | tf_op jit(solution)/shard_map/ppermute | solution.py:26
  74.8 18.1 %collective-permute-start.11 = (bf16[1024,512]{1,0:T(8,128)(2,1)}, bf16[1024,512]{1,0:T(8,128)(2,1)S(1)}, u32[]{:S(2)}, u32[]{:S(2)}) collective-permute-start(bf16[1024,512]{1,0:T(8,128)(2,1)} %copy-done.38), channel_id=1, source_target_pairs={{0,8},{8,0},{16,24},{24,16},{1,9},{9,1},{17,25},{25,17},{2,10},{10... | collective-permute-start | bytes 3145736 | tf_op jit(solution)/shard_map/ppermute | solution.py:26
  105.6 10.8 %collective-permute-start.13 = (bf16[1024,2048]{1,0:T(8,128)(2,1)}, bf16[1024,2048]{1,0:T(8,128)(2,1)S(1)}, u32[]{:S(2)}, u32[]{:S(2)}) collective-permute-start(bf16[1024,2048]{1,0:T(8,128)(2,1)} %all-gather.2.cloned.1.call-done.refs_0_), channel_id=1, source_target_pairs={{0,8},{8,0},{16,24},{24,16},{1,9},{9,1},{17,25},{25,17},{2,10},{10... | collective-permute-start | bytes 12582920 | tf_op jit(solution)/shard_map/ppermute | solution.py:26
  118.1 13.2 %collective-permute-start.14 = (bf16[256,1024]{1,0:T(8,128)(2,1)S(1)}, bf16[256,1024]{1,0:T(8,128)(2,1)S(1)}, u32[]{:S(2)}, u32[]{:S(2)}) collective-permute-start(bf16[256,1024]{1,0:T(8,128)(2,1)S(1)} %get-tuple-element.128), channel_id=1, source_target_pairs={{0,16},{8,24},{16,0},{24,8},{1,17},{9,25},{17,1},{25,9},{2,18},{10... | collective-permute-start | bytes 1572872 | tf_op jit(solution)/shard_map/ppermute | solution.py:26
  133.0 12.2 %collective-permute-start.16 = (bf16[256,1024]{1,0:T(8,128)(2,1)S(1)}, bf16[256,1024]{1,0:T(8,128)(2,1)S(1)}, u32[]{:S(2)}, u32[]{:S(2)}) collective-permute-start(bf16[256,1024]{1,0:T(8,128)(2,1)S(1)} %get-tuple-element.151.rows_ref.left_ref), channel_id=1, source_target_pairs={{0,16},{8,24},{16,0},{24,8},{1,17},{9,25},{17,1},{25,9},{2,18},{10... | collective-permute-start | bytes 1572872 | tf_op jit(solution)/shard_map/ppermute | solution.py:26
  158.3 13.1 %collective-permute-start.17 = (bf16[256,1024]{1,0:T(8,128)(2,1)S(1)}, bf16[256,1024]{1,0:T(8,128)(2,1)S(1)}, u32[]{:S(2)}, u32[]{:S(2)}) collective-permute-start(bf16[256,1024]{1,0:T(8,128)(2,1)S(1)} %get-tuple-element.149), channel_id=1, source_target_pairs={{0,16},{8,24},{16,0},{24,8},{1,17},{9,25},{17,1},{25,9},{2,18},{10... | collective-permute-start | bytes 1572872 | tf_op jit(solution)/shard_map/ppermute | solution.py:26
  159.6 26.7 %collective-permute-start.21 = (bf16[4,128,1024]{2,1,0:T(8,128)(2,1)S(1)}, bf16[4,128,1024]{2,1,0:T(8,128)(2,1)S(1)}, u32[]{:S(2)}, u32[]{:S(2)}) collective-permute-start(bf16[4,128,1024]{2,1,0:T(8,128)(2,1)S(1)} %get-tuple-element.152), channel_id=1, source_target_pairs={{0,1},{1,0},{2,3},{3,2},{4,5},{5,4},{6,7},{7,6},{8,9},{9,8},{10,11... | collective-permute-start | bytes 3145736 | tf_op jit(solution)/shard_map/ppermute | solution.py:31
  193.7 34.9 %collective-permute-start.15 = (bf16[128,1024]{1,0:T(8,128)(2,1)}, bf16[128,1024]{1,0:T(8,128)(2,1)}, u32[]{:S(2)}, u32[]{:S(2)}) collective-permute-start(bf16[128,1024]{1,0:T(8,128)(2,1)} %copy-done.43), channel_id=1, source_target_pairs={{0,8},{8,0},{16,24},{24,16},{1,9},{9,1},{17,25},{25,17},{2,10},{10... | collective-permute-start | bytes 786440 | tf_op jit(solution)/shard_map/ppermute | solution.py:26
  193.7 13.7 %collective-permute-start.23 = (bf16[8,128,768]{2,1,0:T(8,128)(2,1)S(1)}, bf16[8,128,768]{2,1,0:T(8,128)(2,1)}, u32[]{:S(2)}, u32[]{:S(2)}) collective-permute-start(bf16[8,128,768]{2,1,0:T(8,128)(2,1)S(1)} %shard_map.217), channel_id=1, source_target_pairs={{0,8},{8,0},{16,24},{24,16},{1,9},{9,1},{17,25},{25,17},{2,10},{10... | collective-permute-start | bytes 4718600 | tf_op jit(solution)/shard_map/ppermute | solution.py:26
  194.2 27.7 %collective-permute-start.28 = (bf16[4,128,1024]{2,1,0:T(8,128)(2,1)}, bf16[4,128,1024]{2,1,0:T(8,128)(2,1)}, u32[]{:S(2)}, u32[]{:S(2)}) collective-permute-start(bf16[4,128,1024]{2,1,0:T(8,128)(2,1)} %copy-done.37), channel_id=1, source_target_pairs={{0,1},{1,0},{2,3},{3,2},{4,5},{5,4},{6,7},{7,6},{8,9},{9,8},{10,11... | collective-permute-start | bytes 3145736 | tf_op jit(solution)/shard_map/ppermute | solution.py:31
  198.2 90.9 %reduce-scatter.3.cloned.1.call-start = ((), (), s32[]{:S(2)}) async-start(), calls=%async_computation.3 | async-start | bytes 1310720 | tf_op jit(solution)/shard_map/reduce_scatter | solution.py:726
  201.7 20.2 %collective-permute-start.24 = (bf16[1024,256]{1,0:T(8,128)(2,1)S(1)}, bf16[1024,256]{1,0:T(8,128)(2,1)S(1)}, u32[]{:S(2)}, u32[]{:S(2)}) collective-permute-start(bf16[1024,256]{1,0:T(8,128)(2,1)S(1)} %get-tuple-element.171), channel_id=1, source_target_pairs={{0,16},{8,24},{16,0},{24,8},{1,17},{9,25},{17,1},{25,9},{2,18},{10... | collective-permute-start | bytes 1572872 | tf_op jit(solution)/shard_map/ppermute | solution.py:26
  210.6 30.2 %collective-permute-start.25 = (bf16[4,144,768]{2,1,0:T(8,128)(2,1)S(1)}, bf16[4,144,768]{2,1,0:T(8,128)(2,1)S(1)}, u32[]{:S(2)}, u32[]{:S(2)}) collective-permute-start(bf16[4,144,768]{2,1,0:T(8,128)(2,1)S(1)} %get-tuple-element.182), channel_id=1, source_target_pairs={{0,1},{1,0},{2,3},{3,2},{4,5},{5,4},{6,7},{7,6},{8,9},{9,8},{10,11... | collective-permute-start | bytes 2654216 | tf_op jit(solution)/shard_map/ppermute | solution.py:31
  223.5 23.0 %collective-permute-start.29 = (bf16[4,128,256]{2,1,0:T(8,128)(2,1)}, bf16[4,128,256]{2,1,0:T(8,128)(2,1)S(1)}, u32[]{:S(2)}, u32[]{:S(2)}) collective-permute-start(bf16[4,128,256]{2,1,0:T(8,128)(2,1)} %get-tuple-element.184), channel_id=1, source_target_pairs={{0,1},{1,0},{2,3},{3,2},{4,5},{5,4},{6,7},{7,6},{8,9},{9,8},{10,11... | collective-permute-start | bytes 786440 | tf_op jit(solution)/shard_map/ppermute | solution.py:31
  234.4 51.6 %collective-permute-start.39 = (bf16[256,1024]{1,0:T(8,128)(2,1)}, bf16[256,1024]{1,0:T(8,128)(2,1)}, u32[]{:S(2)}, u32[]{:S(2)}) collective-permute-start(bf16[256,1024]{1,0:T(8,128)(2,1)} %pad_maximum_fusion.6), channel_id=1, source_target_pairs={{0,8},{8,0},{16,24},{24,16},{1,9},{9,1},{17,25},{25,17},{2,10},{10... | collective-permute-start | bytes 1572872 | tf_op jit(solution)/shard_map/ppermute | solution.py:26
  249.2 19.9 %collective-permute-start.30 = (bf16[144,1024]{1,0:T(8,128)(2,1)S(1)}, bf16[144,1024]{1,0:T(8,128)(2,1)S(1)}, u32[]{:S(2)}, u32[]{:S(2)}) collective-permute-start(bf16[144,1024]{1,0:T(8,128)(2,1)S(1)} %get-tuple-element.197), channel_id=1, source_target_pairs={{0,2},{1,3},{2,0},{3,1},{4,6},{5,7},{6,4},{7,5},{8,10},{9,11},{10,... | collective-permute-start | bytes 884744 | tf_op jit(solution)/shard_map/ppermute | solution.py:31
  249.3 22.5 %collective-permute-start.31 = (bf16[144,1024]{1,0:T(8,128)(2,1)S(1)}, bf16[144,1024]{1,0:T(8,128)(2,1)S(1)}, u32[]{:S(2)}, u32[]{:S(2)}) collective-permute-start(bf16[144,1024]{1,0:T(8,128)(2,1)S(1)} %get-tuple-element.198), channel_id=1, source_target_pairs={{0,4},{1,5},{2,6},{3,7},{4,0},{5,1},{6,2},{7,3},{8,12},{9,13},{10,... | collective-permute-start | bytes 884744 | tf_op jit(solution)/shard_map/ppermute | solution.py:31
  255.0 28.7 %collective-permute-start.32 = (bf16[144,1024]{1,0:T(8,128)(2,1)S(1)}, bf16[144,1024]{1,0:T(8,128)(2,1)S(1)}, u32[]{:S(2)}, u32[]{:S(2)}) collective-permute-start(bf16[144,1024]{1,0:T(8,128)(2,1)S(1)} %get-tuple-element.199), channel_id=1, source_target_pairs={{0,6},{1,7},{2,4},{3,5},{4,2},{5,3},{6,0},{7,1},{8,14},{9,15},{10,... | collective-permute-start | bytes 884744 | tf_op jit(solution)/shard_map/ppermute | solution.py:31
  258.3 30.3 %collective-permute-start.26 = (bf16[256,1024]{1,0:T(8,128)(2,1)S(1)}, bf16[256,1024]{1,0:T(8,128)(2,1)S(1)}, u32[]{:S(2)}, u32[]{:S(2)}) collective-permute-start(bf16[256,1024]{1,0:T(8,128)(2,1)S(1)} %get-tuple-element.187), channel_id=1, source_target_pairs={{0,16},{8,24},{16,0},{24,8},{1,17},{9,25},{17,1},{25,9},{2,18},{10... | collective-permute-start | bytes 1572872 | tf_op jit(solution)/shard_map/ppermute | solution.py:26
  285.5 14.3 %collective-permute-start.35 = (bf16[144,1024]{1,0:T(8,128)(2,1)S(1)}, bf16[144,1024]{1,0:T(8,128)(2,1)S(1)}, u32[]{:S(2)}, u32[]{:S(2)}) collective-permute-start(bf16[144,1024]{1,0:T(8,128)(2,1)S(1)} %shard_map.227.refs_0_), channel_id=1, source_target_pairs={{0,24},{8,16},{16,8},{24,0},{1,25},{9,17},{17,9},{25,1},{2,26},{10... | collective-permute-start | bytes 884744 | tf_op jit(solution)/shard_map/ppermute | solution.py:26
  288.9 17.5 %collective-permute-start.27 = (f32[128,1024]{1,0:T(8,128)S(1)}, f32[128,1024]{1,0:T(8,128)S(1)}, u32[]{:S(2)}, u32[]{:S(2)}) collective-permute-start(f32[128,1024]{1,0:T(8,128)S(1)} %get-tuple-element.189), channel_id=1, source_target_pairs={{0,8},{8,0},{16,24},{24,16},{1,9},{9,1},{17,25},{25,17},{2,10},{10... | collective-permute-start | bytes 1572872 | tf_op jit(solution)/shard_map/ppermute | solution.py:26
  289.1 15.7 %collective-permute-start.36 = (bf16[128,1024]{1,0:T(8,128)(2,1)}, bf16[128,1024]{1,0:T(8,128)(2,1)S(1)}, u32[]{:S(2)}, u32[]{:S(2)}) collective-permute-start(bf16[128,1024]{1,0:T(8,128)(2,1)} %reduce-scatter.3.cloned.1.call-done.refs_0_), channel_id=1, source_target_pairs={{0,16},{8,24},{16,0},{24,8},{1,17},{9,25},{17,1},{25,9},{2,18},{10... | collective-permute-start | bytes 786440 | tf_op jit(solution)/shard_map/ppermute | solution.py:26
  (90 other events, 528.4 us)
Sparse Core Ops, SparseCore 0:
  24.7 80.9 all-gather.1
  198.3 27.3 reduce-scatter.4
  230.7 34.6 reduce-scatter.2

commit v2 on v1

--- a/solution.py
+++ b/solution.py
@@ -908,6 +908,9 @@
         scalars=[fsdp // 2],
     )
     mine_block = sends[0]
+    if merged:
+        up_spread = over_ctx(up_total, 2)
+        mine_block = after(mine_block, up_spread)
     total = kernel_call(
         functools.partial(z_sum_kernel, shard),
         [shape((shard + PAD, columns + quarter), bf16)],
@@ -920,29 +923,25 @@
     )
 
     if merged:
-        def quarters(own, direct=False):
-            if direct:
-                return [own] + [over_ctx(own, i) for i in range(1, 4)]
-            far_own = over_ctx(own, 2)
-            other = over_ctx(jnp.concatenate([own, far_own]), 1)
-            return [own, other[: own.shape[0]], far_own, other[own.shape[0] :]]
+        def quarters(own, far_own):
+            return [own, over_ctx(own, 1), far_own, over_ctx(far_own, 1)]
 
         grad_down = kernel_call(
             functools.partial(rows_tail_kernel, shard),
             [shape((shard_ff, width))],
-            quarters(after(down_total, up_mixed)),
+            quarters(down_total, over_ctx(after(down_total, up_mixed), 2)),
             scalars=[ctx],
         )[0]
         grad_up = kernel_call(
             functools.partial(columns_tail_kernel, cut_ff),
             [shape((shard, hidden))],
-            quarters(up_total),
+            quarters(up_total, up_spread),
             scalars=[ctx],
         )[0]
         grad_qkv, grad_out, vec_done = kernel_call(
             functools.partial(tail_kernel, shard, group),
             [shape((shard, 3 * width)), shape((shard, width)), shape((VEC, columns))],
-            quarters(total, direct=True),
+            quarters(total, over_ctx(total, 2)),
             scalars=[ctx],
         )
         counts = [b - a for a, b in zip(starts[:-1], starts[1:])]

time: 320 us -> 310 us (0.969)
  waiting for transfers between devices: 135 us -> 116 us
  starting transfers between devices: 59.2 us -> 65.6 us
    ppermute x14, waiting for transfers between devices: 77.4 us -> 57.1 us  [over_fsdp(): return lax.ppermute(value, 'fsdp', [(i, i ^ mask) for i in range(size)])]
    ppermute x26 -> x28, starting transfers between devices: 35.2 us -> 41.5 us  [over_ctx(): return lax.ppermute(value, 'ctx', [(i, i ^ mask) for i in range(size)])]
    ppermute x26 -> x28, waiting for transfers between devices: 56.1 us -> 57.9 us  [over_ctx(): return lax.ppermute(value, 'ctx', [(i, i ^ mask) for i in range(size)])]
    unnamed x172 -> x182, local copies, waits for them, and re-layouts: 19.8 us -> 20.5 us
  transfers between devices with their start and end apart: 43 -> 45, of which waited for: 22 -> 20; matrix products, arithmetic and copies ran while one was open for 8% -> 7% of each run, Pallas kernels for 14% -> 16%
where the time goes in v2:
time: 310 us; the launch traced here: 306 us
  waiting for transfers between devices  116 us (37%)
  starting transfers between devices  65.6 us (21%)
  Pallas kernels  63.6 us (21%)
  local copies, waits for them, and re-layouts  34.9 us (11%)
  between operations  15.6 us (5%)
  other arithmetic  6.38 us (2%)
  matrix products  3.38 us (1%)
    ppermute x28, waiting for transfers between devices, over_ctx(): return lax.ppermute(value, 'ctx', [(i, i ^ mask) for i in range(size)])  57.9 us
    ppermute x14, waiting for transfers between devices, over_fsdp(): return lax.ppermute(value, 'fsdp', [(i, i ^ mask) for i in range(size)])  57.1 us
    pallas_call x32, Pallas kernels, kernel_call(): pl.pallas_call(body, in_specs=specs, out_specs=[pl.BlockSpec(memory_space...  49.9 us
    ppermute x28, starting transfers between devices, over_ctx(): return lax.ppermute(value, 'ctx', [(i, i ^ mask) for i in range(size)])  41.5 us
    ppermute x14, starting transfers between devices, over_fsdp(): return lax.ppermute(value, 'fsdp', [(i, i ^ mask) for i in range(size)])  23.2 us
    unnamed x182, local copies, waits for them, and re-layouts  20.5 us
    pallas_call x2, Pallas kernels, attend_back(): pl.pallas_call(functools.partial(attend_back_kernel, head_size, 1.0 / mat...  8.34 us
  transfers between devices with their start and end apart: 45, of which 20 were waited for; matrix products, arithmetic and copies ran while one was open for 7% of the time, Pallas kernels for 16%

profile of v2, /device:TPU:9, one launch (start us, length us, event | category | flops | bytes accessed | tf_op | source)
XLA Modules:
  0.0 305.8 jit_solution(3392659284786921432)
XLA Ops:
  9.7 2.5 collective-permute-start.5
  18.2 2.6 reshape.208
  20.8 2.8 dynamic-slice_reduce_fusion
  25.6 2.5 collective-permute-done.5.refs_4_
  29.3 29.6 %collective-permute-done.7.refs_6_ = bf16[144,1280]{1,0:T(8,128)(2,1)S(1)} collective-permute-done((bf16[144,1280]{1,0:T(8,128)(2,1)S(1)}, bf16[144,1280]{1,0:T(8,128)(2,1)S(1)}, u32[]{:S(2)}, u32[]{:S(2)}) %collective-permute-start.7) | collective-permute-done | bytes 368672 | tf_op jit(solution)/shard_map/ppermute | solution.py:31
  69.9 4.9 %collective-permute-start.9 = (bf16[1024,768]{1,0:T(8,128)(2,1)}, bf16[1024,768]{1,0:T(8,128)(2,1)}, u32[]{:S(2)}, u32[]{:S(2)}) collective-permute-start(bf16[1024,768]{1,0:T(8,128)(2,1)} %copy-done.30), channel_id=1, source_target_pairs={{0,8},{8,0},{16,24},{24,16},{1,9},{9,1},{17,25},{25,17},{2,10},{10... | collective-permute-start | bytes 4718600 | tf_op jit(solution)/shard_map/ppermute | solution.py:26
  78.7 2.7 shard_map.196
  84.7 2.7 shard_map.197
  89.0 3.9 %collective-permute-done.10 = bf16[256,512]{1,0:T(8,128)(2,1)S(1)} collective-permute-done((bf16[256,512]{1,0:T(8,128)(2,1)S(1)}, bf16[256,512]{1,0:T(8,128)(2,1)S(1)}, u32[]{:S(2)}, u32[]{:S(2)}) %collective-permute-start.10) | collective-permute-done | bytes 262176 | tf_op jit(solution)/shard_map/ppermute | solution.py:26
  96.4 8.0 %collective-permute-done.12.rows_ref.two_ref = bf16[256,1024]{1,0:T(8,128)(2,1)S(1)} collective-permute-done((bf16[256,1024]{1,0:T(8,128)(2,1)S(1)}, bf16[256,1024]{1,0:T(8,128)(2,1)S(1)}, u32[]{:S(2)}, u32[]{:S(2)}) %collective-permute-start.12) | collective-permute-done | bytes 524320 | tf_op jit(solution)/shard_map/ppermute | solution.py:26
  105.6 3.8 %collective-permute-start.13 = (bf16[1024,2048]{1,0:T(8,128)(2,1)}, bf16[1024,2048]{1,0:T(8,128)(2,1)S(1)}, u32[]{:S(2)}, u32[]{:S(2)}) collective-permute-start(bf16[1024,2048]{1,0:T(8,128)(2,1)} %all-gather.2.cloned.1.call-done.refs_0_), channel_id=1, source_target_pairs={{0,8},{8,0},{16,24},{24,16},{1,9},{9,1},{17,25},{25,17},{2,10},{10... | collective-permute-start | bytes 12582920 | tf_op jit(solution)/shard_map/ppermute | solution.py:26
  121.1 10.2 %collective-permute-done.14.got_ref = bf16[256,1024]{1,0:T(8,128)(2,1)S(1)} collective-permute-done((bf16[256,1024]{1,0:T(8,128)(2,1)S(1)}, bf16[256,1024]{1,0:T(8,128)(2,1)S(1)}, u32[]{:S(2)}, u32[]{:S(2)}) %collective-permute-start.14) | collective-permute-done | bytes 524320 | tf_op jit(solution)/shard_map/ppermute | solution.py:26
  137.6 7.6 %collective-permute-done.16.right_ref.rows_ref = bf16[256,1024]{1,0:T(8,128)(2,1)S(1)} collective-permute-done((bf16[256,1024]{1,0:T(8,128)(2,1)S(1)}, bf16[256,1024]{1,0:T(8,128)(2,1)S(1)}, u32[]{:S(2)}, u32[]{:S(2)}) %collective-permute-start.16) | collective-permute-done | bytes 524320 | tf_op jit(solution)/shard_map/ppermute | solution.py:26
  145.3 2.6 shard_map.206
  159.6 3.9 %collective-permute-start.21 = (bf16[4,128,1024]{2,1,0:T(8,128)(2,1)S(1)}, bf16[4,128,1024]{2,1,0:T(8,128)(2,1)S(1)}, u32[]{:S(2)}, u32[]{:S(2)}) collective-permute-start(bf16[4,128,1024]{2,1,0:T(8,128)(2,1)S(1)} %get-tuple-element.153), channel_id=1, source_target_pairs={{0,1},{1,0},{2,3},{3,2},{4,5},{5,4},{6,7},{7,6},{8,9},{9,8},{10,11... | collective-permute-start | bytes 3145736 | tf_op jit(solution)/shard_map/ppermute | solution.py:31
  166.3 5.1 %collective-permute-done.17.got_ref = bf16[256,1024]{1,0:T(8,128)(2,1)S(1)} collective-permute-done((bf16[256,1024]{1,0:T(8,128)(2,1)S(1)}, bf16[256,1024]{1,0:T(8,128)(2,1)S(1)}, u32[]{:S(2)}, u32[]{:S(2)}) %collective-permute-start.17) | collective-permute-done | bytes 524320 | tf_op jit(solution)/shard_map/ppermute | solution.py:26
  175.9 5.2 %collective-permute-done.20.refs_6_ = bf16[256,512]{1,0:T(8,128)(2,1)S(1)} collective-permute-done((bf16[256,512]{1,0:T(8,128)(2,1)S(1)}, bf16[256,512]{1,0:T(8,128)(2,1)S(1)}, u32[]{:S(2)}, u32[]{:S(2)}) %collective-permute-start.20) | collective-permute-done | bytes 262176 | tf_op jit(solution)/shard_map/ppermute | solution.py:26
  181.1 4.2 %shard_map.215 = (bf16[512,256]{1,0:T(8,128)(2,1)S(1)}, bf16[512,512]{1,0:T(8,128)(2,1)S(1)}) custom-call(bf16[512,768]{1,0:T(8,128)(2,1)S(1)} %copy-done.5, bf16[512,768]{1,0:T(8,128)(2,1)S(1)} %copy-done.5, f32[512,1]{1,0:T(8,128)S(1)} %copy-done.7, f32[1,512]{1,0:T(1,128)S(1)} %copy-done.26, f32[4,512]{1,0:T(4,128)S(1)} %get-tuple-element.161.refs_4_, ...), custom_call_target="tpu_custom_call" | custom-call | bytes 1024 | tf_op jit(solution)/shard_map/pallas_call | solution.py:154
  194.2 4.0 %collective-permute-start.28 = (bf16[4,128,1024]{2,1,0:T(8,128)(2,1)}, bf16[4,128,1024]{2,1,0:T(8,128)(2,1)}, u32[]{:S(2)}, u32[]{:S(2)}) collective-permute-start(bf16[4,128,1024]{2,1,0:T(8,128)(2,1)} %copy-done.35), channel_id=1, source_target_pairs={{0,1},{1,0},{2,3},{3,2},{4,5},{5,4},{6,7},{7,6},{8,9},{9,8},{10,11... | collective-permute-start | bytes 3145736 | tf_op jit(solution)/shard_map/ppermute | solution.py:31
  203.3 4.1 %shard_map.220 = (bf16[512,256]{1,0:T(8,128)(2,1)S(1)}, bf16[512,512]{1,0:T(8,128)(2,1)S(1)}) custom-call(bf16[512,768]{1,0:T(8,128)(2,1)S(1)} %copy-done.3, bf16[512,768]{1,0:T(8,128)(2,1)S(1)} %copy-done.3, f32[512,1]{1,0:T(8,128)S(1)} %copy-done.8, f32[1,512]{1,0:T(1,128)S(1)} %copy-done.27, f32[4,512]{1,0:T(4,128)S(1)} %get-tuple-element.159.refs_4_, ...), custom_call_target="tpu_custom_call" | custom-call | bytes 1024 | tf_op jit(solution)/shard_map/pallas_call | solution.py:154
  207.6 3.1 %shard_map.221 = (f32[4,136,768]{2,1,0:T(8,128)S(1)}, bf16[4,144,768]{2,1,0:T(8,128)(2,1)S(1)}) custom-call(s32[2]{0:T(128)S(1)} %pad_add_fusion.2.place_ref, bf16[512,1024]{1,0:T(8,128)(2,1)S(1)} %copy-done.10, bf16[512,256]{1,0:T(8,128)(2,1)S(1)} %get-tuple-element.186.dq_ref, bf16[512,512]{1,0:T(8,128)(2,1)S(1)} %get-tuple-element.176.dkv_ref, ...), custom_call_target="tpu_custom_call" | custom-call | flops 49999998976 | bytes 1024 | tf_op jit(solution)/shard_map/pallas_call | solution.py:49
  212.5 9.5 %collective-permute-done.28.got_ref = bf16[4,128,1024]{2,1,0:T(8,128)(2,1)} collective-permute-done((bf16[4,128,1024]{2,1,0:T(8,128)(2,1)}, bf16[4,128,1024]{2,1,0:T(8,128)(2,1)}, u32[]{:S(2)}, u32[]{:S(2)}) %collective-permute-start.28) | collective-permute-done | bytes 1048608 | tf_op jit(solution)/shard_map/ppermute | solution.py:31
  224.8 2.4 shard_map.225
  233.8 2.5 collective-permute-start.41
  236.3 4.6 %collective-permute-done.25.got_ref = bf16[4,144,768]{2,1,0:T(8,128)(2,1)S(1)} collective-permute-done((bf16[4,144,768]{2,1,0:T(8,128)(2,1)S(1)}, bf16[4,144,768]{2,1,0:T(8,128)(2,1)S(1)}, u32[]{:S(2)}, u32[]{:S(2)}) %collective-permute-start.25) | collective-permute-done | bytes 884768 | tf_op jit(solution)/shard_map/ppermute | solution.py:31
  240.9 5.6 %collective-permute-done.29.out_got_ref = bf16[4,128,256]{2,1,0:T(8,128)(2,1)S(1)} collective-permute-done((bf16[4,128,256]{2,1,0:T(8,128)(2,1)}, bf16[4,128,256]{2,1,0:T(8,128)(2,1)S(1)}, u32[]{:S(2)}, u32[]{:S(2)}) %collective-permute-start.29) | collective-permute-done | bytes 262176 | tf_op jit(solution)/shard_map/ppermute | solution.py:31
  250.9 5.7 %collective-permute-start.32 = (bf16[144,1024]{1,0:T(8,128)(2,1)}, bf16[144,1024]{1,0:T(8,128)(2,1)}, u32[]{:S(2)}, u32[]{:S(2)}) collective-permute-start(bf16[144,1024]{1,0:T(8,128)(2,1)} %get-tuple-element.200), channel_id=1, source_target_pairs={{0,4},{1,5},{2,6},{3,7},{4,0},{5,1},{6,2},{7,3},{8,12},{9,13},{10,... | collective-permute-start | bytes 884744 | tf_op jit(solution)/shard_map/ppermute | solution.py:31
  256.6 3.3 %shard_map.223 = (f32[256,1024]{1,0:T(8,128)S(1)}, bf16[256,1024]{1,0:T(8,128)(2,1)S(1)}) custom-call(bf16[512,256]{1,0:T(8,128)(2,1)S(1)} %copy-done.49, bf16[512,512]{1,0:T(8,128)(2,1)S(1)} %copy-done.38, bf16[512,256]{1,0:T(8,128)(2,1)S(1)} %copy-done.44, bf16[512,512]{1,0:T(8,128)(2,1)S(1)} %get-tuple-element.167.dkv_ref.dkv_other_ref, ...), custom_call_target="tpu_custom_call" | custom-call | flops 49999998976 | bytes 1024 | tf_op jit(solution)/shard_map/pallas_call | solution.py:49
  264.9 8.4 %collective-permute-done.26.got_ref = bf16[256,1024]{1,0:T(8,128)(2,1)S(1)} collective-permute-done((bf16[256,1024]{1,0:T(8,128)(2,1)S(1)}, bf16[256,1024]{1,0:T(8,128)(2,1)S(1)}, u32[]{:S(2)}, u32[]{:S(2)}) %collective-permute-start.26) | collective-permute-done | bytes 524320 | tf_op jit(solution)/shard_map/ppermute | solution.py:26
  273.5 3.6 %collective-permute-start.27 = (f32[128,1024]{1,0:T(8,128)S(1)}, f32[128,1024]{1,0:T(8,128)S(1)}, u32[]{:S(2)}, u32[]{:S(2)}) collective-permute-start(f32[128,1024]{1,0:T(8,128)S(1)} %get-tuple-element.190), channel_id=1, source_target_pairs={{0,8},{8,0},{16,24},{24,16},{1,9},{9,1},{17,25},{25,17},{2,10},{10... | collective-permute-start | bytes 1572872 | tf_op jit(solution)/shard_map/ppermute | solution.py:26
  280.8 2.9 collective-permute-done.33.refs_2_
  288.3 5.0 %collective-permute-done.35.refs_2_ = bf16[144,1024]{1,0:T(8,128)(2,1)S(1)} collective-permute-done((bf16[144,1024]{1,0:T(8,128)(2,1)S(1)}, bf16[144,1024]{1,0:T(8,128)(2,1)S(1)}, u32[]{:S(2)}, u32[]{:S(2)}) %collective-permute-start.35) | collective-permute-done | bytes 294944 | tf_op jit(solution)/shard_map/ppermute | solution.py:26
  (335 shorter events, 120.7 us)
Async XLA Ops:
  7.2 98.4 %all-gather.2.cloned.1.call-start = ((), (), s32[]{:S(2)}) async-start(), calls=%async_computation.2 | async-start | bytes 4718592 | tf_op jit(solution)/shard_map/all_gather | solution.py:613
  9.6 15.6 %collective-permute-start.3 = (bf16[144,1280]{1,0:T(8,128)(2,1)S(1)}, bf16[144,1280]{1,0:T(8,128)(2,1)S(1)}, u32[]{:S(2)}, u32[]{:S(2)}) collective-permute-start(bf16[144,1280]{1,0:T(8,128)(2,1)S(1)} %fusion.3.refs_0_), channel_id=1, source_target_pairs={{0,2},{1,3},{2,0},{3,1},{4,6},{5,7},{6,4},{7,5},{8,10},{9,11},{10,... | collective-permute-start | bytes 1105928 | tf_op jit(solution)/shard_map/ppermute | solution.py:31
  9.7 18.4 %collective-permute-start.5 = (bf16[144,1280]{1,0:T(8,128)(2,1)S(1)}, bf16[144,1280]{1,0:T(8,128)(2,1)S(1)}, u32[]{:S(2)}, u32[]{:S(2)}) collective-permute-start(bf16[144,1280]{1,0:T(8,128)(2,1)S(1)} %fusion.3.refs_0_), channel_id=1, source_target_pairs={{0,4},{1,5},{2,6},{3,7},{4,0},{5,1},{6,2},{7,3},{8,12},{9,13},{10,... | collective-permute-start | bytes 1105928 | tf_op jit(solution)/shard_map/ppermute | solution.py:31
  12.2 46.7 %collective-permute-start.7 = (bf16[144,1280]{1,0:T(8,128)(2,1)S(1)}, bf16[144,1280]{1,0:T(8,128)(2,1)S(1)}, u32[]{:S(2)}, u32[]{:S(2)}) collective-permute-start(bf16[144,1280]{1,0:T(8,128)(2,1)S(1)} %fusion.3.refs_0_), channel_id=1, source_target_pairs={{0,6},{1,7},{2,4},{3,5},{4,2},{5,3},{6,0},{7,1},{8,14},{9,15},{10,... | collective-permute-start | bytes 1105928 | tf_op jit(solution)/shard_map/ppermute | solution.py:31
  12.4 51.7 %collective-permute-start.2 = (bf16[144,1280]{1,0:T(8,128)(2,1)S(1)}, bf16[144,1280]{1,0:T(8,128)(2,1)}, u32[]{:S(2)}, u32[]{:S(2)}) collective-permute-start(bf16[144,1280]{1,0:T(8,128)(2,1)S(1)} %fusion.3.refs_0_), channel_id=1, source_target_pairs={{0,1},{1,0},{2,3},{3,2},{4,5},{5,4},{6,7},{7,6},{8,9},{9,8},{10,11... | collective-permute-start | bytes 1105928 | tf_op jit(solution)/shard_map/ppermute | solution.py:31
  16.4 43.7 %collective-permute-start = (bf16[272,1024]{1,0:T(8,128)(2,1)}, bf16[272,1024]{1,0:T(8,128)(2,1)}, u32[]{:S(2)}, u32[]{:S(2)}) collective-permute-start(bf16[272,1024]{1,0:T(8,128)(2,1)} %pad_maximum_fusion), channel_id=1, source_target_pairs={{0,8},{8,0},{16,24},{24,16},{1,9},{9,1},{17,25},{25,17},{2,10},{10... | collective-permute-start | bytes 1671176 | tf_op jit(solution)/shard_map/ppermute | solution.py:26
  24.5 202.7 %reduce-scatter.5.cloned.1.call-start = ((), (), s32[]{:S(2)}) async-start(), calls=%async_computation.4 | async-start | bytes 1310720 | tf_op jit(solution)/shard_map/reduce_scatter | solution.py:726
  25.3 38.8 %collective-permute-start.4 = (bf16[144,1280]{1,0:T(8,128)(2,1)S(1)}, bf16[144,1280]{1,0:T(8,128)(2,1)S(1)}, u32[]{:S(2)}, u32[]{:S(2)}) collective-permute-start(bf16[144,1280]{1,0:T(8,128)(2,1)S(1)} %collective-permute-done.3.refs_2_), channel_id=1, source_target_pairs={{0,1},{1,0},{2,3},{3,2},{4,5},{5,4},{6,7},{7,6},{8,9},{9,8},{10,11... | collective-permute-start | bytes 1105928 | tf_op jit(solution)/shard_map/ppermute | solution.py:31
  28.1 35.9 %collective-permute-start.6 = (bf16[144,1280]{1,0:T(8,128)(2,1)S(1)}, bf16[144,1280]{1,0:T(8,128)(2,1)S(1)}, u32[]{:S(2)}, u32[]{:S(2)}) collective-permute-start(bf16[144,1280]{1,0:T(8,128)(2,1)S(1)} %collective-permute-done.5.refs_4_), channel_id=1, source_target_pairs={{0,1},{1,0},{2,3},{3,2},{4,5},{5,4},{6,7},{7,6},{8,9},{9,8},{10,11... | collective-permute-start | bytes 1105928 | tf_op jit(solution)/shard_map/ppermute | solution.py:31
  62.7 12.3 %collective-permute-start.1 = (bf16[272,1024]{1,0:T(8,128)(2,1)}, bf16[272,1024]{1,0:T(8,128)(2,1)}, u32[]{:S(2)}, u32[]{:S(2)}) collective-permute-start(bf16[272,1024]{1,0:T(8,128)(2,1)} %fusion.2), channel_id=1, source_target_pairs={{0,16},{8,24},{16,0},{24,8},{1,17},{9,25},{17,1},{25,9},{2,18},{10... | collective-permute-start | bytes 1671176 | tf_op jit(solution)/shard_map/ppermute | solution.py:26
  69.9 12.4 %collective-permute-start.9 = (bf16[1024,768]{1,0:T(8,128)(2,1)}, bf16[1024,768]{1,0:T(8,128)(2,1)}, u32[]{:S(2)}, u32[]{:S(2)}) collective-permute-start(bf16[1024,768]{1,0:T(8,128)(2,1)} %copy-done.30), channel_id=1, source_target_pairs={{0,8},{8,0},{16,24},{24,16},{1,9},{9,1},{17,25},{25,17},{2,10},{10... | collective-permute-start | bytes 4718600 | tf_op jit(solution)/shard_map/ppermute | solution.py:26
  74.8 18.1 %collective-permute-start.11 = (bf16[1024,512]{1,0:T(8,128)(2,1)}, bf16[1024,512]{1,0:T(8,128)(2,1)S(1)}, u32[]{:S(2)}, u32[]{:S(2)}) collective-permute-start(bf16[1024,512]{1,0:T(8,128)(2,1)} %copy-done.36), channel_id=1, source_target_pairs={{0,8},{8,0},{16,24},{24,16},{1,9},{9,1},{17,25},{25,17},{2,10},{10... | collective-permute-start | bytes 3145736 | tf_op jit(solution)/shard_map/ppermute | solution.py:26
  118.1 13.2 %collective-permute-start.14 = (bf16[256,1024]{1,0:T(8,128)(2,1)S(1)}, bf16[256,1024]{1,0:T(8,128)(2,1)S(1)}, u32[]{:S(2)}, u32[]{:S(2)}) collective-permute-start(bf16[256,1024]{1,0:T(8,128)(2,1)S(1)} %get-tuple-element.129), channel_id=1, source_target_pairs={{0,16},{8,24},{16,0},{24,8},{1,17},{9,25},{17,1},{25,9},{2,18},{10... | collective-permute-start | bytes 1572872 | tf_op jit(solution)/shard_map/ppermute | solution.py:26
  133.0 12.2 %collective-permute-start.16 = (bf16[256,1024]{1,0:T(8,128)(2,1)S(1)}, bf16[256,1024]{1,0:T(8,128)(2,1)S(1)}, u32[]{:S(2)}, u32[]{:S(2)}) collective-permute-start(bf16[256,1024]{1,0:T(8,128)(2,1)S(1)} %get-tuple-element.152.rows_ref.left_ref), channel_id=1, source_target_pairs={{0,16},{8,24},{16,0},{24,8},{1,17},{9,25},{17,1},{25,9},{2,18},{10... | collective-permute-start | bytes 1572872 | tf_op jit(solution)/shard_map/ppermute | solution.py:26
  158.3 13.1 %collective-permute-start.17 = (bf16[256,1024]{1,0:T(8,128)(2,1)S(1)}, bf16[256,1024]{1,0:T(8,128)(2,1)S(1)}, u32[]{:S(2)}, u32[]{:S(2)}) collective-permute-start(bf16[256,1024]{1,0:T(8,128)(2,1)S(1)} %get-tuple-element.150), channel_id=1, source_target_pairs={{0,16},{8,24},{16,0},{24,8},{1,17},{9,25},{17,1},{25,9},{2,18},{10... | collective-permute-start | bytes 1572872 | tf_op jit(solution)/shard_map/ppermute | solution.py:26
  159.6 26.7 %collective-permute-start.21 = (bf16[4,128,1024]{2,1,0:T(8,128)(2,1)S(1)}, bf16[4,128,1024]{2,1,0:T(8,128)(2,1)S(1)}, u32[]{:S(2)}, u32[]{:S(2)}) collective-permute-start(bf16[4,128,1024]{2,1,0:T(8,128)(2,1)S(1)} %get-tuple-element.153), channel_id=1, source_target_pairs={{0,1},{1,0},{2,3},{3,2},{4,5},{5,4},{6,7},{7,6},{8,9},{9,8},{10,11... | collective-permute-start | bytes 3145736 | tf_op jit(solution)/shard_map/ppermute | solution.py:31
  193.7 35.0 %collective-permute-start.15 = (bf16[128,1024]{1,0:T(8,128)(2,1)}, bf16[128,1024]{1,0:T(8,128)(2,1)}, u32[]{:S(2)}, u32[]{:S(2)}) collective-permute-start(bf16[128,1024]{1,0:T(8,128)(2,1)} %copy-done.41), channel_id=1, source_target_pairs={{0,8},{8,0},{16,24},{24,16},{1,9},{9,1},{17,25},{25,17},{2,10},{10... | collective-permute-start | bytes 786440 | tf_op jit(solution)/shard_map/ppermute | solution.py:26
  193.7 13.7 %collective-permute-start.23 = (bf16[8,128,768]{2,1,0:T(8,128)(2,1)S(1)}, bf16[8,128,768]{2,1,0:T(8,128)(2,1)}, u32[]{:S(2)}, u32[]{:S(2)}) collective-permute-start(bf16[8,128,768]{2,1,0:T(8,128)(2,1)S(1)} %shard_map.217), channel_id=1, source_target_pairs={{0,8},{8,0},{16,24},{24,16},{1,9},{9,1},{17,25},{25,17},{2,10},{10... | collective-permute-start | bytes 4718600 | tf_op jit(solution)/shard_map/ppermute | solution.py:26
  194.2 27.7 %collective-permute-start.28 = (bf16[4,128,1024]{2,1,0:T(8,128)(2,1)}, bf16[4,128,1024]{2,1,0:T(8,128)(2,1)}, u32[]{:S(2)}, u32[]{:S(2)}) collective-permute-start(bf16[4,128,1024]{2,1,0:T(8,128)(2,1)} %copy-done.35), channel_id=1, source_target_pairs={{0,1},{1,0},{2,3},{3,2},{4,5},{5,4},{6,7},{7,6},{8,9},{9,8},{10,11... | collective-permute-start | bytes 3145736 | tf_op jit(solution)/shard_map/ppermute | solution.py:31
  198.2 66.4 %reduce-scatter.3.cloned.1.call-start = ((), (), s32[]{:S(2)}) async-start(), calls=%async_computation.3 | async-start | bytes 1310720 | tf_op jit(solution)/shard_map/reduce_scatter | solution.py:726
  201.8 20.2 %collective-permute-start.24 = (bf16[1024,256]{1,0:T(8,128)(2,1)S(1)}, bf16[1024,256]{1,0:T(8,128)(2,1)S(1)}, u32[]{:S(2)}, u32[]{:S(2)}) collective-permute-start(bf16[1024,256]{1,0:T(8,128)(2,1)S(1)} %get-tuple-element.172), channel_id=1, source_target_pairs={{0,16},{8,24},{16,0},{24,8},{1,17},{9,25},{17,1},{25,9},{2,18},{10... | collective-permute-start | bytes 1572872 | tf_op jit(solution)/shard_map/ppermute | solution.py:26
  210.7 30.2 %collective-permute-start.25 = (bf16[4,144,768]{2,1,0:T(8,128)(2,1)S(1)}, bf16[4,144,768]{2,1,0:T(8,128)(2,1)S(1)}, u32[]{:S(2)}, u32[]{:S(2)}) collective-permute-start(bf16[4,144,768]{2,1,0:T(8,128)(2,1)S(1)} %get-tuple-element.183), channel_id=1, source_target_pairs={{0,1},{1,0},{2,3},{3,2},{4,5},{5,4},{6,7},{7,6},{8,9},{9,8},{10,11... | collective-permute-start | bytes 2654216 | tf_op jit(solution)/shard_map/ppermute | solution.py:31
  223.6 23.0 %collective-permute-start.29 = (bf16[4,128,256]{2,1,0:T(8,128)(2,1)}, bf16[4,128,256]{2,1,0:T(8,128)(2,1)S(1)}, u32[]{:S(2)}, u32[]{:S(2)}) collective-permute-start(bf16[4,128,256]{2,1,0:T(8,128)(2,1)} %get-tuple-element.185), channel_id=1, source_target_pairs={{0,1},{1,0},{2,3},{3,2},{4,5},{5,4},{6,7},{7,6},{8,9},{9,8},{10,11... | collective-permute-start | bytes 786440 | tf_op jit(solution)/shard_map/ppermute | solution.py:31
  230.6 30.3 %collective-permute-start.39 = (bf16[128,1024]{1,0:T(8,128)(2,1)S(1)}, bf16[128,1024]{1,0:T(8,128)(2,1)S(1)}, u32[]{:S(2)}, u32[]{:S(2)}) collective-permute-start(bf16[128,1024]{1,0:T(8,128)(2,1)S(1)} %copy-done.45), channel_id=1, source_target_pairs={{0,8},{8,0},{16,24},{24,16},{1,9},{9,1},{17,25},{25,17},{2,10},{10... | collective-permute-start | bytes 786440 | tf_op jit(solution)/shard_map/ppermute | solution.py:26
  233.8 28.4 %collective-permute-start.41 = (bf16[128,1024]{1,0:T(8,128)(2,1)}, bf16[128,1024]{1,0:T(8,128)(2,1)S(1)}, u32[]{:S(2)}, u32[]{:S(2)}) collective-permute-start(bf16[128,1024]{1,0:T(8,128)(2,1)} %collective-permute-done.40.refs_2_), channel_id=1, source_target_pairs={{0,8},{8,0},{16,24},{24,16},{1,9},{9,1},{17,25},{25,17},{2,10},{10... | collective-permute-start | bytes 786440 | tf_op jit(solution)/shard_map/ppermute | solution.py:26
  250.9 29.9 %collective-permute-start.31 = (bf16[144,1024]{1,0:T(8,128)(2,1)}, bf16[144,1024]{1,0:T(8,128)(2,1)}, u32[]{:S(2)}, u32[]{:S(2)}) collective-permute-start(bf16[144,1024]{1,0:T(8,128)(2,1)} %get-tuple-element.199), channel_id=1, source_target_pairs={{0,2},{1,3},{2,0},{3,1},{4,6},{5,7},{6,4},{7,5},{8,10},{9,11},{10,... | collective-permute-start | bytes 884744 | tf_op jit(solution)/shard_map/ppermute | solution.py:31
  250.9 29.9 %collective-permute-start.32 = (bf16[144,1024]{1,0:T(8,128)(2,1)}, bf16[144,1024]{1,0:T(8,128)(2,1)}, u32[]{:S(2)}, u32[]{:S(2)}) collective-permute-start(bf16[144,1024]{1,0:T(8,128)(2,1)} %get-tuple-element.200), channel_id=1, source_target_pairs={{0,4},{1,5},{2,6},{3,7},{4,0},{5,1},{6,2},{7,3},{8,12},{9,13},{10,... | collective-permute-start | bytes 884744 | tf_op jit(solution)/shard_map/ppermute | solution.py:31
  256.6 27.2 %collective-permute-start.33 = (bf16[144,1024]{1,0:T(8,128)(2,1)}, bf16[144,1024]{1,0:T(8,128)(2,1)}, u32[]{:S(2)}, u32[]{:S(2)}) collective-permute-start(bf16[144,1024]{1,0:T(8,128)(2,1)} %get-tuple-element.201), channel_id=1, source_target_pairs={{0,6},{1,7},{2,4},{3,5},{4,2},{5,3},{6,0},{7,1},{8,14},{9,15},{10,... | collective-permute-start | bytes 884744 | tf_op jit(solution)/shard_map/ppermute | solution.py:31
  260.9 12.4 %collective-permute-start.26 = (bf16[256,1024]{1,0:T(8,128)(2,1)S(1)}, bf16[256,1024]{1,0:T(8,128)(2,1)S(1)}, u32[]{:S(2)}, u32[]{:S(2)}) collective-permute-start(bf16[256,1024]{1,0:T(8,128)(2,1)S(1)} %get-tuple-element.188), channel_id=1, source_target_pairs={{0,16},{8,24},{16,0},{24,8},{1,17},{9,25},{17,1},{25,9},{2,18},{10... | collective-permute-start | bytes 1572872 | tf_op jit(solution)/shard_map/ppermute | solution.py:26
  264.6 14.3 %collective-permute-start.30 = (bf16[128,1024]{1,0:T(8,128)(2,1)}, bf16[128,1024]{1,0:T(8,128)(2,1)S(1)}, u32[]{:S(2)}, u32[]{:S(2)}) collective-permute-start(bf16[128,1024]{1,0:T(8,128)(2,1)} %reduce-scatter.3.cloned.1.call-done.refs_0_), channel_id=1, source_target_pairs={{0,16},{8,24},{16,0},{24,8},{1,17},{9,25},{17,1},{25,9},{2,18},{10... | collective-permute-start | bytes 786440 | tf_op jit(solution)/shard_map/ppermute | solution.py:26
  273.5 13.6 %collective-permute-start.27 = (f32[128,1024]{1,0:T(8,128)S(1)}, f32[128,1024]{1,0:T(8,128)S(1)}, u32[]{:S(2)}, u32[]{:S(2)}) collective-permute-start(f32[128,1024]{1,0:T(8,128)S(1)} %get-tuple-element.190), channel_id=1, source_target_pairs={{0,8},{8,0},{16,24},{24,16},{1,9},{9,1},{17,25},{25,17},{2,10},{10... | collective-permute-start | bytes 1572872 | tf_op jit(solution)/shard_map/ppermute | solution.py:26
  278.9 15.6 %collective-permute-start.37 = (bf16[128,1024]{1,0:T(8,128)(2,1)S(1)}, bf16[128,1024]{1,0:T(8,128)(2,1)S(1)}, u32[]{:S(2)}, u32[]{:S(2)}) collective-permute-start(bf16[128,1024]{1,0:T(8,128)(2,1)S(1)} %copy-done.47), channel_id=1, source_target_pairs={{0,8},{8,0},{16,24},{24,16},{1,9},{9,1},{17,25},{25,17},{2,10},{10... | collective-permute-start | bytes 786440 | tf_op jit(solution)/shard_map/ppermute | solution.py:26
  (97 other events, 588.2 us)
Sparse Core Ops, SparseCore 0:
  24.7 80.9 all-gather.1
  198.3 27.3 reduce-scatter.4
  230.7 28.1 reduce-scatter.2

commit v3 on v2

--- a/solution.py
+++ b/solution.py
@@ -39,7 +39,7 @@
     return jax.ShapeDtypeStruct(tuple(dims), dtype)
 
 
-def kernel_call(body, outs, args, scalars=(), scratch=(), flops=50_000_000_000):
+def kernel_call(body, outs, args, scalars=(), scratch=(), flops=30_000_000_000):
     scalars = [jnp.asarray(s, jnp.int32).reshape(-1) for s in scalars]
     specs = [pl.BlockSpec(memory_space=pltpu.SMEM)] * len(scalars)
     specs += [pl.BlockSpec(memory_space=pltpu.VMEM)] * len(args)
@@ -708,7 +708,7 @@
     )
     d_feed_rest = gather_tokens(d_feed_own)
 
-    def gradient(args, flops=50_000_000_000):
+    def gradient(args, flops=30_000_000_000):
         return kernel_call(grad_kernel, [shape((width, width), bf16)], args, flops=flops)[0]
 
     def split(kept, got):
@@ -898,8 +898,6 @@
         [shape((own_rows, width)), shape((rest_rows, width), bf16)],
         [after(d_projected[0][0], out_far, got), d_projected[0][1], *d_projected[1], *w_qkv_pair],
     )
-    if merged:
-        got = after(got, up_mixed)
     sends = kernel_call(
         functools.partial(z_send_kernel, shard),
         [shape((shard + VEC, columns + quarter))]

time: 310 us -> 307 us (level)
  Pallas kernels: 63.6 us -> 59.2 us
    pallas_call x32, Pallas kernels: 49.9 us -> 45.4 us  [kernel_call(): pl.pallas_call(body, in_specs=specs, out_specs=[pl.BlockSpec(memory_space...]
    unnamed x182 -> x150, local copies, waits for them, and re-layouts: 20.5 us -> 19.6 us
  transfers between devices with their start and end apart: 45 -> 45, of which waited for: 20 -> 19; matrix products, arithmetic and copies ran while one was open for 7% -> 7% of each run, Pallas kernels for 16% -> 15%
where the time goes in v3:
time: 307 us; the launch traced here: 303 us
  waiting for transfers between devices  117 us (38%)
  starting transfers between devices  66.6 us (22%)
  Pallas kernels  59.2 us (19%)
  local copies, waits for them, and re-layouts  34 us (11%)
  between operations  15.5 us (5%)
  other arithmetic  7.33 us (2%)
  matrix products  3.38 us (1%)
    ppermute x14, waiting for transfers between devices, over_fsdp(): return lax.ppermute(value, 'fsdp', [(i, i ^ mask) for i in range(size)])  59.4 us
    ppermute x28, waiting for transfers between devices, over_ctx(): return lax.ppermute(value, 'ctx', [(i, i ^ mask) for i in range(size)])  56.9 us
    pallas_call x32, Pallas kernels, kernel_call(): pl.pallas_call(body, in_specs=specs, out_specs=[pl.BlockSpec(memory_space...  45.4 us
    ppermute x28, starting transfers between devices, over_ctx(): return lax.ppermute(value, 'ctx', [(i, i ^ mask) for i in range(size)])  42.8 us
    ppermute x14, starting transfers between devices, over_fsdp(): return lax.ppermute(value, 'fsdp', [(i, i ^ mask) for i in range(size)])  22.9 us
    unnamed x150, local copies, waits for them, and re-layouts  19.6 us
    pallas_call x2, Pallas kernels, attend_back(): pl.pallas_call(functools.partial(attend_back_kernel, head_size, 1.0 / mat...  8.32 us
  transfers between devices with their start and end apart: 45, of which 19 were waited for; matrix products, arithmetic and copies ran while one was open for 7% of the time, Pallas kernels for 15%

profile of v3, /device:TPU:9, one launch (start us, length us, event | category | flops | bytes accessed | tf_op | source)
XLA Modules:
  0.0 302.8 jit_solution(10297310146118244330)
XLA Ops:
  9.7 2.5 collective-permute-start.5
  18.2 2.6 reshape.208
  20.8 2.8 dynamic-slice_reduce_fusion
  25.6 2.5 collective-permute-done.5.refs_4_
  29.3 29.6 %collective-permute-done.7.refs_6_ = bf16[144,1280]{1,0:T(8,128)(2,1)S(1)} collective-permute-done((bf16[144,1280]{1,0:T(8,128)(2,1)S(1)}, bf16[144,1280]{1,0:T(8,128)(2,1)S(1)}, u32[]{:S(2)}, u32[]{:S(2)}) %collective-permute-start.7) | collective-permute-done | bytes 368672 | tf_op jit(solution)/shard_map/ppermute | solution.py:31
  69.9 4.9 %collective-permute-start.9 = (bf16[1024,768]{1,0:T(8,128)(2,1)}, bf16[1024,768]{1,0:T(8,128)(2,1)}, u32[]{:S(2)}, u32[]{:S(2)}) collective-permute-start(bf16[1024,768]{1,0:T(8,128)(2,1)} %copy-done.23), channel_id=1, source_target_pairs={{0,8},{8,0},{16,24},{24,16},{1,9},{9,1},{17,25},{25,17},{2,10},{10... | collective-permute-start | bytes 4718600 | tf_op jit(solution)/shard_map/ppermute | solution.py:26
  79.4 2.7 shard_map.196
  83.1 2.4 add_convert_fusion.1.block_ref.whole_ref.refs_0_.refs_1_
  85.5 2.7 shard_map.197
  89.8 3.8 %collective-permute-done.10 = bf16[256,512]{1,0:T(8,128)(2,1)S(1)} collective-permute-done((bf16[256,512]{1,0:T(8,128)(2,1)S(1)}, bf16[256,512]{1,0:T(8,128)(2,1)S(1)}, u32[]{:S(2)}, u32[]{:S(2)}) %collective-permute-start.10) | collective-permute-done | bytes 262176 | tf_op jit(solution)/shard_map/ppermute | solution.py:26
  97.2 8.0 %collective-permute-done.12.rows_ref.two_ref = bf16[256,1024]{1,0:T(8,128)(2,1)S(1)} collective-permute-done((bf16[256,1024]{1,0:T(8,128)(2,1)S(1)}, bf16[256,1024]{1,0:T(8,128)(2,1)S(1)}, u32[]{:S(2)}, u32[]{:S(2)}) %collective-permute-start.12) | collective-permute-done | bytes 524320 | tf_op jit(solution)/shard_map/ppermute | solution.py:26
  105.6 4.6 %collective-permute-start.13 = (bf16[1024,2048]{1,0:T(8,128)(2,1)}, bf16[1024,2048]{1,0:T(8,128)(2,1)S(1)}, u32[]{:S(2)}, u32[]{:S(2)}) collective-permute-start(bf16[1024,2048]{1,0:T(8,128)(2,1)} %all-gather.2.cloned.1.call-done.refs_0_), channel_id=1, source_target_pairs={{0,8},{8,0},{16,24},{24,16},{1,9},{9,1},{17,25},{25,17},{2,10},{10... | collective-permute-start | bytes 12582920 | tf_op jit(solution)/shard_map/ppermute | solution.py:26
  121.9 10.2 %collective-permute-done.14.got_ref = bf16[256,1024]{1,0:T(8,128)(2,1)S(1)} collective-permute-done((bf16[256,1024]{1,0:T(8,128)(2,1)S(1)}, bf16[256,1024]{1,0:T(8,128)(2,1)S(1)}, u32[]{:S(2)}, u32[]{:S(2)}) %collective-permute-start.14) | collective-permute-done | bytes 524320 | tf_op jit(solution)/shard_map/ppermute | solution.py:26
  138.2 8.2 %collective-permute-done.16.right_ref.rows_ref = bf16[256,1024]{1,0:T(8,128)(2,1)S(1)} collective-permute-done((bf16[256,1024]{1,0:T(8,128)(2,1)S(1)}, bf16[256,1024]{1,0:T(8,128)(2,1)S(1)}, u32[]{:S(2)}, u32[]{:S(2)}) %collective-permute-start.16) | collective-permute-done | bytes 524320 | tf_op jit(solution)/shard_map/ppermute | solution.py:26
  158.0 3.9 %collective-permute-start.21 = (bf16[4,128,1024]{2,1,0:T(8,128)(2,1)S(1)}, bf16[4,128,1024]{2,1,0:T(8,128)(2,1)S(1)}, u32[]{:S(2)}, u32[]{:S(2)}) collective-permute-start(bf16[4,128,1024]{2,1,0:T(8,128)(2,1)S(1)} %get-tuple-element.152), channel_id=1, source_target_pairs={{0,1},{1,0},{2,3},{3,2},{4,5},{5,4},{6,7},{7,6},{8,9},{9,8},{10,11... | collective-permute-start | bytes 3145736 | tf_op jit(solution)/shard_map/ppermute | solution.py:31
  164.7 5.0 %collective-permute-done.17.got_ref = bf16[256,1024]{1,0:T(8,128)(2,1)S(1)} collective-permute-done((bf16[256,1024]{1,0:T(8,128)(2,1)S(1)}, bf16[256,1024]{1,0:T(8,128)(2,1)S(1)}, u32[]{:S(2)}, u32[]{:S(2)}) %collective-permute-start.17) | collective-permute-done | bytes 524320 | tf_op jit(solution)/shard_map/ppermute | solution.py:26
  173.7 5.1 %collective-permute-done.20.refs_6_ = bf16[256,512]{1,0:T(8,128)(2,1)S(1)} collective-permute-done((bf16[256,512]{1,0:T(8,128)(2,1)S(1)}, bf16[256,512]{1,0:T(8,128)(2,1)S(1)}, u32[]{:S(2)}, u32[]{:S(2)}) %collective-permute-start.20) | collective-permute-done | bytes 262176 | tf_op jit(solution)/shard_map/ppermute | solution.py:26
  178.8 4.2 %shard_map.215 = (bf16[512,256]{1,0:T(8,128)(2,1)S(1)}, bf16[512,512]{1,0:T(8,128)(2,1)S(1)}) custom-call(bf16[512,768]{1,0:T(8,128)(2,1)S(1)} %copy-done.5, bf16[512,768]{1,0:T(8,128)(2,1)S(1)} %copy-done.5, f32[512,1]{1,0:T(8,128)S(1)} %copy-done.7, f32[1,512]{1,0:T(1,128)S(1)} %copy-done.20, f32[4,512]{1,0:T(4,128)S(1)} %get-tuple-element.160.refs_4_, ...), custom_call_target="tpu_custom_call" | custom-call | bytes 1024 | tf_op jit(solution)/shard_map/pallas_call | solution.py:154
  193.7 3.5 %collective-permute-start.29 = (bf16[4,128,1024]{2,1,0:T(8,128)(2,1)}, bf16[4,128,1024]{2,1,0:T(8,128)(2,1)}, u32[]{:S(2)}, u32[]{:S(2)}) collective-permute-start(bf16[4,128,1024]{2,1,0:T(8,128)(2,1)} %copy-done.29), channel_id=1, source_target_pairs={{0,1},{1,0},{2,3},{3,2},{4,5},{5,4},{6,7},{7,6},{8,9},{9,8},{10,11... | collective-permute-start | bytes 3145736 | tf_op jit(solution)/shard_map/ppermute | solution.py:31
  202.2 4.1 %shard_map.220 = (bf16[512,256]{1,0:T(8,128)(2,1)S(1)}, bf16[512,512]{1,0:T(8,128)(2,1)S(1)}) custom-call(bf16[512,768]{1,0:T(8,128)(2,1)S(1)} %copy-done.3, bf16[512,768]{1,0:T(8,128)(2,1)S(1)} %copy-done.3, f32[512,1]{1,0:T(8,128)S(1)} %copy-done.7, f32[1,512]{1,0:T(1,128)S(1)} %copy-done.20, f32[4,512]{1,0:T(4,128)S(1)} %get-tuple-element.158.refs_4_, ...), custom_call_target="tpu_custom_call" | custom-call | bytes 1024 | tf_op jit(solution)/shard_map/pallas_call | solution.py:154
  206.4 3.1 %shard_map.221 = (f32[4,136,768]{2,1,0:T(8,128)S(1)}, bf16[4,144,768]{2,1,0:T(8,128)(2,1)S(1)}) custom-call(s32[2]{0:T(128)S(1)} %pad_add_fusion.2.place_ref, bf16[512,1024]{1,0:T(8,128)(2,1)S(1)} %copy-done.9, bf16[512,256]{1,0:T(8,128)(2,1)S(1)} %get-tuple-element.185.dq_ref, bf16[512,512]{1,0:T(8,128)(2,1)S(1)} %get-tuple-element.175.dkv_ref, ...), custom_call_target="tpu_custom_call" | custom-call | flops 30000001024 | bytes 1024 | tf_op jit(solution)/shard_map/pallas_call | solution.py:49
  211.4 9.6 %collective-permute-done.29.got_ref = bf16[4,128,1024]{2,1,0:T(8,128)(2,1)} collective-permute-done((bf16[4,128,1024]{2,1,0:T(8,128)(2,1)}, bf16[4,128,1024]{2,1,0:T(8,128)(2,1)}, u32[]{:S(2)}, u32[]{:S(2)}) %collective-permute-start.29) | collective-permute-done | bytes 1048608 | tf_op jit(solution)/shard_map/ppermute | solution.py:31
  222.4 2.4 shard_map.226
  231.4 2.5 collective-permute-start.41
  233.9 11.7 %collective-permute-done.28.out_got_ref = bf16[4,128,256]{2,1,0:T(8,128)(2,1)S(1)} collective-permute-done((bf16[4,128,256]{2,1,0:T(8,128)(2,1)S(1)}, bf16[4,128,256]{2,1,0:T(8,128)(2,1)S(1)}, u32[]{:S(2)}, u32[]{:S(2)}) %collective-permute-start.28) | collective-permute-done | bytes 262176 | tf_op jit(solution)/shard_map/ppermute | solution.py:31
  248.8 5.8 %collective-permute-start.32 = (bf16[144,1024]{1,0:T(8,128)(2,1)}, bf16[144,1024]{1,0:T(8,128)(2,1)S(1)}, u32[]{:S(2)}, u32[]{:S(2)}) collective-permute-start(bf16[144,1024]{1,0:T(8,128)(2,1)} %get-tuple-element.198), channel_id=1, source_target_pairs={{0,4},{1,5},{2,6},{3,7},{4,0},{5,1},{6,2},{7,3},{8,12},{9,13},{10,... | collective-permute-start | bytes 884744 | tf_op jit(solution)/shard_map/ppermute | solution.py:31
  254.7 3.3 %shard_map.223 = (f32[256,1024]{1,0:T(8,128)S(1)}, bf16[256,1024]{1,0:T(8,128)(2,1)S(1)}) custom-call(bf16[512,256]{1,0:T(8,128)(2,1)S(1)} %copy-done.43, bf16[512,512]{1,0:T(8,128)(2,1)S(1)} %copy-done.34, bf16[512,256]{1,0:T(8,128)(2,1)S(1)} %copy-done.38, bf16[512,512]{1,0:T(8,128)(2,1)S(1)} %copy-done.32, bf16[1024,768]{1,0:T(8,128)(2,1)S(1)} %copy-done.25, ...), custom_call_target="tpu_custom_call" | custom-call | flops 30000001024 | bytes 1024 | tf_op jit(solution)/shard_map/pallas_call | solution.py:49
  260.3 2.4 shard_map.230
  262.9 8.3 %collective-permute-done.26.got_ref = bf16[256,1024]{1,0:T(8,128)(2,1)S(1)} collective-permute-done((bf16[256,1024]{1,0:T(8,128)(2,1)S(1)}, bf16[256,1024]{1,0:T(8,128)(2,1)S(1)}, u32[]{:S(2)}, u32[]{:S(2)}) %collective-permute-start.26) | collective-permute-done | bytes 524320 | tf_op jit(solution)/shard_map/ppermute | solution.py:26
  272.6 3.7 %collective-permute-start.27 = (f32[128,1024]{1,0:T(8,128)S(1)}, f32[128,1024]{1,0:T(8,128)S(1)}, u32[]{:S(2)}, u32[]{:S(2)}) collective-permute-start(f32[128,1024]{1,0:T(8,128)S(1)} %get-tuple-element.189), channel_id=1, source_target_pairs={{0,8},{8,0},{16,24},{24,16},{1,9},{9,1},{17,25},{25,17},{2,10},{10... | collective-permute-start | bytes 1572872 | tf_op jit(solution)/shard_map/ppermute | solution.py:26
  278.9 3.0 collective-permute-done.33.refs_2_
  285.2 5.1 %collective-permute-done.35.refs_2_ = bf16[144,1024]{1,0:T(8,128)(2,1)S(1)} collective-permute-done((bf16[144,1024]{1,0:T(8,128)(2,1)S(1)}, bf16[144,1024]{1,0:T(8,128)(2,1)S(1)}, u32[]{:S(2)}, u32[]{:S(2)}) %collective-permute-start.35) | collective-permute-done | bytes 294944 | tf_op jit(solution)/shard_map/ppermute | solution.py:26
  (303 shorter events, 113.1 us)
Async XLA Ops:
  7.2 98.4 %all-gather.2.cloned.1.call-start = ((), (), s32[]{:S(2)}) async-start(), calls=%async_computation.2 | async-start | bytes 4718592 | tf_op jit(solution)/shard_map/all_gather | solution.py:613
  9.6 15.6 %collective-permute-start.3 = (bf16[144,1280]{1,0:T(8,128)(2,1)S(1)}, bf16[144,1280]{1,0:T(8,128)(2,1)S(1)}, u32[]{:S(2)}, u32[]{:S(2)}) collective-permute-start(bf16[144,1280]{1,0:T(8,128)(2,1)S(1)} %fusion.3.refs_0_), channel_id=1, source_target_pairs={{0,2},{1,3},{2,0},{3,1},{4,6},{5,7},{6,4},{7,5},{8,10},{9,11},{10,... | collective-permute-start | bytes 1105928 | tf_op jit(solution)/shard_map/ppermute | solution.py:31
  9.7 18.4 %collective-permute-start.5 = (bf16[144,1280]{1,0:T(8,128)(2,1)S(1)}, bf16[144,1280]{1,0:T(8,128)(2,1)S(1)}, u32[]{:S(2)}, u32[]{:S(2)}) collective-permute-start(bf16[144,1280]{1,0:T(8,128)(2,1)S(1)} %fusion.3.refs_0_), channel_id=1, source_target_pairs={{0,4},{1,5},{2,6},{3,7},{4,0},{5,1},{6,2},{7,3},{8,12},{9,13},{10,... | collective-permute-start | bytes 1105928 | tf_op jit(solution)/shard_map/ppermute | solution.py:31
  12.2 46.7 %collective-permute-start.7 = (bf16[144,1280]{1,0:T(8,128)(2,1)S(1)}, bf16[144,1280]{1,0:T(8,128)(2,1)S(1)}, u32[]{:S(2)}, u32[]{:S(2)}) collective-permute-start(bf16[144,1280]{1,0:T(8,128)(2,1)S(1)} %fusion.3.refs_0_), channel_id=1, source_target_pairs={{0,6},{1,7},{2,4},{3,5},{4,2},{5,3},{6,0},{7,1},{8,14},{9,15},{10,... | collective-permute-start | bytes 1105928 | tf_op jit(solution)/shard_map/ppermute | solution.py:31
  12.4 51.7 %collective-permute-start.2 = (bf16[144,1280]{1,0:T(8,128)(2,1)S(1)}, bf16[144,1280]{1,0:T(8,128)(2,1)}, u32[]{:S(2)}, u32[]{:S(2)}) collective-permute-start(bf16[144,1280]{1,0:T(8,128)(2,1)S(1)} %fusion.3.refs_0_), channel_id=1, source_target_pairs={{0,1},{1,0},{2,3},{3,2},{4,5},{5,4},{6,7},{7,6},{8,9},{9,8},{10,11... | collective-permute-start | bytes 1105928 | tf_op jit(solution)/shard_map/ppermute | solution.py:31
  16.4 43.7 %collective-permute-start = (bf16[272,1024]{1,0:T(8,128)(2,1)}, bf16[272,1024]{1,0:T(8,128)(2,1)}, u32[]{:S(2)}, u32[]{:S(2)}) collective-permute-start(bf16[272,1024]{1,0:T(8,128)(2,1)} %pad_maximum_fusion), channel_id=1, source_target_pairs={{0,8},{8,0},{16,24},{24,16},{1,9},{9,1},{17,25},{25,17},{2,10},{10... | collective-permute-start | bytes 1671176 | tf_op jit(solution)/shard_map/ppermute | solution.py:26
  24.5 200.3 %reduce-scatter.5.cloned.1.call-start = ((), (), s32[]{:S(2)}) async-start(), calls=%async_computation.4 | async-start | bytes 1310720 | tf_op jit(solution)/shard_map/reduce_scatter | solution.py:726
  25.3 38.8 %collective-permute-start.4 = (bf16[144,1280]{1,0:T(8,128)(2,1)S(1)}, bf16[144,1280]{1,0:T(8,128)(2,1)S(1)}, u32[]{:S(2)}, u32[]{:S(2)}) collective-permute-start(bf16[144,1280]{1,0:T(8,128)(2,1)S(1)} %collective-permute-done.3.refs_2_), channel_id=1, source_target_pairs={{0,1},{1,0},{2,3},{3,2},{4,5},{5,4},{6,7},{7,6},{8,9},{9,8},{10,11... | collective-permute-start | bytes 1105928 | tf_op jit(solution)/shard_map/ppermute | solution.py:31
  28.1 35.9 %collective-permute-start.6 = (bf16[144,1280]{1,0:T(8,128)(2,1)S(1)}, bf16[144,1280]{1,0:T(8,128)(2,1)S(1)}, u32[]{:S(2)}, u32[]{:S(2)}) collective-permute-start(bf16[144,1280]{1,0:T(8,128)(2,1)S(1)} %collective-permute-done.5.refs_4_), channel_id=1, source_target_pairs={{0,1},{1,0},{2,3},{3,2},{4,5},{5,4},{6,7},{7,6},{8,9},{9,8},{10,11... | collective-permute-start | bytes 1105928 | tf_op jit(solution)/shard_map/ppermute | solution.py:31
  62.7 12.3 %collective-permute-start.1 = (bf16[272,1024]{1,0:T(8,128)(2,1)}, bf16[272,1024]{1,0:T(8,128)(2,1)}, u32[]{:S(2)}, u32[]{:S(2)}) collective-permute-start(bf16[272,1024]{1,0:T(8,128)(2,1)} %fusion.2), channel_id=1, source_target_pairs={{0,16},{8,24},{16,0},{24,8},{1,17},{9,25},{17,1},{25,9},{2,18},{10... | collective-permute-start | bytes 1671176 | tf_op jit(solution)/shard_map/ppermute | solution.py:26
  69.9 13.2 %collective-permute-start.9 = (bf16[1024,768]{1,0:T(8,128)(2,1)}, bf16[1024,768]{1,0:T(8,128)(2,1)}, u32[]{:S(2)}, u32[]{:S(2)}) collective-permute-start(bf16[1024,768]{1,0:T(8,128)(2,1)} %copy-done.23), channel_id=1, source_target_pairs={{0,8},{8,0},{16,24},{24,16},{1,9},{9,1},{17,25},{25,17},{2,10},{10... | collective-permute-start | bytes 4718600 | tf_op jit(solution)/shard_map/ppermute | solution.py:26
  74.8 18.9 %collective-permute-start.11 = (bf16[1024,512]{1,0:T(8,128)(2,1)}, bf16[1024,512]{1,0:T(8,128)(2,1)S(1)}, u32[]{:S(2)}, u32[]{:S(2)}) collective-permute-start(bf16[1024,512]{1,0:T(8,128)(2,1)} %copy-done.30), channel_id=1, source_target_pairs={{0,8},{8,0},{16,24},{24,16},{1,9},{9,1},{17,25},{25,17},{2,10},{10... | collective-permute-start | bytes 3145736 | tf_op jit(solution)/shard_map/ppermute | solution.py:26
  105.6 11.5 %collective-permute-start.13 = (bf16[1024,2048]{1,0:T(8,128)(2,1)}, bf16[1024,2048]{1,0:T(8,128)(2,1)S(1)}, u32[]{:S(2)}, u32[]{:S(2)}) collective-permute-start(bf16[1024,2048]{1,0:T(8,128)(2,1)} %all-gather.2.cloned.1.call-done.refs_0_), channel_id=1, source_target_pairs={{0,8},{8,0},{16,24},{24,16},{1,9},{9,1},{17,25},{25,17},{2,10},{10... | collective-permute-start | bytes 12582920 | tf_op jit(solution)/shard_map/ppermute | solution.py:26
  118.8 13.2 %collective-permute-start.14 = (bf16[256,1024]{1,0:T(8,128)(2,1)S(1)}, bf16[256,1024]{1,0:T(8,128)(2,1)S(1)}, u32[]{:S(2)}, u32[]{:S(2)}) collective-permute-start(bf16[256,1024]{1,0:T(8,128)(2,1)S(1)} %get-tuple-element.128), channel_id=1, source_target_pairs={{0,16},{8,24},{16,0},{24,8},{1,17},{9,25},{17,1},{25,9},{2,18},{10... | collective-permute-start | bytes 1572872 | tf_op jit(solution)/shard_map/ppermute | solution.py:26
  134.2 12.2 %collective-permute-start.16 = (bf16[256,1024]{1,0:T(8,128)(2,1)S(1)}, bf16[256,1024]{1,0:T(8,128)(2,1)S(1)}, u32[]{:S(2)}, u32[]{:S(2)}) collective-permute-start(bf16[256,1024]{1,0:T(8,128)(2,1)S(1)} %get-tuple-element.151.rows_ref.left_ref), channel_id=1, source_target_pairs={{0,16},{8,24},{16,0},{24,8},{1,17},{9,25},{17,1},{25,9},{2,18},{10... | collective-permute-start | bytes 1572872 | tf_op jit(solution)/shard_map/ppermute | solution.py:26
  156.6 13.1 %collective-permute-start.17 = (bf16[256,1024]{1,0:T(8,128)(2,1)S(1)}, bf16[256,1024]{1,0:T(8,128)(2,1)S(1)}, u32[]{:S(2)}, u32[]{:S(2)}) collective-permute-start(bf16[256,1024]{1,0:T(8,128)(2,1)S(1)} %get-tuple-element.149), channel_id=1, source_target_pairs={{0,16},{8,24},{16,0},{24,8},{1,17},{9,25},{17,1},{25,9},{2,18},{10... | collective-permute-start | bytes 1572872 | tf_op jit(solution)/shard_map/ppermute | solution.py:26
  158.0 26.7 %collective-permute-start.21 = (bf16[4,128,1024]{2,1,0:T(8,128)(2,1)S(1)}, bf16[4,128,1024]{2,1,0:T(8,128)(2,1)S(1)}, u32[]{:S(2)}, u32[]{:S(2)}) collective-permute-start(bf16[4,128,1024]{2,1,0:T(8,128)(2,1)S(1)} %get-tuple-element.152), channel_id=1, source_target_pairs={{0,1},{1,0},{2,3},{3,2},{4,5},{5,4},{6,7},{7,6},{8,9},{9,8},{10,11... | collective-permute-start | bytes 3145736 | tf_op jit(solution)/shard_map/ppermute | solution.py:31
  193.2 33.1 %collective-permute-start.15 = (bf16[128,1024]{1,0:T(8,128)(2,1)}, bf16[128,1024]{1,0:T(8,128)(2,1)}, u32[]{:S(2)}, u32[]{:S(2)}) collective-permute-start(bf16[128,1024]{1,0:T(8,128)(2,1)} %get-tuple-element.130), channel_id=1, source_target_pairs={{0,8},{8,0},{16,24},{24,16},{1,9},{9,1},{17,25},{25,17},{2,10},{10... | collective-permute-start | bytes 786440 | tf_op jit(solution)/shard_map/ppermute | solution.py:26
  193.2 13.2 %collective-permute-start.23 = (bf16[8,128,768]{2,1,0:T(8,128)(2,1)}, bf16[8,128,768]{2,1,0:T(8,128)(2,1)}, u32[]{:S(2)}, u32[]{:S(2)}) collective-permute-start(bf16[8,128,768]{2,1,0:T(8,128)(2,1)} %copy-done.26), channel_id=1, source_target_pairs={{0,8},{8,0},{16,24},{24,16},{1,9},{9,1},{17,25},{25,17},{2,10},{10... | collective-permute-start | bytes 4718600 | tf_op jit(solution)/shard_map/ppermute | solution.py:26
  193.7 27.3 %collective-permute-start.29 = (bf16[4,128,1024]{2,1,0:T(8,128)(2,1)}, bf16[4,128,1024]{2,1,0:T(8,128)(2,1)}, u32[]{:S(2)}, u32[]{:S(2)}) collective-permute-start(bf16[4,128,1024]{2,1,0:T(8,128)(2,1)} %copy-done.29), channel_id=1, source_target_pairs={{0,1},{1,0},{2,3},{3,2},{4,5},{5,4},{6,7},{7,6},{8,9},{9,8},{10,11... | collective-permute-start | bytes 3145736 | tf_op jit(solution)/shard_map/ppermute | solution.py:31
  197.3 65.4 %reduce-scatter.3.cloned.1.call-start = ((), (), s32[]{:S(2)}) async-start(), calls=%async_computation.3 | async-start | bytes 1310720 | tf_op jit(solution)/shard_map/reduce_scatter | solution.py:726
  200.7 20.3 %collective-permute-start.24 = (bf16[1024,256]{1,0:T(8,128)(2,1)S(1)}, bf16[1024,256]{1,0:T(8,128)(2,1)S(1)}, u32[]{:S(2)}, u32[]{:S(2)}) collective-permute-start(bf16[1024,256]{1,0:T(8,128)(2,1)S(1)} %get-tuple-element.171), channel_id=1, source_target_pairs={{0,16},{8,24},{16,0},{24,8},{1,17},{9,25},{17,1},{25,9},{2,18},{10... | collective-permute-start | bytes 1572872 | tf_op jit(solution)/shard_map/ppermute | solution.py:26
  209.6 36.0 %collective-permute-start.25 = (bf16[4,144,768]{2,1,0:T(8,128)(2,1)S(1)}, bf16[4,144,768]{2,1,0:T(8,128)(2,1)S(1)}, u32[]{:S(2)}, u32[]{:S(2)}) collective-permute-start(bf16[4,144,768]{2,1,0:T(8,128)(2,1)S(1)} %get-tuple-element.182), channel_id=1, source_target_pairs={{0,1},{1,0},{2,3},{3,2},{4,5},{5,4},{6,7},{7,6},{8,9},{9,8},{10,11... | collective-permute-start | bytes 2654216 | tf_op jit(solution)/shard_map/ppermute | solution.py:31
  221.1 24.5 %collective-permute-start.28 = (bf16[4,128,256]{2,1,0:T(8,128)(2,1)S(1)}, bf16[4,128,256]{2,1,0:T(8,128)(2,1)S(1)}, u32[]{:S(2)}, u32[]{:S(2)}) collective-permute-start(bf16[4,128,256]{2,1,0:T(8,128)(2,1)S(1)} %get-tuple-element.184), channel_id=1, source_target_pairs={{0,1},{1,0},{2,3},{3,2},{4,5},{5,4},{6,7},{7,6},{8,9},{9,8},{10,11... | collective-permute-start | bytes 786440 | tf_op jit(solution)/shard_map/ppermute | solution.py:31
  228.2 30.7 %collective-permute-start.39 = (bf16[128,1024]{1,0:T(8,128)(2,1)S(1)}, bf16[128,1024]{1,0:T(8,128)(2,1)S(1)}, u32[]{:S(2)}, u32[]{:S(2)}) collective-permute-start(bf16[128,1024]{1,0:T(8,128)(2,1)S(1)} %copy-done.39), channel_id=1, source_target_pairs={{0,8},{8,0},{16,24},{24,16},{1,9},{9,1},{17,25},{25,17},{2,10},{10... | collective-permute-start | bytes 786440 | tf_op jit(solution)/shard_map/ppermute | solution.py:26
  231.4 28.9 %collective-permute-start.41 = (bf16[128,1024]{1,0:T(8,128)(2,1)}, bf16[128,1024]{1,0:T(8,128)(2,1)S(1)}, u32[]{:S(2)}, u32[]{:S(2)}) collective-permute-start(bf16[128,1024]{1,0:T(8,128)(2,1)} %collective-permute-done.40.refs_2_), channel_id=1, source_target_pairs={{0,8},{8,0},{16,24},{24,16},{1,9},{9,1},{17,25},{25,17},{2,10},{10... | collective-permute-start | bytes 786440 | tf_op jit(solution)/shard_map/ppermute | solution.py:26
  248.8 30.1 %collective-permute-start.31 = (bf16[144,1024]{1,0:T(8,128)(2,1)}, bf16[144,1024]{1,0:T(8,128)(2,1)S(1)}, u32[]{:S(2)}, u32[]{:S(2)}) collective-permute-start(bf16[144,1024]{1,0:T(8,128)(2,1)} %get-tuple-element.197), channel_id=1, source_target_pairs={{0,2},{1,3},{2,0},{3,1},{4,6},{5,7},{6,4},{7,5},{8,10},{9,11},{10,... | collective-permute-start | bytes 884744 | tf_op jit(solution)/shard_map/ppermute | solution.py:31
  248.8 30.1 %collective-permute-start.32 = (bf16[144,1024]{1,0:T(8,128)(2,1)}, bf16[144,1024]{1,0:T(8,128)(2,1)S(1)}, u32[]{:S(2)}, u32[]{:S(2)}) collective-permute-start(bf16[144,1024]{1,0:T(8,128)(2,1)} %get-tuple-element.198), channel_id=1, source_target_pairs={{0,4},{1,5},{2,6},{3,7},{4,0},{5,1},{6,2},{7,3},{8,12},{9,13},{10,... | collective-permute-start | bytes 884744 | tf_op jit(solution)/shard_map/ppermute | solution.py:31
  254.7 27.3 %collective-permute-start.33 = (bf16[144,1024]{1,0:T(8,128)(2,1)S(1)}, bf16[144,1024]{1,0:T(8,128)(2,1)S(1)}, u32[]{:S(2)}, u32[]{:S(2)}) collective-permute-start(bf16[144,1024]{1,0:T(8,128)(2,1)S(1)} %get-tuple-element.199), channel_id=1, source_target_pairs={{0,6},{1,7},{2,4},{3,5},{4,2},{5,3},{6,0},{7,1},{8,14},{9,15},{10,... | collective-permute-start | bytes 884744 | tf_op jit(solution)/shard_map/ppermute | solution.py:31
  259.0 12.3 %collective-permute-start.26 = (bf16[256,1024]{1,0:T(8,128)(2,1)S(1)}, bf16[256,1024]{1,0:T(8,128)(2,1)S(1)}, u32[]{:S(2)}, u32[]{:S(2)}) collective-permute-start(bf16[256,1024]{1,0:T(8,128)(2,1)S(1)} %get-tuple-element.187), channel_id=1, source_target_pairs={{0,16},{8,24},{16,0},{24,8},{1,17},{9,25},{17,1},{25,9},{2,18},{10... | collective-permute-start | bytes 1572872 | tf_op jit(solution)/shard_map/ppermute | solution.py:26
  262.7 14.2 %collective-permute-start.30 = (bf16[128,1024]{1,0:T(8,128)(2,1)}, bf16[128,1024]{1,0:T(8,128)(2,1)S(1)}, u32[]{:S(2)}, u32[]{:S(2)}) collective-permute-start(bf16[128,1024]{1,0:T(8,128)(2,1)} %reduce-scatter.3.cloned.1.call-done.refs_0_), channel_id=1, source_target_pairs={{0,16},{8,24},{16,0},{24,8},{1,17},{9,25},{17,1},{25,9},{2,18},{10... | collective-permute-start | bytes 786440 | tf_op jit(solution)/shard_map/ppermute | solution.py:26
  276.9 14.7 %collective-permute-start.37 = (bf16[128,1024]{1,0:T(8,128)(2,1)S(1)}, bf16[128,1024]{1,0:T(8,128)(2,1)S(1)}, u32[]{:S(2)}, u32[]{:S(2)}) collective-permute-start(bf16[128,1024]{1,0:T(8,128)(2,1)S(1)} %copy-done.41), channel_id=1, source_target_pairs={{0,8},{8,0},{16,24},{24,16},{1,9},{9,1},{17,25},{25,17},{2,10},{10... | collective-permute-start | bytes 786440 | tf_op jit(solution)/shard_map/ppermute | solution.py:26
  (81 other events, 535.0 us)
Sparse Core Ops, SparseCore 0:
  24.7 80.9 all-gather.1
  197.4 27.4 reduce-scatter.4
  228.4 28.9 reduce-scatter.2

commit v4 on v3

--- a/solution.py
+++ b/solution.py
@@ -405,12 +405,13 @@
 
 
 def pack(values):
-    high = values.astype(bf16)
-    return jnp.concatenate([high, (values - high.astype(f32)).astype(bf16)])
+    high = values.astype(bf16).astype(f32)
+    return jnp.concatenate([high, values - high]).astype(bf16)
 
 
 def unpack(rows):
-    return rows[:VEC].astype(f32) + rows[VEC:].astype(f32)
+    rows = rows.astype(f32)
+    return rows[:VEC] + rows[VEC:]
 
 
 def qkv_send_kernel(shard, r0_ref, dq_ref, dkv_ref, out_ref):

time: 307 us -> 307 us (level)
  no operation moved by 1% of the time
where the time goes in v4:
time: 307 us; the launch traced here: 303 us
  waiting for transfers between devices  117 us (38%)
  starting transfers between devices  66.6 us (22%)
  Pallas kernels  59.2 us (19%)
  local copies, waits for them, and re-layouts  34 us (11%)
  between operations  15.5 us (5%)
  other arithmetic  7.33 us (2%)
  matrix products  3.38 us (1%)
    ppermute x14, waiting for transfers between devices, over_fsdp(): return lax.ppermute(value, 'fsdp', [(i, i ^ mask) for i in range(size)])  59.4 us
    ppermute x28, waiting for transfers between devices, over_ctx(): return lax.ppermute(value, 'ctx', [(i, i ^ mask) for i in range(size)])  56.9 us
    pallas_call x32, Pallas kernels, kernel_call(): pl.pallas_call(body, in_specs=specs, out_specs=[pl.BlockSpec(memory_space...  45.4 us
    ppermute x28, starting transfers between devices, over_ctx(): return lax.ppermute(value, 'ctx', [(i, i ^ mask) for i in range(size)])  42.8 us
    ppermute x14, starting transfers between devices, over_fsdp(): return lax.ppermute(value, 'fsdp', [(i, i ^ mask) for i in range(size)])  22.9 us
    unnamed x150, local copies, waits for them, and re-layouts  19.6 us
    pallas_call x2, Pallas kernels, attend_back(): pl.pallas_call(functools.partial(attend_back_kernel, head_size, 1.0 / mat...  8.32 us
  transfers between devices with their start and end apart: 45, of which 19 were waited for; matrix products, arithmetic and copies ran while one was open for 7% of the time, Pallas kernels for 15%

profile of v4, /device:TPU:9, one launch (start us, length us, event | category | flops | bytes accessed | tf_op | source)
XLA Modules:
  0.0 302.8 jit_solution(8608112123884814678)
XLA Ops:
  9.7 2.5 collective-permute-start.5
  18.2 2.6 reshape.208
  20.8 2.8 dynamic-slice_reduce_fusion
  25.6 2.5 collective-permute-done.5.refs_4_
  29.3 29.6 %collective-permute-done.7.refs_6_ = bf16[144,1280]{1,0:T(8,128)(2,1)S(1)} collective-permute-done((bf16[144,1280]{1,0:T(8,128)(2,1)S(1)}, bf16[144,1280]{1,0:T(8,128)(2,1)S(1)}, u32[]{:S(2)}, u32[]{:S(2)}) %collective-permute-start.7) | collective-permute-done | bytes 368672 | tf_op jit(solution)/shard_map/ppermute | solution.py:31
  69.9 4.9 %collective-permute-start.9 = (bf16[1024,768]{1,0:T(8,128)(2,1)}, bf16[1024,768]{1,0:T(8,128)(2,1)}, u32[]{:S(2)}, u32[]{:S(2)}) collective-permute-start(bf16[1024,768]{1,0:T(8,128)(2,1)} %copy-done.23), channel_id=1, source_target_pairs={{0,8},{8,0},{16,24},{24,16},{1,9},{9,1},{17,25},{25,17},{2,10},{10... | collective-permute-start | bytes 4718600 | tf_op jit(solution)/shard_map/ppermute | solution.py:26
  79.4 2.7 shard_map.196
  83.1 2.4 add_convert_fusion.1.block_ref.whole_ref.refs_0_.refs_1_
  85.5 2.7 shard_map.197
  89.8 3.8 %collective-permute-done.10 = bf16[256,512]{1,0:T(8,128)(2,1)S(1)} collective-permute-done((bf16[256,512]{1,0:T(8,128)(2,1)S(1)}, bf16[256,512]{1,0:T(8,128)(2,1)S(1)}, u32[]{:S(2)}, u32[]{:S(2)}) %collective-permute-start.10) | collective-permute-done | bytes 262176 | tf_op jit(solution)/shard_map/ppermute | solution.py:26
  97.2 8.0 %collective-permute-done.12.rows_ref.two_ref = bf16[256,1024]{1,0:T(8,128)(2,1)S(1)} collective-permute-done((bf16[256,1024]{1,0:T(8,128)(2,1)S(1)}, bf16[256,1024]{1,0:T(8,128)(2,1)S(1)}, u32[]{:S(2)}, u32[]{:S(2)}) %collective-permute-start.12) | collective-permute-done | bytes 524320 | tf_op jit(solution)/shard_map/ppermute | solution.py:26
  105.6 4.6 %collective-permute-start.13 = (bf16[1024,2048]{1,0:T(8,128)(2,1)}, bf16[1024,2048]{1,0:T(8,128)(2,1)S(1)}, u32[]{:S(2)}, u32[]{:S(2)}) collective-permute-start(bf16[1024,2048]{1,0:T(8,128)(2,1)} %all-gather.2.cloned.1.call-done.refs_0_), channel_id=1, source_target_pairs={{0,8},{8,0},{16,24},{24,16},{1,9},{9,1},{17,25},{25,17},{2,10},{10... | collective-permute-start | bytes 12582920 | tf_op jit(solution)/shard_map/ppermute | solution.py:26
  121.9 10.2 %collective-permute-done.14.got_ref = bf16[256,1024]{1,0:T(8,128)(2,1)S(1)} collective-permute-done((bf16[256,1024]{1,0:T(8,128)(2,1)S(1)}, bf16[256,1024]{1,0:T(8,128)(2,1)S(1)}, u32[]{:S(2)}, u32[]{:S(2)}) %collective-permute-start.14) | collective-permute-done | bytes 524320 | tf_op jit(solution)/shard_map/ppermute | solution.py:26
  138.2 8.2 %collective-permute-done.16.right_ref.rows_ref = bf16[256,1024]{1,0:T(8,128)(2,1)S(1)} collective-permute-done((bf16[256,1024]{1,0:T(8,128)(2,1)S(1)}, bf16[256,1024]{1,0:T(8,128)(2,1)S(1)}, u32[]{:S(2)}, u32[]{:S(2)}) %collective-permute-start.16) | collective-permute-done | bytes 524320 | tf_op jit(solution)/shard_map/ppermute | solution.py:26
  158.0 3.9 %collective-permute-start.21 = (bf16[4,128,1024]{2,1,0:T(8,128)(2,1)S(1)}, bf16[4,128,1024]{2,1,0:T(8,128)(2,1)S(1)}, u32[]{:S(2)}, u32[]{:S(2)}) collective-permute-start(bf16[4,128,1024]{2,1,0:T(8,128)(2,1)S(1)} %get-tuple-element.152), channel_id=1, source_target_pairs={{0,1},{1,0},{2,3},{3,2},{4,5},{5,4},{6,7},{7,6},{8,9},{9,8},{10,11... | collective-permute-start | bytes 3145736 | tf_op jit(solution)/shard_map/ppermute | solution.py:31
  164.7 5.0 %collective-permute-done.17.got_ref = bf16[256,1024]{1,0:T(8,128)(2,1)S(1)} collective-permute-done((bf16[256,1024]{1,0:T(8,128)(2,1)S(1)}, bf16[256,1024]{1,0:T(8,128)(2,1)S(1)}, u32[]{:S(2)}, u32[]{:S(2)}) %collective-permute-start.17) | collective-permute-done | bytes 524320 | tf_op jit(solution)/shard_map/ppermute | solution.py:26
  173.7 5.1 %collective-permute-done.20.refs_6_ = bf16[256,512]{1,0:T(8,128)(2,1)S(1)} collective-permute-done((bf16[256,512]{1,0:T(8,128)(2,1)S(1)}, bf16[256,512]{1,0:T(8,128)(2,1)S(1)}, u32[]{:S(2)}, u32[]{:S(2)}) %collective-permute-start.20) | collective-permute-done | bytes 262176 | tf_op jit(solution)/shard_map/ppermute | solution.py:26
  178.8 4.2 %shard_map.215 = (bf16[512,256]{1,0:T(8,128)(2,1)S(1)}, bf16[512,512]{1,0:T(8,128)(2,1)S(1)}) custom-call(bf16[512,768]{1,0:T(8,128)(2,1)S(1)} %copy-done.5, bf16[512,768]{1,0:T(8,128)(2,1)S(1)} %copy-done.5, f32[512,1]{1,0:T(8,128)S(1)} %copy-done.7, f32[1,512]{1,0:T(1,128)S(1)} %copy-done.20, f32[4,512]{1,0:T(4,128)S(1)} %get-tuple-element.160.refs_4_, ...), custom_call_target="tpu_custom_call" | custom-call | bytes 1024 | tf_op jit(solution)/shard_map/pallas_call | solution.py:154
  193.7 3.5 %collective-permute-start.29 = (bf16[4,128,1024]{2,1,0:T(8,128)(2,1)}, bf16[4,128,1024]{2,1,0:T(8,128)(2,1)}, u32[]{:S(2)}, u32[]{:S(2)}) collective-permute-start(bf16[4,128,1024]{2,1,0:T(8,128)(2,1)} %copy-done.29), channel_id=1, source_target_pairs={{0,1},{1,0},{2,3},{3,2},{4,5},{5,4},{6,7},{7,6},{8,9},{9,8},{10,11... | collective-permute-start | bytes 3145736 | tf_op jit(solution)/shard_map/ppermute | solution.py:31
  202.2 4.1 %shard_map.220 = (bf16[512,256]{1,0:T(8,128)(2,1)S(1)}, bf16[512,512]{1,0:T(8,128)(2,1)S(1)}) custom-call(bf16[512,768]{1,0:T(8,128)(2,1)S(1)} %copy-done.3, bf16[512,768]{1,0:T(8,128)(2,1)S(1)} %copy-done.3, f32[512,1]{1,0:T(8,128)S(1)} %copy-done.7, f32[1,512]{1,0:T(1,128)S(1)} %copy-done.20, f32[4,512]{1,0:T(4,128)S(1)} %get-tuple-element.158.refs_4_, ...), custom_call_target="tpu_custom_call" | custom-call | bytes 1024 | tf_op jit(solution)/shard_map/pallas_call | solution.py:154
  206.4 3.1 %shard_map.221 = (f32[4,136,768]{2,1,0:T(8,128)S(1)}, bf16[4,144,768]{2,1,0:T(8,128)(2,1)S(1)}) custom-call(s32[2]{0:T(128)S(1)} %pad_add_fusion.2.place_ref, bf16[512,1024]{1,0:T(8,128)(2,1)S(1)} %copy-done.9, bf16[512,256]{1,0:T(8,128)(2,1)S(1)} %get-tuple-element.185.dq_ref, bf16[512,512]{1,0:T(8,128)(2,1)S(1)} %get-tuple-element.175.dkv_ref, ...), custom_call_target="tpu_custom_call" | custom-call | flops 30000001024 | bytes 1024 | tf_op jit(solution)/shard_map/pallas_call | solution.py:49
  211.4 9.6 %collective-permute-done.29.got_ref = bf16[4,128,1024]{2,1,0:T(8,128)(2,1)} collective-permute-done((bf16[4,128,1024]{2,1,0:T(8,128)(2,1)}, bf16[4,128,1024]{2,1,0:T(8,128)(2,1)}, u32[]{:S(2)}, u32[]{:S(2)}) %collective-permute-start.29) | collective-permute-done | bytes 1048608 | tf_op jit(solution)/shard_map/ppermute | solution.py:31
  222.4 2.4 shard_map.226
  231.4 2.5 collective-permute-start.41
  233.9 11.7 %collective-permute-done.28.out_got_ref = bf16[4,128,256]{2,1,0:T(8,128)(2,1)S(1)} collective-permute-done((bf16[4,128,256]{2,1,0:T(8,128)(2,1)S(1)}, bf16[4,128,256]{2,1,0:T(8,128)(2,1)S(1)}, u32[]{:S(2)}, u32[]{:S(2)}) %collective-permute-start.28) | collective-permute-done | bytes 262176 | tf_op jit(solution)/shard_map/ppermute | solution.py:31
  248.8 5.8 %collective-permute-start.32 = (bf16[144,1024]{1,0:T(8,128)(2,1)}, bf16[144,1024]{1,0:T(8,128)(2,1)S(1)}, u32[]{:S(2)}, u32[]{:S(2)}) collective-permute-start(bf16[144,1024]{1,0:T(8,128)(2,1)} %get-tuple-element.198), channel_id=1, source_target_pairs={{0,4},{1,5},{2,6},{3,7},{4,0},{5,1},{6,2},{7,3},{8,12},{9,13},{10,... | collective-permute-start | bytes 884744 | tf_op jit(solution)/shard_map/ppermute | solution.py:31
  254.7 3.3 %shard_map.223 = (f32[256,1024]{1,0:T(8,128)S(1)}, bf16[256,1024]{1,0:T(8,128)(2,1)S(1)}) custom-call(bf16[512,256]{1,0:T(8,128)(2,1)S(1)} %copy-done.43, bf16[512,512]{1,0:T(8,128)(2,1)S(1)} %copy-done.34, bf16[512,256]{1,0:T(8,128)(2,1)S(1)} %copy-done.38, bf16[512,512]{1,0:T(8,128)(2,1)S(1)} %copy-done.32, bf16[1024,768]{1,0:T(8,128)(2,1)S(1)} %copy-done.25, ...), custom_call_target="tpu_custom_call" | custom-call | flops 30000001024 | bytes 1024 | tf_op jit(solution)/shard_map/pallas_call | solution.py:49
  260.3 2.4 shard_map.230
  262.9 8.3 %collective-permute-done.26.got_ref = bf16[256,1024]{1,0:T(8,128)(2,1)S(1)} collective-permute-done((bf16[256,1024]{1,0:T(8,128)(2,1)S(1)}, bf16[256,1024]{1,0:T(8,128)(2,1)S(1)}, u32[]{:S(2)}, u32[]{:S(2)}) %collective-permute-start.26) | collective-permute-done | bytes 524320 | tf_op jit(solution)/shard_map/ppermute | solution.py:26
  272.6 3.7 %collective-permute-start.27 = (f32[128,1024]{1,0:T(8,128)S(1)}, f32[128,1024]{1,0:T(8,128)S(1)}, u32[]{:S(2)}, u32[]{:S(2)}) collective-permute-start(f32[128,1024]{1,0:T(8,128)S(1)} %get-tuple-element.189), channel_id=1, source_target_pairs={{0,8},{8,0},{16,24},{24,16},{1,9},{9,1},{17,25},{25,17},{2,10},{10... | collective-permute-start | bytes 1572872 | tf_op jit(solution)/shard_map/ppermute | solution.py:26
  278.9 3.0 collective-permute-done.33.refs_2_
  285.2 5.1 %collective-permute-done.35.refs_2_ = bf16[144,1024]{1,0:T(8,128)(2,1)S(1)} collective-permute-done((bf16[144,1024]{1,0:T(8,128)(2,1)S(1)}, bf16[144,1024]{1,0:T(8,128)(2,1)S(1)}, u32[]{:S(2)}, u32[]{:S(2)}) %collective-permute-start.35) | collective-permute-done | bytes 294944 | tf_op jit(solution)/shard_map/ppermute | solution.py:26
  (303 shorter events, 113.1 us)
Async XLA Ops:
  7.2 98.4 %all-gather.2.cloned.1.call-start = ((), (), s32[]{:S(2)}) async-start(), calls=%async_computation.2 | async-start | bytes 4718592 | tf_op jit(solution)/shard_map/all_gather | solution.py:614
  9.6 15.6 %collective-permute-start.3 = (bf16[144,1280]{1,0:T(8,128)(2,1)S(1)}, bf16[144,1280]{1,0:T(8,128)(2,1)S(1)}, u32[]{:S(2)}, u32[]{:S(2)}) collective-permute-start(bf16[144,1280]{1,0:T(8,128)(2,1)S(1)} %fusion.3.refs_0_), channel_id=1, source_target_pairs={{0,2},{1,3},{2,0},{3,1},{4,6},{5,7},{6,4},{7,5},{8,10},{9,11},{10,... | collective-permute-start | bytes 1105928 | tf_op jit(solution)/shard_map/ppermute | solution.py:31
  9.7 18.4 %collective-permute-start.5 = (bf16[144,1280]{1,0:T(8,128)(2,1)S(1)}, bf16[144,1280]{1,0:T(8,128)(2,1)S(1)}, u32[]{:S(2)}, u32[]{:S(2)}) collective-permute-start(bf16[144,1280]{1,0:T(8,128)(2,1)S(1)} %fusion.3.refs_0_), channel_id=1, source_target_pairs={{0,4},{1,5},{2,6},{3,7},{4,0},{5,1},{6,2},{7,3},{8,12},{9,13},{10,... | collective-permute-start | bytes 1105928 | tf_op jit(solution)/shard_map/ppermute | solution.py:31
  12.2 46.7 %collective-permute-start.7 = (bf16[144,1280]{1,0:T(8,128)(2,1)S(1)}, bf16[144,1280]{1,0:T(8,128)(2,1)S(1)}, u32[]{:S(2)}, u32[]{:S(2)}) collective-permute-start(bf16[144,1280]{1,0:T(8,128)(2,1)S(1)} %fusion.3.refs_0_), channel_id=1, source_target_pairs={{0,6},{1,7},{2,4},{3,5},{4,2},{5,3},{6,0},{7,1},{8,14},{9,15},{10,... | collective-permute-start | bytes 1105928 | tf_op jit(solution)/shard_map/ppermute | solution.py:31
  12.4 51.7 %collective-permute-start.2 = (bf16[144,1280]{1,0:T(8,128)(2,1)S(1)}, bf16[144,1280]{1,0:T(8,128)(2,1)}, u32[]{:S(2)}, u32[]{:S(2)}) collective-permute-start(bf16[144,1280]{1,0:T(8,128)(2,1)S(1)} %fusion.3.refs_0_), channel_id=1, source_target_pairs={{0,1},{1,0},{2,3},{3,2},{4,5},{5,4},{6,7},{7,6},{8,9},{9,8},{10,11... | collective-permute-start | bytes 1105928 | tf_op jit(solution)/shard_map/ppermute | solution.py:31
  16.4 43.7 %collective-permute-start = (bf16[272,1024]{1,0:T(8,128)(2,1)}, bf16[272,1024]{1,0:T(8,128)(2,1)}, u32[]{:S(2)}, u32[]{:S(2)}) collective-permute-start(bf16[272,1024]{1,0:T(8,128)(2,1)} %pad_maximum_fusion), channel_id=1, source_target_pairs={{0,8},{8,0},{16,24},{24,16},{1,9},{9,1},{17,25},{25,17},{2,10},{10... | collective-permute-start | bytes 1671176 | tf_op jit(solution)/shard_map/ppermute | solution.py:26
  24.5 200.3 %reduce-scatter.5.cloned.1.call-start = ((), (), s32[]{:S(2)}) async-start(), calls=%async_computation.4 | async-start | bytes 1310720 | tf_op jit(solution)/shard_map/reduce_scatter | solution.py:727
  25.3 38.8 %collective-permute-start.4 = (bf16[144,1280]{1,0:T(8,128)(2,1)S(1)}, bf16[144,1280]{1,0:T(8,128)(2,1)S(1)}, u32[]{:S(2)}, u32[]{:S(2)}) collective-permute-start(bf16[144,1280]{1,0:T(8,128)(2,1)S(1)} %collective-permute-done.3.refs_2_), channel_id=1, source_target_pairs={{0,1},{1,0},{2,3},{3,2},{4,5},{5,4},{6,7},{7,6},{8,9},{9,8},{10,11... | collective-permute-start | bytes 1105928 | tf_op jit(solution)/shard_map/ppermute | solution.py:31
  28.1 35.9 %collective-permute-start.6 = (bf16[144,1280]{1,0:T(8,128)(2,1)S(1)}, bf16[144,1280]{1,0:T(8,128)(2,1)S(1)}, u32[]{:S(2)}, u32[]{:S(2)}) collective-permute-start(bf16[144,1280]{1,0:T(8,128)(2,1)S(1)} %collective-permute-done.5.refs_4_), channel_id=1, source_target_pairs={{0,1},{1,0},{2,3},{3,2},{4,5},{5,4},{6,7},{7,6},{8,9},{9,8},{10,11... | collective-permute-start | bytes 1105928 | tf_op jit(solution)/shard_map/ppermute | solution.py:31
  62.7 12.3 %collective-permute-start.1 = (bf16[272,1024]{1,0:T(8,128)(2,1)}, bf16[272,1024]{1,0:T(8,128)(2,1)}, u32[]{:S(2)}, u32[]{:S(2)}) collective-permute-start(bf16[272,1024]{1,0:T(8,128)(2,1)} %fusion.2), channel_id=1, source_target_pairs={{0,16},{8,24},{16,0},{24,8},{1,17},{9,25},{17,1},{25,9},{2,18},{10... | collective-permute-start | bytes 1671176 | tf_op jit(solution)/shard_map/ppermute | solution.py:26
  69.9 13.2 %collective-permute-start.9 = (bf16[1024,768]{1,0:T(8,128)(2,1)}, bf16[1024,768]{1,0:T(8,128)(2,1)}, u32[]{:S(2)}, u32[]{:S(2)}) collective-permute-start(bf16[1024,768]{1,0:T(8,128)(2,1)} %copy-done.23), channel_id=1, source_target_pairs={{0,8},{8,0},{16,24},{24,16},{1,9},{9,1},{17,25},{25,17},{2,10},{10... | collective-permute-start | bytes 4718600 | tf_op jit(solution)/shard_map/ppermute | solution.py:26
  74.8 18.9 %collective-permute-start.11 = (bf16[1024,512]{1,0:T(8,128)(2,1)}, bf16[1024,512]{1,0:T(8,128)(2,1)S(1)}, u32[]{:S(2)}, u32[]{:S(2)}) collective-permute-start(bf16[1024,512]{1,0:T(8,128)(2,1)} %copy-done.30), channel_id=1, source_target_pairs={{0,8},{8,0},{16,24},{24,16},{1,9},{9,1},{17,25},{25,17},{2,10},{10... | collective-permute-start | bytes 3145736 | tf_op jit(solution)/shard_map/ppermute | solution.py:26
  105.6 11.5 %collective-permute-start.13 = (bf16[1024,2048]{1,0:T(8,128)(2,1)}, bf16[1024,2048]{1,0:T(8,128)(2,1)S(1)}, u32[]{:S(2)}, u32[]{:S(2)}) collective-permute-start(bf16[1024,2048]{1,0:T(8,128)(2,1)} %all-gather.2.cloned.1.call-done.refs_0_), channel_id=1, source_target_pairs={{0,8},{8,0},{16,24},{24,16},{1,9},{9,1},{17,25},{25,17},{2,10},{10... | collective-permute-start | bytes 12582920 | tf_op jit(solution)/shard_map/ppermute | solution.py:26
  118.8 13.2 %collective-permute-start.14 = (bf16[256,1024]{1,0:T(8,128)(2,1)S(1)}, bf16[256,1024]{1,0:T(8,128)(2,1)S(1)}, u32[]{:S(2)}, u32[]{:S(2)}) collective-permute-start(bf16[256,1024]{1,0:T(8,128)(2,1)S(1)} %get-tuple-element.128), channel_id=1, source_target_pairs={{0,16},{8,24},{16,0},{24,8},{1,17},{9,25},{17,1},{25,9},{2,18},{10... | collective-permute-start | bytes 1572872 | tf_op jit(solution)/shard_map/ppermute | solution.py:26
  134.2 12.2 %collective-permute-start.16 = (bf16[256,1024]{1,0:T(8,128)(2,1)S(1)}, bf16[256,1024]{1,0:T(8,128)(2,1)S(1)}, u32[]{:S(2)}, u32[]{:S(2)}) collective-permute-start(bf16[256,1024]{1,0:T(8,128)(2,1)S(1)} %get-tuple-element.151.rows_ref.left_ref), channel_id=1, source_target_pairs={{0,16},{8,24},{16,0},{24,8},{1,17},{9,25},{17,1},{25,9},{2,18},{10... | collective-permute-start | bytes 1572872 | tf_op jit(solution)/shard_map/ppermute | solution.py:26
  156.6 13.1 %collective-permute-start.17 = (bf16[256,1024]{1,0:T(8,128)(2,1)S(1)}, bf16[256,1024]{1,0:T(8,128)(2,1)S(1)}, u32[]{:S(2)}, u32[]{:S(2)}) collective-permute-start(bf16[256,1024]{1,0:T(8,128)(2,1)S(1)} %get-tuple-element.149), channel_id=1, source_target_pairs={{0,16},{8,24},{16,0},{24,8},{1,17},{9,25},{17,1},{25,9},{2,18},{10... | collective-permute-start | bytes 1572872 | tf_op jit(solution)/shard_map/ppermute | solution.py:26
  158.0 26.7 %collective-permute-start.21 = (bf16[4,128,1024]{2,1,0:T(8,128)(2,1)S(1)}, bf16[4,128,1024]{2,1,0:T(8,128)(2,1)S(1)}, u32[]{:S(2)}, u32[]{:S(2)}) collective-permute-start(bf16[4,128,1024]{2,1,0:T(8,128)(2,1)S(1)} %get-tuple-element.152), channel_id=1, source_target_pairs={{0,1},{1,0},{2,3},{3,2},{4,5},{5,4},{6,7},{7,6},{8,9},{9,8},{10,11... | collective-permute-start | bytes 3145736 | tf_op jit(solution)/shard_map/ppermute | solution.py:31
  193.2 33.1 %collective-permute-start.15 = (bf16[128,1024]{1,0:T(8,128)(2,1)}, bf16[128,1024]{1,0:T(8,128)(2,1)}, u32[]{:S(2)}, u32[]{:S(2)}) collective-permute-start(bf16[128,1024]{1,0:T(8,128)(2,1)} %get-tuple-element.130), channel_id=1, source_target_pairs={{0,8},{8,0},{16,24},{24,16},{1,9},{9,1},{17,25},{25,17},{2,10},{10... | collective-permute-start | bytes 786440 | tf_op jit(solution)/shard_map/ppermute | solution.py:26
  193.2 13.2 %collective-permute-start.23 = (bf16[8,128,768]{2,1,0:T(8,128)(2,1)}, bf16[8,128,768]{2,1,0:T(8,128)(2,1)}, u32[]{:S(2)}, u32[]{:S(2)}) collective-permute-start(bf16[8,128,768]{2,1,0:T(8,128)(2,1)} %copy-done.26), channel_id=1, source_target_pairs={{0,8},{8,0},{16,24},{24,16},{1,9},{9,1},{17,25},{25,17},{2,10},{10... | collective-permute-start | bytes 4718600 | tf_op jit(solution)/shard_map/ppermute | solution.py:26
  193.7 27.3 %collective-permute-start.29 = (bf16[4,128,1024]{2,1,0:T(8,128)(2,1)}, bf16[4,128,1024]{2,1,0:T(8,128)(2,1)}, u32[]{:S(2)}, u32[]{:S(2)}) collective-permute-start(bf16[4,128,1024]{2,1,0:T(8,128)(2,1)} %copy-done.29), channel_id=1, source_target_pairs={{0,1},{1,0},{2,3},{3,2},{4,5},{5,4},{6,7},{7,6},{8,9},{9,8},{10,11... | collective-permute-start | bytes 3145736 | tf_op jit(solution)/shard_map/ppermute | solution.py:31
  197.3 65.4 %reduce-scatter.3.cloned.1.call-start = ((), (), s32[]{:S(2)}) async-start(), calls=%async_computation.3 | async-start | bytes 1310720 | tf_op jit(solution)/shard_map/reduce_scatter | solution.py:727
  200.7 20.3 %collective-permute-start.24 = (bf16[1024,256]{1,0:T(8,128)(2,1)S(1)}, bf16[1024,256]{1,0:T(8,128)(2,1)S(1)}, u32[]{:S(2)}, u32[]{:S(2)}) collective-permute-start(bf16[1024,256]{1,0:T(8,128)(2,1)S(1)} %get-tuple-element.171), channel_id=1, source_target_pairs={{0,16},{8,24},{16,0},{24,8},{1,17},{9,25},{17,1},{25,9},{2,18},{10... | collective-permute-start | bytes 1572872 | tf_op jit(solution)/shard_map/ppermute | solution.py:26
  209.6 36.0 %collective-permute-start.25 = (bf16[4,144,768]{2,1,0:T(8,128)(2,1)S(1)}, bf16[4,144,768]{2,1,0:T(8,128)(2,1)S(1)}, u32[]{:S(2)}, u32[]{:S(2)}) collective-permute-start(bf16[4,144,768]{2,1,0:T(8,128)(2,1)S(1)} %get-tuple-element.182), channel_id=1, source_target_pairs={{0,1},{1,0},{2,3},{3,2},{4,5},{5,4},{6,7},{7,6},{8,9},{9,8},{10,11... | collective-permute-start | bytes 2654216 | tf_op jit(solution)/shard_map/ppermute | solution.py:31
  221.1 24.5 %collective-permute-start.28 = (bf16[4,128,256]{2,1,0:T(8,128)(2,1)S(1)}, bf16[4,128,256]{2,1,0:T(8,128)(2,1)S(1)}, u32[]{:S(2)}, u32[]{:S(2)}) collective-permute-start(bf16[4,128,256]{2,1,0:T(8,128)(2,1)S(1)} %get-tuple-element.184), channel_id=1, source_target_pairs={{0,1},{1,0},{2,3},{3,2},{4,5},{5,4},{6,7},{7,6},{8,9},{9,8},{10,11... | collective-permute-start | bytes 786440 | tf_op jit(solution)/shard_map/ppermute | solution.py:31
  228.2 30.7 %collective-permute-start.39 = (bf16[128,1024]{1,0:T(8,128)(2,1)S(1)}, bf16[128,1024]{1,0:T(8,128)(2,1)S(1)}, u32[]{:S(2)}, u32[]{:S(2)}) collective-permute-start(bf16[128,1024]{1,0:T(8,128)(2,1)S(1)} %copy-done.39), channel_id=1, source_target_pairs={{0,8},{8,0},{16,24},{24,16},{1,9},{9,1},{17,25},{25,17},{2,10},{10... | collective-permute-start | bytes 786440 | tf_op jit(solution)/shard_map/ppermute | solution.py:26
  231.4 28.9 %collective-permute-start.41 = (bf16[128,1024]{1,0:T(8,128)(2,1)}, bf16[128,1024]{1,0:T(8,128)(2,1)S(1)}, u32[]{:S(2)}, u32[]{:S(2)}) collective-permute-start(bf16[128,1024]{1,0:T(8,128)(2,1)} %collective-permute-done.40.refs_2_), channel_id=1, source_target_pairs={{0,8},{8,0},{16,24},{24,16},{1,9},{9,1},{17,25},{25,17},{2,10},{10... | collective-permute-start | bytes 786440 | tf_op jit(solution)/shard_map/ppermute | solution.py:26
  248.8 30.1 %collective-permute-start.31 = (bf16[144,1024]{1,0:T(8,128)(2,1)}, bf16[144,1024]{1,0:T(8,128)(2,1)S(1)}, u32[]{:S(2)}, u32[]{:S(2)}) collective-permute-start(bf16[144,1024]{1,0:T(8,128)(2,1)} %get-tuple-element.197), channel_id=1, source_target_pairs={{0,2},{1,3},{2,0},{3,1},{4,6},{5,7},{6,4},{7,5},{8,10},{9,11},{10,... | collective-permute-start | bytes 884744 | tf_op jit(solution)/shard_map/ppermute | solution.py:31
  248.8 30.1 %collective-permute-start.32 = (bf16[144,1024]{1,0:T(8,128)(2,1)}, bf16[144,1024]{1,0:T(8,128)(2,1)S(1)}, u32[]{:S(2)}, u32[]{:S(2)}) collective-permute-start(bf16[144,1024]{1,0:T(8,128)(2,1)} %get-tuple-element.198), channel_id=1, source_target_pairs={{0,4},{1,5},{2,6},{3,7},{4,0},{5,1},{6,2},{7,3},{8,12},{9,13},{10,... | collective-permute-start | bytes 884744 | tf_op jit(solution)/shard_map/ppermute | solution.py:31
  254.7 27.3 %collective-permute-start.33 = (bf16[144,1024]{1,0:T(8,128)(2,1)S(1)}, bf16[144,1024]{1,0:T(8,128)(2,1)S(1)}, u32[]{:S(2)}, u32[]{:S(2)}) collective-permute-start(bf16[144,1024]{1,0:T(8,128)(2,1)S(1)} %get-tuple-element.199), channel_id=1, source_target_pairs={{0,6},{1,7},{2,4},{3,5},{4,2},{5,3},{6,0},{7,1},{8,14},{9,15},{10,... | collective-permute-start | bytes 884744 | tf_op jit(solution)/shard_map/ppermute | solution.py:31
  259.0 12.3 %collective-permute-start.26 = (bf16[256,1024]{1,0:T(8,128)(2,1)S(1)}, bf16[256,1024]{1,0:T(8,128)(2,1)S(1)}, u32[]{:S(2)}, u32[]{:S(2)}) collective-permute-start(bf16[256,1024]{1,0:T(8,128)(2,1)S(1)} %get-tuple-element.187), channel_id=1, source_target_pairs={{0,16},{8,24},{16,0},{24,8},{1,17},{9,25},{17,1},{25,9},{2,18},{10... | collective-permute-start | bytes 1572872 | tf_op jit(solution)/shard_map/ppermute | solution.py:26
  262.7 14.2 %collective-permute-start.30 = (bf16[128,1024]{1,0:T(8,128)(2,1)}, bf16[128,1024]{1,0:T(8,128)(2,1)S(1)}, u32[]{:S(2)}, u32[]{:S(2)}) collective-permute-start(bf16[128,1024]{1,0:T(8,128)(2,1)} %reduce-scatter.3.cloned.1.call-done.refs_0_), channel_id=1, source_target_pairs={{0,16},{8,24},{16,0},{24,8},{1,17},{9,25},{17,1},{25,9},{2,18},{10... | collective-permute-start | bytes 786440 | tf_op jit(solution)/shard_map/ppermute | solution.py:26
  276.9 14.7 %collective-permute-start.37 = (bf16[128,1024]{1,0:T(8,128)(2,1)S(1)}, bf16[128,1024]{1,0:T(8,128)(2,1)S(1)}, u32[]{:S(2)}, u32[]{:S(2)}) collective-permute-start(bf16[128,1024]{1,0:T(8,128)(2,1)S(1)} %copy-done.41), channel_id=1, source_target_pairs={{0,8},{8,0},{16,24},{24,16},{1,9},{9,1},{17,25},{25,17},{2,10},{10... | collective-permute-start | bytes 786440 | tf_op jit(solution)/shard_map/ppermute | solution.py:26
  (81 other events, 535.0 us)
Sparse Core Ops, SparseCore 0:
  24.7 80.9 all-gather.1
  197.4 27.4 reduce-scatter.4
  228.4 28.9 reduce-scatter.2
